TPU v7x, 32 devices: a whole 2x2x4 slice. The times are simulated.
32 devices in a mesh: row: 4 (over y, core), col: 8 (over z, x).
Axes of the slice: x: 2, y: 2, z: 4, core: 2. Of those that a mesh axis runs over, the one named last changes fastest.
Arguments:
- stored_inverse: bfloat16 [6, 4, 3, 8, 256, 256], P(None, 'row', None, 'col'), may hold values from -6 to 6
- panel_first: bfloat16 [6, 4, 256, 256], P(None, 'row', 'col'), may hold values from -0.09375 to 0.09375
- panel_second: bfloat16 [6, 4, 256, 256], P(None, 'row', 'col'), may hold values from -0.109375 to 0.109375
- panel_link: bfloat16 [256, 256], replicated, may hold values from -0.375 to 0.375
- inv_first: float32 [256, 256], replicated, as said below
- inv_second: float32 [256, 256], replicated, as said below
- struct_first: int32 [18], replicated, may hold values from 0 to 23, as said below
- struct_second: int32 [12], replicated, may hold values from 0 to 23, as said below
Outputs:
- column_first: float32 [6, 4, 256, 256], P(None, 'row', 'col')
- column_second: float32 [6, 4, 256, 256], P(None, 'row', 'col')
- diag_first: float32 [256, 256], P('col')
- link_block: float32 [256, 256], P('col')
- diag_second: float32 [256, 256], P('col')
Inputs may be any that keep to these rules, and one draw needn't show every extreme that they name: `struct_first`: 18 distinct block indices in increasing order; the last is always 24 - 1. `struct_second`: 12 distinct block indices in increasing order, each also listed in struct_first; the last is always 24 - 1; the second supernode's whole structure is the first supernode together with these blocks. `inv_first`: lower triangular with a positive diagonal. `inv_second`: lower triangular with a positive diagonal.
All inputs are finite; a program needn't handle non-finite values.
Results may differ from a plain program's by a relative error of at most 0.0041.
Values may be sent and summed in bfloat16 or wider, within the bound.
No kernel may reach another device: no remote copies, remote signals or barrier semaphores. Data moves between devices by JAX's collectives and lax.ppermute only.
A program may use at most 64 MiB of HBM per device.

v0:
```python
import functools

import jax
import jax.numpy as jnp
from jax import lax
from jax.experimental import pallas as pl
from jax.experimental.pallas import tpu as pltpu
from jax.sharding import PartitionSpec as P

precise = lax.Precision.HIGHEST
SMEM = pl.BlockSpec(memory_space=pltpu.SMEM)
VMEM = pl.BlockSpec(memory_space=pltpu.VMEM)
HBM = pl.BlockSpec(memory_space=pltpu.HBM)


def exact_dot(left, right, left_dim=1):
    dims = (((left_dim,), (0,)), ((), ()))
    return lax.dot_general(left, right, dims, precision=precise, preferred_element_type=jnp.float32)


def split_dot(left, right, left_dim=1):
    def halves(value):
        if value.dtype == jnp.bfloat16:
            return [value]
        high = value.astype(jnp.bfloat16)
        return [high, (value - high.astype(jnp.float32)).astype(jnp.bfloat16)]

    dims = (((left_dim,), (0,)), ((), ()))
    total = None
    for i, a in enumerate(halves(left)):
        for j, b in enumerate(halves(right)):
            if i + j < 2:
                term = lax.dot_general(a, b, dims, preferred_element_type=jnp.float32)
                total = term if total is None else total + term
    return total


def listed(struct_ref, blocks, n_row):
    ids = lax.broadcasted_iota(jnp.int32, (blocks, 1, 1), 0) * n_row + lax.axis_index("row")

    def look(place, found):
        return jnp.where(ids == struct_ref[place], 1, found)

    found = lax.fori_loop(0, struct_ref.shape[0], look, jnp.zeros((blocks, 1, 1), jnp.int32))
    return found == 1


def factor_kernel(n_row, cycle, struct1, struct2, *refs):
    sources, (own, linked, *parts) = refs[:5], refs[5 : 7 + cycle]
    held, sems = refs[7 + cycle : 12 + cycle], refs[12 + cycle]
    copies = [pltpu.make_async_copy(a, b, sems.at[i]) for i, (a, b) in enumerate(zip(sources, held))]
    for copy in copies:
        copy.start()
    panel1, panel2, link, inv1, inv2 = held
    blocks, slab, width = panel1.shape
    keep = [listed(struct, blocks, n_row) for struct in (struct1, struct2)]
    turn = lax.rem(lax.axis_index("col"), cycle)
    for copy in copies:
        copy.wait()
    for p, (panel, inverse) in enumerate(((panel1, inv1), (panel2, inv2))):
        rows = panel[...].astype(jnp.float32).reshape(blocks * slab, width)
        product = exact_dot(rows, inverse[...]).reshape(blocks, slab, width)
        own[p] = jnp.where(keep[p], product, 0.0).astype(jnp.bfloat16)
    for s, part in enumerate(parts):
        pick = lax.rem(s - turn + cycle, cycle)
        for p in range(2):
            for b in range(blocks // cycle):
                part[p, b] = own[p, b * cycle + pick]
    linked[...] = exact_dot(link[...].astype(jnp.float32), inv2[...])


def product_kernel(n_row, n_col, first_bits, stored, pieces, *rest):
    cycle = n_col // n_row
    keeps, sends = rest[:2], rest[2:4]
    held, loose, factor, sems = rest[4:]
    row_blocks = held.shape[0]
    col_blocks, _, slab, double = loose.shape
    width = double // 2
    here_row, here_col = lax.axis_index("row"), lax.axis_index("col")
    copies = [pltpu.make_async_copy(stored.at[a], held.at[a], sems.at[a]) for a in range(row_blocks)]
    for copy in copies:
        copy.start()

    group = here_col // n_row
    for m in range(n_row):
        for s in range(cycle):
            slot = (here_row ^ m) * cycle + lax.rem(s - group + cycle, cycle)
            for p in range(2):
                for b in range(col_blocks):
                    loose[b, slot, :, p * width : (p + 1) * width] = pieces[m, s, p, b].astype(jnp.float32)
    for b in range(col_blocks):
        factor[b] = loose[b].reshape(n_col * slab, double).astype(jnp.bfloat16)

    for a in range(row_blocks):
        copies[a].wait()
        total = jnp.dot(held[a, 0], factor[0], preferred_element_type=jnp.float32)
        for b in range(1, col_blocks):
            total += jnp.dot(held[a, b], factor[b], preferred_element_type=jnp.float32)
        for p in range(2):
            bit = first_bits[p]
            upper = ((here_col >> bit) & 1) == 1
            for j in range(n_col // 2):
                low = ((j >> bit) << (bit + 1)) | (j & ((1 << bit) - 1))
                high = low | (1 << bit)
                x = total[low * slab : (low + 1) * slab, p * width : (p + 1) * width]
                y = total[high * slab : (high + 1) * slab, p * width : (p + 1) * width]
                keeps[p][j, a] = jnp.where(upper, y, x)
                sends[p][j, a] = jnp.where(upper, x, y).astype(jnp.bfloat16)


def sum_kernel(own, other, mine1, theirs1, mine2, theirs2, linked, out):
    blocks, slab, width = mine1.shape
    flat = (blocks * slab, width)

    def both(a, b):
        return jnp.concatenate([a.reshape(flat), b.reshape(flat)], axis=0)

    def factor(p):
        return both(own[p].astype(jnp.float32), other[p].astype(jnp.float32)).astype(jnp.bfloat16)

    link = linked[...]
    sum1 = both(mine1[...], theirs1[...])
    u2 = factor(1)
    first = split_dot(factor(0), sum1, 0)
    cross = split_dot(u2, sum1, 0)
    top = cross.T - split_dot(first, link)
    second = split_dot(u2, both(mine2[...], theirs2[...]), 0) - split_dot(cross, link) - split_dot(link, top, 0)
    n_col = width // slab
    out[0] = first.reshape(n_col, slab, width)
    out[1] = top.reshape(n_col, slab, width)
    out[2] = second.reshape(n_col, slab, width)


def column_kernel(n_row, struct1, struct2, kept1, came1, kept2, came2, linked, column1, column2):
    blocks, slab, width = column1.shape
    sum1 = kept1[...] + came1[...].astype(jnp.float32)
    sum2 = kept2[...] + came2[...].astype(jnp.float32)
    col1 = jnp.where(listed(struct1, blocks, n_row), -sum1, 0.0)
    column1[...] = col1
    carried = split_dot(col1.reshape(blocks * slab, width), linked[...]).reshape(sum2.shape)
    column2[...] = jnp.where(listed(struct2, blocks, n_row), -(sum2 + carried), 0.0)


def gram_kernel(inv1, inv2, linked, out, held1, held2, whole, sems):
    copies = [pltpu.make_async_copy(inv1, held1, sems.at[0]), pltpu.make_async_copy(inv2, held2, sems.at[1])]
    for copy in copies:
        copy.start()
    for copy in copies:
        copy.wait()
    slab = out.shape[1]
    link = linked[...]
    gram1 = exact_dot(held1[...], held1[...], 0)
    across = exact_dot(gram1, link)
    whole[0] = gram1
    whole[1] = -across
    whole[2] = exact_dot(held2[...], held2[...], 0) + exact_dot(link, across, 0)
    place = pl.ds(pl.multiple_of(lax.axis_index("col") * slab, slab), slab)
    out[...] = whole[:, place, :]


def swapped(value, axis, size, mask):
    return lax.ppermute(value, axis, [(i, i ^ mask) for i in range(size)])


def halves(value, axis, mine):
    kept = lax.dynamic_index_in_dim(value, mine, axis, keepdims=False)
    sent = lax.dynamic_index_in_dim(value, 1 - mine, axis, keepdims=False)
    return kept, sent.astype(jnp.bfloat16)


def body(stored_inverse, panel_first, panel_second, panel_link, inv_first, inv_second, struct_first, struct_second):
    n_row, n_col = lax.axis_size("row"), lax.axis_size("col")
    here_col = lax.axis_index("col")
    row_blocks, _, col_blocks, _, width, _ = stored_inverse.shape
    slab = width // n_col
    cycle = n_col // n_row
    n_bits = n_col.bit_length() - 1
    f32, bf16 = jnp.float32, jnp.bfloat16
    shape = jax.ShapeDtypeStruct
    big = pltpu.CompilerParams(vmem_limit_bytes=24 * 1024 * 1024)
    stored = stored_inverse.reshape(row_blocks, col_blocks, width, width)
    panel = (row_blocks, slab, width)
    square = pltpu.VMEM((width, width), f32)

    own, linked, *parts = pl.pallas_call(
        functools.partial(factor_kernel, n_row, cycle),
        out_shape=[shape((2,) + panel, bf16), shape((width, width), f32)]
        + [shape((2, col_blocks, slab, width), bf16)] * cycle,
        in_specs=[SMEM, SMEM] + [HBM] * 5,
        out_specs=[VMEM] * (2 + cycle),
        scratch_shapes=[pltpu.VMEM(panel, bf16)] * 2
        + [pltpu.VMEM((width, width), bf16), square, square, pltpu.SemaphoreType.DMA((5,))],
        compiler_params=big,
        name="factors",
    )(struct_first, struct_second, panel_first.reshape(panel), panel_second.reshape(panel), panel_link, inv_first, inv_second)

    got = []
    for s, part in enumerate(parts):
        moves = []
        for r in range(n_row):
            for c in range(n_col):
                j = (s - c) % cycle
                moves.append((r * n_col + c, (c // cycle) * n_col + r + j * n_row))
        got.append(lax.ppermute(part, ("row", "col"), moves))
    pieces = jnp.stack(got)[None]

    consts = pl.pallas_call(
        gram_kernel,
        out_shape=shape((3, slab, width), f32),
        in_specs=[HBM, HBM, VMEM],
        out_specs=VMEM,
        scratch_shapes=[square, square, pltpu.VMEM((3, width, width), f32), pltpu.SemaphoreType.DMA((2,))],
        compiler_params=big,
        name="grams",
        cost_estimate=pl.CostEstimate(flops=6 * 8 * width**3, bytes_accessed=8 * width**2, transcendentals=0),
    )(inv_first, inv_second, linked)

    order = [0]
    bit = n_row // 2
    while bit:
        pieces = jnp.concatenate([pieces, swapped(pieces, "row", n_row, bit)])
        order += [o ^ bit for o in order]
        bit //= 2
    pieces = jnp.stack([pieces[order.index(m)] for m in range(n_row)])
    pieces, consts, own = lax.optimization_barrier((pieces, consts, own))
    other = swapped(own, "col", n_col, n_col // 2)

    orders = (list(range(n_bits)), [1, 0] + list(range(2, n_bits)))
    half = (n_col // 2,) + panel
    split = pl.pallas_call(
        functools.partial(product_kernel, n_row, n_col, (orders[0][0], orders[1][0])),
        out_shape=[shape(half, f32)] * 2 + [shape(half, bf16)] * 2,
        in_specs=[HBM, VMEM],
        out_specs=[VMEM] * 4,
        scratch_shapes=[
            pltpu.VMEM(stored.shape, bf16),
            pltpu.VMEM((col_blocks, n_col, slab, 2 * width), f32),
            pltpu.VMEM((col_blocks, width, 2 * width), bf16),
            pltpu.SemaphoreType.DMA((row_blocks,)),
        ],
        compiler_params=big,
        name="products",
    )(stored, pieces)

    last = []
    for p in range(2):
        keep, send = split[p], split[2 + p]
        left = sorted(set(range(n_bits)) - {orders[p][0]})
        came = swapped(send, "col", n_col, 1 << orders[p][0])
        for bit in orders[p][1:]:
            low = 1 << left.index(bit)
            left.remove(bit)
            total = (keep + came.astype(f32)).reshape((-1, 2, low) + panel)
            keep, send = halves(total, 1, (here_col >> bit) & 1)
            keep, send = keep.reshape((-1,) + panel), send.reshape((-1,) + panel)
            if left:
                came = swapped(send, "col", n_col, 1 << bit)
        theirs = lax.dynamic_index_in_dim(total, 1 - ((here_col >> bit) & 1), 1, keepdims=False)
        last.append((keep.reshape(panel), theirs.reshape(panel), send))

    sums = pl.pallas_call(
        sum_kernel,
        out_shape=shape((3, n_col, slab, width), f32),
        in_specs=[VMEM] * 7,
        out_specs=VMEM,
        compiler_params=big,
        name="sums",
    )(own, other, last[0][0], last[0][1], last[1][0], last[1][1], linked)
    for bit in range(n_bits):
        keep, send = halves(sums.reshape(3, -1, 2, slab, width), 2, (here_col >> bit) & 1)
        sums = keep + swapped(send, "col", n_col, 1 << bit).astype(f32)

    done = []
    for keep, _, send in last:
        done += [keep, swapped(send, "col", n_col, n_col // 2).reshape(panel)]
    column_first, column_second = pl.pallas_call(
        functools.partial(column_kernel, n_row),
        out_shape=[shape(panel, f32)] * 2,
        in_specs=[SMEM, SMEM] + [VMEM] * 5,
        out_specs=[VMEM] * 2,
        compiler_params=big,
        name="columns",
    )(struct_first, struct_second, *done, linked)

    total = sums.reshape(3, slab, width)
    send = total.astype(bf16)
    for m in range(1, n_row):
        total = total + swapped(send, "row", n_row, m).astype(f32)
    diag_first, link_block, diag_second = consts + total
    out = (row_blocks, 1, slab, width)
    return column_first.reshape(out), column_second.reshape(out), diag_first, link_block, diag_second


def solution(mesh):
    placed = (
        P(None, "row", None, "col", None, None),
        P(None, "row", "col", None),
        P(None, "row", "col", None),
        P(),
        P(),
        P(),
        P(),
        P(),
    )
    return jax.shard_map(
        body,
        mesh=mesh,
        in_specs=placed,
        out_specs=(
            P(None, "row", "col", None),
            P(None, "row", "col", None),
            P("col", None),
            P("col", None),
            P("col", None),
        ),
        check_vma=False,
    )
```

profile of v0, /device:TPU:0, one launch (start us, length us, event | category | flops | bytes accessed | tf_op | source)
XLA Modules:
  0.0 88.1 jit_solution(952048316098743885)
XLA Ops:
  0.6 0.0 copy-start.1
  0.6 0.9 %copy-done.1 = f32[256,256]{1,0:T(8,128)S(1)} copy-done((f32[256,256]{1,0:T(8,128)S(1)}, f32[256,256]{1,0:T(8,128)}, u32[]{:S(2)}) %copy-start.1) | copy-done | bytes 262168
  1.6 0.9 %copy-done.3 = f32[256,256]{1,0:T(8,128)S(1)} copy-done((f32[256,256]{1,0:T(8,128)S(1)}, f32[256,256]{1,0:T(8,128)}, u32[]{:S(2)}) %copy-start.3) | copy-done | bytes 262168
  2.5 0.9 %copy-done.5 = bf16[256,256]{1,0:T(8,128)(2,1)S(1)} copy-done((bf16[256,256]{1,0:T(8,128)(2,1)S(1)}, bf16[256,256]{1,0:T(8,128)(2,1)}, u32[]{:S(2)}) %copy-start.5) | copy-done | bytes 131096
  3.4 0.9 %copy-done.6 = bf16[6,1,32,256]{3,2,1,0:T(8,128)(2,1)S(1)} copy-done((bf16[6,1,32,256]{3,2,1,0:T(8,128)(2,1)S(1)}, bf16[6,1,32,256]{3,2,1,0:T(8,128)(2,1)}, u32[]{:S(2)}) %copy-start.6) | copy-done | bytes 98328
  4.3 0.9 %copy-done.7 = bf16[6,1,32,256]{3,2,1,0:T(8,128)(2,1)S(1)} copy-done((bf16[6,1,32,256]{3,2,1,0:T(8,128)(2,1)S(1)}, bf16[6,1,32,256]{3,2,1,0:T(8,128)(2,1)}, u32[]{:S(2)}) %copy-start.7) | copy-done | bytes 98328
  5.2 0.7 copy-done.8
  5.9 0.7 copy-done.10
  6.5 2.1 %factors.1 = (bf16[2,6,32,256]{3,2,1,0:T(8,128)(2,1)S(1)}, f32[256,256]{1,0:T(8,128)S(1)}, bf16[2,3,32,256]{3,2,1,0:T(8,128)(2,1)S(1)}, bf16[2,3,32,256]{3,2,1,0:T(8,128)(2,1)S(1)}) custom-call(s32[18]{0:T(128)S(1)} %copy-done.8, s32[12]{0:T(128)S(1)} %copy-done.10, bf16[6,32,256]{2,1,0:T(8,128)(2,1)S(1)} %bitcast.73, bf16[6,32,256]{2,1,0:T(8,128)(2,1)S(1)} %bitcast.74, ...), custom_call_target="tpu_custom_call" | custom-call | tf_op jit(solution)/shard_map/factors/pallas_call | solution.py:185
  8.6 0.7 collective-permute-start
  9.3 6.6 %collective-permute-start.1 = (bf16[2,3,32,256]{3,2,1,0:T(8,128)(2,1)S(1)}, bf16[2,3,32,256]{3,2,1,0:T(8,128)(2,1)S(1)}, u32[]{:S(2)}, u32[]{:S(2)}) collective-permute-start(bf16[2,3,32,256]{3,2,1,0:T(8,128)(2,1)S(1)} %get-tuple-element.19), channel_id=1, source_target_pairs={{0,4},{1,0},{2,12},{3,8},{4,20},{5,16},{6,28},{7,24},{8,5},{9,1},{... | collective-permute-start | bytes 294920 | tf_op jit(solution)/shard_map/ppermute | solution.py:204
  15.9 3.8 %collective-permute-done.1 = bf16[2,3,32,256]{3,2,1,0:T(8,128)(2,1)S(1)} collective-permute-done((bf16[2,3,32,256]{3,2,1,0:T(8,128)(2,1)S(1)}, bf16[2,3,32,256]{3,2,1,0:T(8,128)(2,1)S(1)}, u32[]{:S(2)}, u32[]{:S(2)}) %collective-permute-start.1) | collective-permute-done | bytes 98336 | tf_op jit(solution)/shard_map/ppermute | solution.py:204
  19.7 3.4 %collective-permute-start.2 = (bf16[1,2,2,3,32,256]{5,4,3,2,1,0:T(8,128)(2,1)S(1)}, bf16[1,2,2,3,32,256]{5,4,3,2,1,0:T(8,128)(2,1)S(1)}, u32[]{:S(2)}, u32[]{:S(2)}) collective-permute-start(bf16[1,2,2,3,32,256]{5,4,3,2,1,0:T(8,128)(2,1)S(1)} %maximum_bitcast_fusion), channel_id=1, source_target_pairs={{0,16},{8,24},{16,0},{24,8},{1,17},{9,25},{17,1},{25,9},{2,18},{10... | collective-permute-start | bytes 589832 | tf_op jit(solution)/shard_map/ppermute | solution.py:162
  23.1 5.1 %collective-permute-done.2 = bf16[1,2,2,3,32,256]{5,4,3,2,1,0:T(8,128)(2,1)S(1)} collective-permute-done((bf16[1,2,2,3,32,256]{5,4,3,2,1,0:T(8,128)(2,1)S(1)}, bf16[1,2,2,3,32,256]{5,4,3,2,1,0:T(8,128)(2,1)S(1)}, u32[]{:S(2)}, u32[]{:S(2)}) %collective-permute-start.2) | collective-permute-done | bytes 196640 | tf_op jit(solution)/shard_map/ppermute | solution.py:162
  28.3 0.5 collective-permute-start.3
  28.8 0.9 %copy-done.2 = f32[256,256]{1,0:T(8,128)S(1)} copy-done((f32[256,256]{1,0:T(8,128)S(1)}, f32[256,256]{1,0:T(8,128)}, u32[]{:S(2)}) %copy-start.2) | copy-done | bytes 262168
  29.8 0.9 %copy-done.4 = f32[256,256]{1,0:T(8,128)S(1)} copy-done((f32[256,256]{1,0:T(8,128)S(1)}, f32[256,256]{1,0:T(8,128)}, u32[]{:S(2)}) %copy-start.4) | copy-done | bytes 262168
  30.7 2.0 %grams.1 = f32[3,32,256]{2,1,0:T(8,128)S(1)} custom-call(f32[256,256]{1,0:T(8,128)S(1)} %copy-done.2, f32[256,256]{1,0:T(8,128)S(1)} %copy-done.4, f32[256,256]{1,0:T(8,128)S(1)} %get-tuple-element.20.linked), custom_call_target="tpu_custom_call" | custom-call | flops 805306368 | bytes 524288 | tf_op jit(solution)/shard_map/grams/pallas_call | solution.py:207
  32.8 0.1 pad_maximum_fusion.pieces
  32.9 3.6 %products.1 = (f32[4,6,32,256]{3,2,1,0:T(8,128)S(1)}, f32[4,6,32,256]{3,2,1,0:T(8,128)S(1)}, bf16[4,6,32,256]{3,2,1,0:T(8,128)(2,1)S(1)}, bf16[4,6,32,256]{3,2,1,0:T(8,128)(2,1)S(1)}) custom-call(bf16[6,3,256,256]{3,2,1,0:T(8,128)(2,1)S(1)} %bitcast.72, bf16[4,2,2,3,32,256]{5,4,3,2,1,0:T(8,128)(2,1)S(1)} %pad_maximum_fusion.pieces), custom_call_target="tpu_custom_call" | custom-call | tf_op jit(solution)/shard_map/products/pallas_call | solution.py:230
  36.6 1.7 %collective-permute-start.7 = (bf16[4,6,32,256]{3,2,1,0:T(8,128)(2,1)S(1)}, bf16[4,6,32,256]{3,2,1,0:T(8,128)(2,1)}, u32[]{:S(2)}, u32[]{:S(2)}) collective-permute-start(bf16[4,6,32,256]{3,2,1,0:T(8,128)(2,1)S(1)} %get-tuple-element.26), channel_id=1, source_target_pairs={{0,2},{1,3},{2,0},{3,1},{4,6},{5,7},{6,4},{7,5},{8,10},{9,11},{10,... | collective-permute-start | bytes 1179656 | tf_op jit(solution)/shard_map/ppermute | solution.py:162
  38.3 0.3 collective-permute-start.4
  38.6 4.0 %collective-permute-start.10 = (bf16[2,6,32,256]{3,2,1,0:T(8,128)(2,1)S(1)}, bf16[2,6,32,256]{3,2,1,0:T(8,128)(2,1)S(1)}, u32[]{:S(2)}, u32[]{:S(2)}) collective-permute-start(bf16[2,6,32,256]{3,2,1,0:T(8,128)(2,1)S(1)} %get-tuple-element.30.own), channel_id=1, source_target_pairs={{0,4},{1,5},{2,6},{3,7},{4,0},{5,1},{6,2},{7,3},{8,12},{9,13},{10,... | collective-permute-start | bytes 589832 | tf_op jit(solution)/shard_map/ppermute | solution.py:162
  42.6 9.8 %collective-permute-done.7 = bf16[4,6,32,256]{3,2,1,0:T(8,128)(2,1)} collective-permute-done((bf16[4,6,32,256]{3,2,1,0:T(8,128)(2,1)S(1)}, bf16[4,6,32,256]{3,2,1,0:T(8,128)(2,1)}, u32[]{:S(2)}, u32[]{:S(2)}) %collective-permute-start.7) | collective-permute-done | bytes 393248 | tf_op jit(solution)/shard_map/ppermute | solution.py:162
  52.4 1.1 %convert_add_fusion = f32[4,6,32,256]{3,2,1,0:T(8,128)S(1)} fusion(f32[4,6,32,256]{3,2,1,0:T(8,128)S(1)} %get-tuple-element.25, bf16[4,6,32,256]{3,2,1,0:T(8,128)(2,1)} %collective-permute-done.7), kind=kLoop, calls=%fused_computation.1 | loop fusion | flops 393216 | bytes 1966080 | tf_op jit(solution)/shard_map/add | solution.py:253
  53.6 2.0 %collective-permute-start.8 = (bf16[2,6,32,256]{3,2,1,0:T(8,128)(2,1)S(1)}, bf16[2,6,32,256]{3,2,1,0:T(8,128)(2,1)S(1)}, u32[]{:S(2)}, u32[]{:S(2)}) collective-permute-start(bf16[2,6,32,256]{3,2,1,0:T(8,128)(2,1)S(1)} %fusion.1), channel_id=1, source_target_pairs={{0,1},{1,0},{2,3},{3,2},{4,5},{5,4},{6,7},{7,6},{8,9},{9,8},{10,11... | collective-permute-start | bytes 589832 | tf_op jit(solution)/shard_map/ppermute | solution.py:162
  55.6 0.1 convert_add_fusion.1
  55.8 0.1 collective-permute-start.5
  55.8 4.5 %collective-permute-done.8 = bf16[2,6,32,256]{3,2,1,0:T(8,128)(2,1)S(1)} collective-permute-done((bf16[2,6,32,256]{3,2,1,0:T(8,128)(2,1)S(1)}, bf16[2,6,32,256]{3,2,1,0:T(8,128)(2,1)S(1)}, u32[]{:S(2)}, u32[]{:S(2)}) %collective-permute-start.8) | collective-permute-done | bytes 196640 | tf_op jit(solution)/shard_map/ppermute | solution.py:162
  60.4 1.6 %collective-permute-done.5 = bf16[2,6,32,256]{3,2,1,0:T(8,128)(2,1)S(1)} collective-permute-done((bf16[2,6,32,256]{3,2,1,0:T(8,128)(2,1)S(1)}, bf16[2,6,32,256]{3,2,1,0:T(8,128)(2,1)S(1)}, u32[]{:S(2)}, u32[]{:S(2)}) %collective-permute-start.5) | collective-permute-done | bytes 196640 | tf_op jit(solution)/shard_map/ppermute | solution.py:162
  62.2 0.0 copy-start.9
  62.2 0.0 copy-start.11
  62.2 1.0 %sums.1 = f32[3,8,32,256]{3,2,1,0:T(8,128)S(1)} custom-call(bf16[2,6,32,256]{3,2,1,0:T(8,128)(2,1)S(1)} %get-tuple-element.30.own, bf16[2,6,32,256]{3,2,1,0:T(8,128)(2,1)S(1)} %collective-permute-done.10.other, f32[6,32,256]{2,1,0:T(8,128)S(1)} %get-tuple-element.44.kept1.mine1, f32[6,32,256]{2,1,0:T(8,128)S(1)} %get-tuple-element.43.theirs1, ...), custom_call_target="tpu_custom_call" | custom-call | tf_op jit(solution)/shard_map/sums/pallas_call | solution.py:261
  63.3 0.4 collective-permute-start.11
  63.7 5.4 %collective-permute-done.11 = bf16[3,4,32,256]{3,2,1,0:T(8,128)(2,1)S(1)} collective-permute-done((bf16[3,4,32,256]{3,2,1,0:T(8,128)(2,1)S(1)}, bf16[3,4,32,256]{3,2,1,0:T(8,128)(2,1)S(1)}, u32[]{:S(2)}, u32[]{:S(2)}) %collective-permute-start.11) | collective-permute-done | bytes 196640 | tf_op jit(solution)/shard_map/ppermute | solution.py:162
  69.1 0.4 collective-permute-start.12
  69.5 4.8 %collective-permute-done.12 = bf16[3,2,32,256]{3,2,0,1:T(8,128)(2,1)S(1)} collective-permute-done((bf16[3,2,32,256]{3,2,0,1:T(8,128)(2,1)S(1)}, bf16[3,2,32,256]{3,2,0,1:T(8,128)(2,1)S(1)}, u32[]{:S(2)}, u32[]{:S(2)}) %collective-permute-start.12) | collective-permute-done | bytes 98336 | tf_op jit(solution)/shard_map/ppermute | solution.py:162
  74.4 2.4 %collective-permute-start.13 = (bf16[3,1,32,256]{3,2,0,1:T(8,128)(2,1)S(1)}, bf16[3,1,32,256]{3,2,0,1:T(8,128)(2,1)S(1)}, u32[]{:S(2)}, u32[]{:S(2)}) collective-permute-start(bf16[3,1,32,256]{3,2,0,1:T(8,128)(2,1)S(1)} %dynamic-slice_convert_fusion.2), channel_id=1, source_target_pairs={{0,4},{1,5},{2,6},{3,7},{4,0},{5,1},{6,2},{7,3},{8,12},{9,13},{10,... | collective-permute-start | bytes 147464 | tf_op jit(solution)/shard_map/ppermute | solution.py:162
  76.8 0.7 collective-permute-start.9
  77.5 2.3 %collective-permute-start.6 = (bf16[1,6,32,256]{3,2,1,0:T(8,128)(2,1)S(1)}, bf16[1,6,32,256]{3,2,1,0:T(8,128)(2,1)S(1)}, u32[]{:S(2)}, u32[]{:S(2)}) collective-permute-start(bf16[1,6,32,256]{3,2,1,0:T(8,128)(2,1)S(1)} %dynamic-slice_convert_fusion.1), channel_id=1, source_target_pairs={{0,4},{1,5},{2,6},{3,7},{4,0},{5,1},{6,2},{7,3},{8,12},{9,13},{10,... | collective-permute-start | bytes 294920 | tf_op jit(solution)/shard_map/ppermute | solution.py:162
  79.8 1.0 %collective-permute-done.13 = bf16[3,1,32,256]{3,2,0,1:T(8,128)(2,1)S(1)} collective-permute-done((bf16[3,1,32,256]{3,2,0,1:T(8,128)(2,1)S(1)}, bf16[3,1,32,256]{3,2,0,1:T(8,128)(2,1)S(1)}, u32[]{:S(2)}, u32[]{:S(2)}) %collective-permute-start.13) | collective-permute-done | bytes 49184 | tf_op jit(solution)/shard_map/ppermute | solution.py:162
  80.8 0.1 collective-permute-start.14
  80.9 1.0 %collective-permute-start.15 = (bf16[3,32,256]{2,1,0:T(8,128)(2,1)S(1)}, bf16[3,32,256]{2,1,0:T(8,128)(2,1)S(1)}, u32[]{:S(2)}, u32[]{:S(2)}) collective-permute-start(bf16[3,32,256]{2,1,0:T(8,128)(2,1)S(1)} %bitcast_convert_fusion.3), channel_id=1, source_target_pairs={{0,16},{8,24},{16,0},{24,8},{1,17},{9,25},{17,1},{25,9},{2,18},{10... | collective-permute-start | bytes 147464 | tf_op jit(solution)/shard_map/ppermute | solution.py:162
  81.9 0.9 %collective-permute-start.16 = (bf16[3,32,256]{2,1,0:T(8,128)(2,1)S(1)}, bf16[3,32,256]{2,1,0:T(8,128)(2,1)S(1)}, u32[]{:S(2)}, u32[]{:S(2)}) collective-permute-start(bf16[3,32,256]{2,1,0:T(8,128)(2,1)S(1)} %bitcast_convert_fusion.3), channel_id=1, source_target_pairs={{0,24},{8,16},{16,8},{24,0},{1,25},{9,17},{17,9},{25,1},{2,26},{10... | collective-permute-start | bytes 147464 | tf_op jit(solution)/shard_map/ppermute | solution.py:162
  82.8 1.8 %collective-permute-done.9 = bf16[1,6,32,256]{3,2,1,0:T(8,128)(2,1)S(1)} collective-permute-done((bf16[1,6,32,256]{3,2,1,0:T(8,128)(2,1)S(1)}, bf16[1,6,32,256]{3,2,1,0:T(8,128)(2,1)S(1)}, u32[]{:S(2)}, u32[]{:S(2)}) %collective-permute-start.9) | collective-permute-done | bytes 98336 | tf_op jit(solution)/shard_map/ppermute | solution.py:162
  84.5 1.1 %collective-permute-done.6 = bf16[1,6,32,256]{3,2,1,0:T(8,128)(2,1)S(1)} collective-permute-done((bf16[1,6,32,256]{3,2,1,0:T(8,128)(2,1)S(1)}, bf16[1,6,32,256]{3,2,1,0:T(8,128)(2,1)S(1)}, u32[]{:S(2)}, u32[]{:S(2)}) %collective-permute-start.6) | collective-permute-done | bytes 98336 | tf_op jit(solution)/shard_map/ppermute | solution.py:162
  85.6 1.8 %columns.1 = (f32[6,32,256]{2,1,0:T(8,128)}, f32[6,32,256]{2,1,0:T(8,128)}) custom-call(s32[18]{0:T(128)S(1)} %copy-done.9, s32[12]{0:T(128)S(1)} %copy-done.11, f32[6,32,256]{2,1,0:T(8,128)S(1)} %get-tuple-element.44.kept1.mine1, bf16[6,32,256]{2,1,0:T(8,128)(2,1)S(1)} %bitcast.76, f32[6,32,256]{2,1,0:T(8,128)S(1)} %get-tuple-element.42.kept2.mine2, ...), custom_call_target="tpu_custom_call" | custom-call | tf_op jit(solution)/shard_map/columns/pallas_call | solution.py:276
  87.4 0.6 slice_bitcast_fusion
  (37 shorter events, 0.6 us)
Async XLA Ops:
  0.6 1.0 %copy-start.1 = (f32[256,256]{1,0:T(8,128)S(1)}, f32[256,256]{1,0:T(8,128)}, u32[]{:S(2)}) copy-start(f32[256,256]{1,0:T(8,128)} %inv1.1) | copy-start | bytes 786436
  1.6 0.9 %copy-start.3 = (f32[256,256]{1,0:T(8,128)S(1)}, f32[256,256]{1,0:T(8,128)}, u32[]{:S(2)}) copy-start(f32[256,256]{1,0:T(8,128)} %inv2.1) | copy-start | bytes 786436
  2.5 0.9 %copy-start.5 = (bf16[256,256]{1,0:T(8,128)(2,1)S(1)}, bf16[256,256]{1,0:T(8,128)(2,1)}, u32[]{:S(2)}) copy-start(bf16[256,256]{1,0:T(8,128)(2,1)} %refs_2_.1) | copy-start | bytes 393220
  3.4 0.9 %copy-start.6 = (bf16[6,1,32,256]{3,2,1,0:T(8,128)(2,1)S(1)}, bf16[6,1,32,256]{3,2,1,0:T(8,128)(2,1)}, u32[]{:S(2)}) copy-start(bf16[6,1,32,256]{3,2,1,0:T(8,128)(2,1)} %param.9) | copy-start | bytes 294916
  4.3 0.9 %copy-start.7 = (bf16[6,1,32,256]{3,2,1,0:T(8,128)(2,1)S(1)}, bf16[6,1,32,256]{3,2,1,0:T(8,128)(2,1)}, u32[]{:S(2)}) copy-start(bf16[6,1,32,256]{3,2,1,0:T(8,128)(2,1)} %param.10) | copy-start | bytes 294916
  5.2 0.7 copy-start.8
  5.9 0.7 copy-start.10
  8.6 7.3 %collective-permute-start = (bf16[2,3,32,256]{3,2,1,0:T(8,128)(2,1)S(1)}, bf16[2,3,32,256]{3,2,1,0:T(8,128)(2,1)S(1)}, u32[]{:S(2)}, u32[]{:S(2)}) collective-permute-start(bf16[2,3,32,256]{3,2,1,0:T(8,128)(2,1)S(1)} %get-tuple-element.18), channel_id=1, source_target_pairs={{0,0},{1,4},{2,8},{3,12},{4,16},{5,20},{6,24},{7,28},{8,1},{9,5},{... | collective-permute-start | bytes 294920 | tf_op jit(solution)/shard_map/ppermute | solution.py:204
  9.3 10.4 %collective-permute-start.1 = (bf16[2,3,32,256]{3,2,1,0:T(8,128)(2,1)S(1)}, bf16[2,3,32,256]{3,2,1,0:T(8,128)(2,1)S(1)}, u32[]{:S(2)}, u32[]{:S(2)}) collective-permute-start(bf16[2,3,32,256]{3,2,1,0:T(8,128)(2,1)S(1)} %get-tuple-element.19), channel_id=1, source_target_pairs={{0,4},{1,0},{2,12},{3,8},{4,20},{5,16},{6,28},{7,24},{8,5},{9,1},{... | collective-permute-start | bytes 294920 | tf_op jit(solution)/shard_map/ppermute | solution.py:204
  19.7 8.5 %collective-permute-start.2 = (bf16[1,2,2,3,32,256]{5,4,3,2,1,0:T(8,128)(2,1)S(1)}, bf16[1,2,2,3,32,256]{5,4,3,2,1,0:T(8,128)(2,1)S(1)}, u32[]{:S(2)}, u32[]{:S(2)}) collective-permute-start(bf16[1,2,2,3,32,256]{5,4,3,2,1,0:T(8,128)(2,1)S(1)} %maximum_bitcast_fusion), channel_id=1, source_target_pairs={{0,16},{8,24},{16,0},{24,8},{1,17},{9,25},{17,1},{25,9},{2,18},{10... | collective-permute-start | bytes 589832 | tf_op jit(solution)/shard_map/ppermute | solution.py:162
  28.3 4.5 %collective-permute-start.3 = (bf16[2,2,2,3,32,256]{5,4,3,2,1,0:T(8,128)(2,1)S(1)}, bf16[2,2,2,3,32,256]{5,4,3,2,1,0:T(8,128)(2,1)S(1)}, u32[]{:S(2)}, u32[]{:S(2)}) collective-permute-start(bf16[2,2,2,3,32,256]{5,4,3,2,1,0:T(8,128)(2,1)S(1)} %pad_maximum_fusion.1), channel_id=1, source_target_pairs={{0,8},{8,0},{16,24},{24,16},{1,9},{9,1},{17,25},{25,17},{2,10},{10... | collective-permute-start | bytes 1179656 | tf_op jit(solution)/shard_map/ppermute | solution.py:162
  28.8 0.9 %copy-start.2 = (f32[256,256]{1,0:T(8,128)S(1)}, f32[256,256]{1,0:T(8,128)}, u32[]{:S(2)}) copy-start(f32[256,256]{1,0:T(8,128)} %inv1.1) | copy-start | bytes 786436
  29.8 0.9 %copy-start.4 = (f32[256,256]{1,0:T(8,128)S(1)}, f32[256,256]{1,0:T(8,128)}, u32[]{:S(2)}) copy-start(f32[256,256]{1,0:T(8,128)} %inv2.1) | copy-start | bytes 786436
  30.7 2.2 %copy-start = (bf16[6,1,3,1,256,256]{5,4,3,2,1,0:T(8,128)(2,1)S(1)}, bf16[6,1,3,1,256,256]{5,4,3,2,1,0:T(8,128)(2,1)}, u32[]{:S(2)}) copy-start(bf16[6,1,3,1,256,256]{5,4,3,2,1,0:T(8,128)(2,1)} %param.8) | copy-start | bytes 7077892
  36.6 15.8 %collective-permute-start.7 = (bf16[4,6,32,256]{3,2,1,0:T(8,128)(2,1)S(1)}, bf16[4,6,32,256]{3,2,1,0:T(8,128)(2,1)}, u32[]{:S(2)}, u32[]{:S(2)}) collective-permute-start(bf16[4,6,32,256]{3,2,1,0:T(8,128)(2,1)S(1)} %get-tuple-element.26), channel_id=1, source_target_pairs={{0,2},{1,3},{2,0},{3,1},{4,6},{5,7},{6,4},{7,5},{8,10},{9,11},{10,... | collective-permute-start | bytes 1179656 | tf_op jit(solution)/shard_map/ppermute | solution.py:162
  38.3 17.3 %collective-permute-start.4 = (bf16[4,6,32,256]{3,2,1,0:T(8,128)(2,1)S(1)}, bf16[4,6,32,256]{3,2,1,0:T(8,128)(2,1)S(1)}, u32[]{:S(2)}, u32[]{:S(2)}) collective-permute-start(bf16[4,6,32,256]{3,2,1,0:T(8,128)(2,1)S(1)} %get-tuple-element.24), channel_id=1, source_target_pairs={{0,1},{1,0},{2,3},{3,2},{4,5},{5,4},{6,7},{7,6},{8,9},{9,8},{10,11... | collective-permute-start | bytes 1179656 | tf_op jit(solution)/shard_map/ppermute | solution.py:162
  38.6 23.6 %collective-permute-start.10 = (bf16[2,6,32,256]{3,2,1,0:T(8,128)(2,1)S(1)}, bf16[2,6,32,256]{3,2,1,0:T(8,128)(2,1)S(1)}, u32[]{:S(2)}, u32[]{:S(2)}) collective-permute-start(bf16[2,6,32,256]{3,2,1,0:T(8,128)(2,1)S(1)} %get-tuple-element.30.own), channel_id=1, source_target_pairs={{0,4},{1,5},{2,6},{3,7},{4,0},{5,1},{6,2},{7,3},{8,12},{9,13},{10,... | collective-permute-start | bytes 589832 | tf_op jit(solution)/shard_map/ppermute | solution.py:162
  53.6 6.8 %collective-permute-start.8 = (bf16[2,6,32,256]{3,2,1,0:T(8,128)(2,1)S(1)}, bf16[2,6,32,256]{3,2,1,0:T(8,128)(2,1)S(1)}, u32[]{:S(2)}, u32[]{:S(2)}) collective-permute-start(bf16[2,6,32,256]{3,2,1,0:T(8,128)(2,1)S(1)} %fusion.1), channel_id=1, source_target_pairs={{0,1},{1,0},{2,3},{3,2},{4,5},{5,4},{6,7},{7,6},{8,9},{9,8},{10,11... | collective-permute-start | bytes 589832 | tf_op jit(solution)/shard_map/ppermute | solution.py:162
  55.8 6.3 %collective-permute-start.5 = (bf16[2,6,32,256]{3,2,1,0:T(8,128)(2,1)S(1)}, bf16[2,6,32,256]{3,2,1,0:T(8,128)(2,1)S(1)}, u32[]{:S(2)}, u32[]{:S(2)}) collective-permute-start(bf16[2,6,32,256]{3,2,1,0:T(8,128)(2,1)S(1)} %fusion), channel_id=1, source_target_pairs={{0,2},{1,3},{2,0},{3,1},{4,6},{5,7},{6,4},{7,5},{8,10},{9,11},{10,... | collective-permute-start | bytes 589832 | tf_op jit(solution)/shard_map/ppermute | solution.py:162
  62.2 23.4 %copy-start.9 = (s32[18]{0:T(128)S(1)}, s32[18]{0:T(128)}, u32[]{:S(2)}) copy-start(s32[18]{0:T(128)} %struct1.3) | copy-start | bytes 220
  62.2 23.3 %copy-start.11 = (s32[12]{0:T(128)S(1)}, s32[12]{0:T(128)}, u32[]{:S(2)}) copy-start(s32[12]{0:T(128)} %struct2.3) | copy-start | bytes 148
  63.3 5.7 %collective-permute-start.11 = (bf16[3,4,32,256]{3,2,1,0:T(8,128)(2,1)S(1)}, bf16[3,4,32,256]{3,2,1,0:T(8,128)(2,1)S(1)}, u32[]{:S(2)}, u32[]{:S(2)}) collective-permute-start(bf16[3,4,32,256]{3,2,1,0:T(8,128)(2,1)S(1)} %fusion.2), channel_id=1, source_target_pairs={{0,1},{1,0},{2,3},{3,2},{4,5},{5,4},{6,7},{7,6},{8,9},{9,8},{10,11... | collective-permute-start | bytes 589832 | tf_op jit(solution)/shard_map/ppermute | solution.py:162
  69.1 5.2 %collective-permute-start.12 = (bf16[3,2,32,256]{3,2,0,1:T(8,128)(2,1)S(1)}, bf16[3,2,32,256]{3,2,0,1:T(8,128)(2,1)S(1)}, u32[]{:S(2)}, u32[]{:S(2)}) collective-permute-start(bf16[3,2,32,256]{3,2,0,1:T(8,128)(2,1)S(1)} %fusion.3), channel_id=1, source_target_pairs={{0,2},{1,3},{2,0},{3,1},{4,6},{5,7},{6,4},{7,5},{8,10},{9,11},{10,... | collective-permute-start | bytes 294920 | tf_op jit(solution)/shard_map/ppermute | solution.py:162
  74.4 6.4 %collective-permute-start.13 = (bf16[3,1,32,256]{3,2,0,1:T(8,128)(2,1)S(1)}, bf16[3,1,32,256]{3,2,0,1:T(8,128)(2,1)S(1)}, u32[]{:S(2)}, u32[]{:S(2)}) collective-permute-start(bf16[3,1,32,256]{3,2,0,1:T(8,128)(2,1)S(1)} %dynamic-slice_convert_fusion.2), channel_id=1, source_target_pairs={{0,4},{1,5},{2,6},{3,7},{4,0},{5,1},{6,2},{7,3},{8,12},{9,13},{10,... | collective-permute-start | bytes 147464 | tf_op jit(solution)/shard_map/ppermute | solution.py:162
  76.8 7.7 %collective-permute-start.9 = (bf16[1,6,32,256]{3,2,1,0:T(8,128)(2,1)S(1)}, bf16[1,6,32,256]{3,2,1,0:T(8,128)(2,1)S(1)}, u32[]{:S(2)}, u32[]{:S(2)}) collective-permute-start(bf16[1,6,32,256]{3,2,1,0:T(8,128)(2,1)S(1)} %dynamic-slice_convert_fusion), channel_id=1, source_target_pairs={{0,4},{1,5},{2,6},{3,7},{4,0},{5,1},{6,2},{7,3},{8,12},{9,13},{10,... | collective-permute-start | bytes 294920 | tf_op jit(solution)/shard_map/ppermute | solution.py:162
  77.5 8.1 %collective-permute-start.6 = (bf16[1,6,32,256]{3,2,1,0:T(8,128)(2,1)S(1)}, bf16[1,6,32,256]{3,2,1,0:T(8,128)(2,1)S(1)}, u32[]{:S(2)}, u32[]{:S(2)}) collective-permute-start(bf16[1,6,32,256]{3,2,1,0:T(8,128)(2,1)S(1)} %dynamic-slice_convert_fusion.1), channel_id=1, source_target_pairs={{0,4},{1,5},{2,6},{3,7},{4,0},{5,1},{6,2},{7,3},{8,12},{9,13},{10,... | collective-permute-start | bytes 294920 | tf_op jit(solution)/shard_map/ppermute | solution.py:162
  80.8 6.5 %collective-permute-start.14 = (bf16[3,32,256]{2,1,0:T(8,128)(2,1)S(1)}, bf16[3,32,256]{2,1,0:T(8,128)(2,1)S(1)}, u32[]{:S(2)}, u32[]{:S(2)}) collective-permute-start(bf16[3,32,256]{2,1,0:T(8,128)(2,1)S(1)} %bitcast_convert_fusion.3), channel_id=1, source_target_pairs={{0,8},{8,0},{16,24},{24,16},{1,9},{9,1},{17,25},{25,17},{2,10},{10... | collective-permute-start | bytes 147464 | tf_op jit(solution)/shard_map/ppermute | solution.py:162
  80.9 6.5 %collective-permute-start.15 = (bf16[3,32,256]{2,1,0:T(8,128)(2,1)S(1)}, bf16[3,32,256]{2,1,0:T(8,128)(2,1)S(1)}, u32[]{:S(2)}, u32[]{:S(2)}) collective-permute-start(bf16[3,32,256]{2,1,0:T(8,128)(2,1)S(1)} %bitcast_convert_fusion.3), channel_id=1, source_target_pairs={{0,16},{8,24},{16,0},{24,8},{1,17},{9,25},{17,1},{25,9},{2,18},{10... | collective-permute-start | bytes 147464 | tf_op jit(solution)/shard_map/ppermute | solution.py:162
  81.9 5.5 %collective-permute-start.16 = (bf16[3,32,256]{2,1,0:T(8,128)(2,1)S(1)}, bf16[3,32,256]{2,1,0:T(8,128)(2,1)S(1)}, u32[]{:S(2)}, u32[]{:S(2)}) collective-permute-start(bf16[3,32,256]{2,1,0:T(8,128)(2,1)S(1)} %bitcast_convert_fusion.3), channel_id=1, source_target_pairs={{0,24},{8,16},{16,8},{24,0},{1,25},{9,17},{17,9},{25,1},{2,26},{10... | collective-permute-start | bytes 147464 | tf_op jit(solution)/shard_map/ppermute | solution.py:162
where the time goes:
time: 88.4 us; the launch traced here: 88.1 us
  waiting for transfers between devices  38.9 us (44%)
  starting transfers between devices  27.4 us (31%)
  Pallas kernels  10.5 us (12%)
  local copies, waits for them, and re-layouts  8.71 us (10%)
  other arithmetic  1.57 us (2%)
  between operations  0.9 us (1%)
    ppermute x15, waiting for transfers between devices, swapped(): return lax.ppermute(value, axis, [(i, i ^ mask) for i in range(size)])  35.1 us
    ppermute x15, starting transfers between devices, swapped(): return lax.ppermute(value, axis, [(i, i ^ mask) for i in range(size)])  20.1 us
    unnamed x24, local copies, waits for them, and re-layouts  7.81 us
    ppermute x2, starting transfers between devices, body(): got.append(lax.ppermute(part, ('row', 'col'), moves))  7.3 us
    ppermute x2, waiting for transfers between devices, body(): got.append(lax.ppermute(part, ('row', 'col'), moves))  3.82 us
    pallas_call x1, Pallas kernels, body(): pl.pallas_call(functools.partial(product_kernel, n_row, n_col, (orders[0]...  3.63 us
    pallas_call x1, Pallas kernels, body(): pl.pallas_call(functools.partial(factor_kernel, n_row, cycle), out_shape=...  2.05 us
    pallas_call x1, Pallas kernels, body(): pl.pallas_call(gram_kernel, out_shape=shape((3, slab, width), f32), in_sp...  2.05 us
  transfers between devices with their start and end apart: 17, of which 10 were waited for; matrix products, arithmetic and copies ran while one was open for 2% of the time, Pallas kernels for 4%

commit v1 on v0

--- a/solution.py
+++ b/solution.py
@@ -11,6 +11,7 @@
 SMEM = pl.BlockSpec(memory_space=pltpu.SMEM)
 VMEM = pl.BlockSpec(memory_space=pltpu.VMEM)
 HBM = pl.BlockSpec(memory_space=pltpu.HBM)
+ANY = pl.BlockSpec(memory_space=pl.ANY)
 
 
 def exact_dot(left, right, left_dim=1):
@@ -45,37 +46,12 @@
     return found == 1
 
 
-def factor_kernel(n_row, cycle, struct1, struct2, *refs):
-    sources, (own, linked, *parts) = refs[:5], refs[5 : 7 + cycle]
-    held, sems = refs[7 + cycle : 12 + cycle], refs[12 + cycle]
-    copies = [pltpu.make_async_copy(a, b, sems.at[i]) for i, (a, b) in enumerate(zip(sources, held))]
-    for copy in copies:
-        copy.start()
-    panel1, panel2, link, inv1, inv2 = held
-    blocks, slab, width = panel1.shape
-    keep = [listed(struct, blocks, n_row) for struct in (struct1, struct2)]
-    turn = lax.rem(lax.axis_index("col"), cycle)
-    for copy in copies:
-        copy.wait()
-    for p, (panel, inverse) in enumerate(((panel1, inv1), (panel2, inv2))):
-        rows = panel[...].astype(jnp.float32).reshape(blocks * slab, width)
-        product = exact_dot(rows, inverse[...]).reshape(blocks, slab, width)
-        own[p] = jnp.where(keep[p], product, 0.0).astype(jnp.bfloat16)
-    for s, part in enumerate(parts):
-        pick = lax.rem(s - turn + cycle, cycle)
-        for p in range(2):
-            for b in range(blocks // cycle):
-                part[p, b] = own[p, b * cycle + pick]
-    linked[...] = exact_dot(link[...].astype(jnp.float32), inv2[...])
-
-
-def product_kernel(n_row, n_col, first_bits, stored, pieces, *rest):
+def product_kernel(n_row, n_col, first_bits, struct1, struct2, inv1, inv2, stored, pieces, *rest):
     cycle = n_col // n_row
     keeps, sends = rest[:2], rest[2:4]
     held, loose, factor, sems = rest[4:]
     row_blocks = held.shape[0]
-    col_blocks, _, slab, double = loose.shape
-    width = double // 2
+    _, col_blocks, _, slab, width = loose.shape
     here_row, here_col = lax.axis_index("row"), lax.axis_index("col")
     copies = [pltpu.make_async_copy(stored.at[a], held.at[a], sems.at[a]) for a in range(row_blocks)]
     for copy in copies:
@@ -87,9 +63,18 @@
             slot = (here_row ^ m) * cycle + lax.rem(s - group + cycle, cycle)
             for p in range(2):
                 for b in range(col_blocks):
-                    loose[b, slot, :, p * width : (p + 1) * width] = pieces[m, s, p, b].astype(jnp.float32)
-    for b in range(col_blocks):
-        factor[b] = loose[b].reshape(n_col * slab, double).astype(jnp.bfloat16)
+                    loose[p, b, slot] = pieces[m, s, p, b].astype(jnp.float32)
+    for p, (struct, inverse) in enumerate(((struct1, inv1), (struct2, inv2))):
+
+        def look(place, found):
+            return tuple(f | (struct[place] == b * n_col + here_col).astype(jnp.int32) for b, f in enumerate(found))
+
+        found = lax.fori_loop(0, struct.shape[0], look, (jnp.int32(0),) * col_blocks)
+        blocks = loose[p].reshape(col_blocks * n_col * slab, width).astype(jnp.bfloat16)
+        product = split_dot(blocks, inverse[...])
+        for b in range(col_blocks):
+            block = product[b * width : (b + 1) * width]
+            factor[b, :, p * width : (p + 1) * width] = jnp.where(found[b] == 1, block, 0.0).astype(jnp.bfloat16)
 
     for a in range(row_blocks):
         copies[a].wait()
@@ -108,7 +93,26 @@
                 sends[p][j, a] = jnp.where(upper, x, y).astype(jnp.bfloat16)
 
 
-def sum_kernel(own, other, mine1, theirs1, mine2, theirs2, linked, out):
+def prepare_kernel(n_row, struct1, struct2, mine1, mine2, other1, other2, link, inv1, inv2, after, rows, linked, out, whole):
+    blocks, slab, width = mine1.shape
+    for p, (struct, inverse, parts) in enumerate(((struct1, inv1, (mine1, other1)), (struct2, inv2, (mine2, other2)))):
+        keep = listed(struct, blocks, n_row)
+        for i, part in enumerate(parts):
+            flat = part[...].astype(jnp.float32).reshape(blocks * slab, width).astype(jnp.bfloat16)
+            product = split_dot(flat, inverse[...]).reshape(blocks, slab, width)
+            rows[p, i] = jnp.where(keep, product, 0.0).astype(jnp.bfloat16)
+    linked[...] = exact_dot(link[...].astype(jnp.float32), inv2[...])
+    link = linked[...]
+    gram1 = exact_dot(inv1[...], inv1[...], 0)
+    across = exact_dot(gram1, link)
+    whole[0] = gram1
+    whole[1] = -across
+    whole[2] = exact_dot(inv2[...], inv2[...], 0) + exact_dot(link, across, 0)
+    place = pl.ds(pl.multiple_of(lax.axis_index("col") * slab, slab), slab)
+    out[...] = whole[:, place, :]
+
+
+def sum_kernel(rows, mine1, theirs1, mine2, theirs2, linked, after, out):
     blocks, slab, width = mine1.shape
     flat = (blocks * slab, width)
 
@@ -116,7 +120,7 @@
         return jnp.concatenate([a.reshape(flat), b.reshape(flat)], axis=0)
 
     def factor(p):
-        return both(own[p].astype(jnp.float32), other[p].astype(jnp.float32)).astype(jnp.bfloat16)
+        return rows[p].astype(jnp.float32).reshape(2 * blocks * slab, width).astype(jnp.bfloat16)
 
     link = linked[...]
     sum1 = both(mine1[...], theirs1[...])
@@ -139,23 +143,6 @@
     column1[...] = col1
     carried = split_dot(col1.reshape(blocks * slab, width), linked[...]).reshape(sum2.shape)
     column2[...] = jnp.where(listed(struct2, blocks, n_row), -(sum2 + carried), 0.0)
-
-
-def gram_kernel(inv1, inv2, linked, out, held1, held2, whole, sems):
-    copies = [pltpu.make_async_copy(inv1, held1, sems.at[0]), pltpu.make_async_copy(inv2, held2, sems.at[1])]
-    for copy in copies:
-        copy.start()
-    for copy in copies:
-        copy.wait()
-    slab = out.shape[1]
-    link = linked[...]
-    gram1 = exact_dot(held1[...], held1[...], 0)
-    across = exact_dot(gram1, link)
-    whole[0] = gram1
-    whole[1] = -across
-    whole[2] = exact_dot(held2[...], held2[...], 0) + exact_dot(link, across, 0)
-    place = pl.ds(pl.multiple_of(lax.axis_index("col") * slab, slab), slab)
-    out[...] = whole[:, place, :]
 
 
 def swapped(value, axis, size, mask):
@@ -180,67 +167,61 @@
     big = pltpu.CompilerParams(vmem_limit_bytes=24 * 1024 * 1024)
     stored = stored_inverse.reshape(row_blocks, col_blocks, width, width)
     panel = (row_blocks, slab, width)
-    square = pltpu.VMEM((width, width), f32)
-
-    own, linked, *parts = pl.pallas_call(
-        functools.partial(factor_kernel, n_row, cycle),
-        out_shape=[shape((2,) + panel, bf16), shape((width, width), f32)]
-        + [shape((2, col_blocks, slab, width), bf16)] * cycle,
-        in_specs=[SMEM, SMEM] + [HBM] * 5,
-        out_specs=[VMEM] * (2 + cycle),
-        scratch_shapes=[pltpu.VMEM(panel, bf16)] * 2
-        + [pltpu.VMEM((width, width), bf16), square, square, pltpu.SemaphoreType.DMA((5,))],
-        compiler_params=big,
-        name="factors",
-    )(struct_first, struct_second, panel_first.reshape(panel), panel_second.reshape(panel), panel_link, inv_first, inv_second)
-
+
+    panels = [panel_first.reshape(panel), panel_second.reshape(panel)]
+
+    turns = [p.reshape(col_blocks, cycle, slab, width) for p in panels]
     got = []
-    for s, part in enumerate(parts):
+    for s in range(cycle):
         moves = []
         for r in range(n_row):
             for c in range(n_col):
                 j = (s - c) % cycle
                 moves.append((r * n_col + c, (c // cycle) * n_col + r + j * n_row))
+        pick = (s - here_col) % cycle
+        part = jnp.stack([lax.dynamic_index_in_dim(t, pick, 1, keepdims=False) for t in turns])
         got.append(lax.ppermute(part, ("row", "col"), moves))
     pieces = jnp.stack(got)[None]
-
-    consts = pl.pallas_call(
-        gram_kernel,
-        out_shape=shape((3, slab, width), f32),
-        in_specs=[HBM, HBM, VMEM],
-        out_specs=VMEM,
-        scratch_shapes=[square, square, pltpu.VMEM((3, width, width), f32), pltpu.SemaphoreType.DMA((2,))],
-        compiler_params=big,
-        name="grams",
-        cost_estimate=pl.CostEstimate(flops=6 * 8 * width**3, bytes_accessed=8 * width**2, transcendentals=0),
-    )(inv_first, inv_second, linked)
+    others = [swapped(p, "col", n_col, n_col // 2) for p in panels]
 
     order = [0]
     bit = n_row // 2
     while bit:
+        if bit == 1:
+            pieces, others[0] = lax.optimization_barrier((pieces, others[0]))
         pieces = jnp.concatenate([pieces, swapped(pieces, "row", n_row, bit)])
         order += [o ^ bit for o in order]
         bit //= 2
     pieces = jnp.stack([pieces[order.index(m)] for m in range(n_row)])
-    pieces, consts, own = lax.optimization_barrier((pieces, consts, own))
-    other = swapped(own, "col", n_col, n_col // 2)
+    pieces, others[1] = lax.optimization_barrier((pieces, others[1]))
 
     orders = (list(range(n_bits)), [1, 0] + list(range(2, n_bits)))
     half = (n_col // 2,) + panel
     split = pl.pallas_call(
         functools.partial(product_kernel, n_row, n_col, (orders[0][0], orders[1][0])),
         out_shape=[shape(half, f32)] * 2 + [shape(half, bf16)] * 2,
-        in_specs=[HBM, VMEM],
+        in_specs=[SMEM, SMEM, VMEM, VMEM, HBM, VMEM],
         out_specs=[VMEM] * 4,
         scratch_shapes=[
             pltpu.VMEM(stored.shape, bf16),
-            pltpu.VMEM((col_blocks, n_col, slab, 2 * width), f32),
+            pltpu.VMEM((2, col_blocks, n_col, slab, width), f32),
             pltpu.VMEM((col_blocks, width, 2 * width), bf16),
             pltpu.SemaphoreType.DMA((row_blocks,)),
         ],
         compiler_params=big,
         name="products",
-    )(stored, pieces)
+    )(struct_first, struct_second, inv_first, inv_second, stored, pieces)
+
+    rows, linked, consts = pl.pallas_call(
+        functools.partial(prepare_kernel, n_row),
+        out_shape=[shape((2, 2) + panel, bf16), shape((width, width), f32), shape((3, slab, width), f32)],
+        in_specs=[SMEM, SMEM] + [VMEM] * 7 + [ANY],
+        out_specs=[VMEM] * 3,
+        scratch_shapes=[pltpu.VMEM((3, width, width), f32)],
+        compiler_params=big,
+        name="prepare",
+        cost_estimate=pl.CostEstimate(flops=6 * 10 * width**3, bytes_accessed=8 * width**2, transcendentals=0),
+    )(struct_first, struct_second, *panels, *others, panel_link, inv_first, inv_second, split[0])
 
     last = []
     for p in range(2):
@@ -261,18 +242,20 @@
     sums = pl.pallas_call(
         sum_kernel,
         out_shape=shape((3, n_col, slab, width), f32),
-        in_specs=[VMEM] * 7,
+        in_specs=[VMEM] * 6 + [ANY],
         out_specs=VMEM,
         compiler_params=big,
         name="sums",
-    )(own, other, last[0][0], last[0][1], last[1][0], last[1][1], linked)
-    for bit in range(n_bits):
-        keep, send = halves(sums.reshape(3, -1, 2, slab, width), 2, (here_col >> bit) & 1)
-        sums = keep + swapped(send, "col", n_col, 1 << bit).astype(f32)
-
+    )(rows, last[0][0], last[0][1], last[1][0], last[1][1], linked, consts)
     done = []
     for keep, _, send in last:
         done += [keep, swapped(send, "col", n_col, n_col // 2).reshape(panel)]
+    for bit in range(n_bits):
+        if bit == n_bits - 1:
+            sums, done = lax.optimization_barrier((sums, done))
+        keep, send = halves(sums.reshape(3, -1, 2, slab, width), 2, (here_col >> bit) & 1)
+        sums = keep + swapped(send, "col", n_col, 1 << bit).astype(f32)
+
     column_first, column_second = pl.pallas_call(
         functools.partial(column_kernel, n_row),
         out_shape=[shape(panel, f32)] * 2,

time: 88.4 us -> 84.8 us (0.959)
  waiting for transfers between devices: 38.9 us -> 46.3 us
  local copies, waits for them, and re-layouts: 8.71 us -> 2.64 us
  starting transfers between devices: 27.4 us -> 21.5 us
  Pallas kernels: 10.5 us -> 11.7 us
    unnamed x24 -> x16, local copies, waits for them, and re-layouts: 7.81 us -> 0.05 us
    ppermute x15 -> x16, waiting for transfers between devices: 35.1 us -> 42.5 us  [swapped(): return lax.ppermute(value, axis, [(i, i ^ mask) for i in range(size)])]
    ppermute x15 -> x16, starting transfers between devices: 20.1 us -> 13.9 us  [swapped(): return lax.ppermute(value, axis, [(i, i ^ mask) for i in range(size)])]
    pallas_call x1, Pallas kernels: 3.63 us -> 5.51 us  [body(): pl.pallas_call(functools.partial(product_kernel, n_row, n_col, (orders[0]...]
    another operation x0 -> x2, local copies, waits for them, and re-layouts: none -> 1.67 us  [body(): jnp.stack([lax.dynamic_index_in_dim(t, pick, 1, keepdims=False) for t in...]
    pallas_call x2 -> x1, Pallas kernels: 4.1 us -> 3.33 us  [body(): pl.pallas_call(functools.partial(prepare_kernel, n_row), out_shape=[shape...]
  transfers between devices with their start and end apart: 17 -> 18, of which waited for: 10 -> 14; matrix products, arithmetic and copies ran while one was open for 2% -> 2% of each run, Pallas kernels for 4% -> 6%
where the time goes in v1:
time: 84.8 us; the launch traced here: 84.6 us
  waiting for transfers between devices  46.3 us (55%)
  starting transfers between devices  21.5 us (25%)
  Pallas kernels  11.7 us (14%)
  local copies, waits for them, and re-layouts  2.64 us (3%)
  other arithmetic  1.56 us (2%)
  between operations  0.98 us (1%)
    ppermute x16, waiting for transfers between devices, swapped(): return lax.ppermute(value, axis, [(i, i ^ mask) for i in range(size)])  42.5 us
    ppermute x16, starting transfers between devices, swapped(): return lax.ppermute(value, axis, [(i, i ^ mask) for i in range(size)])  13.9 us
    ppermute x2, starting transfers between devices, body(): got.append(lax.ppermute(part, ('row', 'col'), moves))  7.56 us
    pallas_call x1, Pallas kernels, body(): pl.pallas_call(functools.partial(product_kernel, n_row, n_col, (orders[0]...  5.51 us
    ppermute x2, waiting for transfers between devices, body(): got.append(lax.ppermute(part, ('row', 'col'), moves))  3.82 us
    pallas_call x1, Pallas kernels, body(): pl.pallas_call(functools.partial(prepare_kernel, n_row), out_shape=[shape...  3.33 us
    pallas_call x1, Pallas kernels, body(): pl.pallas_call(functools.partial(column_kernel, n_row), out_shape=[shape(...  1.78 us
  transfers between devices with their start and end apart: 18, of which 14 were waited for; matrix products, arithmetic and copies ran while one was open for 2% of the time, Pallas kernels for 6%

profile of v1, /device:TPU:0, one launch (start us, length us, event | category | flops | bytes accessed | tf_op | source)
XLA Modules:
  0.0 84.6 jit_solution(15396358737681087128)
XLA Ops:
  0.7 0.8 dynamic-slice_bitcast_fusion.7
  1.5 0.8 dynamic-slice_bitcast_fusion.6
  2.4 0.0 copy-start.1
  2.4 0.0 copy-start.2
  2.4 0.0 copy-start.5
  2.4 0.0 copy-start.6
  2.4 0.8 collective-permute-start
  3.3 6.8 %collective-permute-start.1 = (bf16[2,3,32,256]{3,2,1,0:T(8,128)(2,1)S(1)}, bf16[2,3,32,256]{3,2,1,0:T(8,128)(2,1)S(1)}, u32[]{:S(2)}, u32[]{:S(2)}) collective-permute-start(bf16[2,3,32,256]{3,2,1,0:T(8,128)(2,1)S(1)} %pad_maximum_fusion.3), channel_id=1, source_target_pairs={{0,4},{1,0},{2,12},{3,8},{4,20},{5,16},{6,28},{7,24},{8,5},{9,1},{... | collective-permute-start | bytes 294920 | tf_op jit(solution)/shard_map/ppermute | solution.py:183
  10.0 3.8 %collective-permute-done.1 = bf16[2,3,32,256]{3,2,1,0:T(8,128)(2,1)S(1)} collective-permute-done((bf16[2,3,32,256]{3,2,1,0:T(8,128)(2,1)S(1)}, bf16[2,3,32,256]{3,2,1,0:T(8,128)(2,1)S(1)}, u32[]{:S(2)}, u32[]{:S(2)}) %collective-permute-start.1) | collective-permute-done | bytes 98336 | tf_op jit(solution)/shard_map/ppermute | solution.py:183
  13.9 3.4 %collective-permute-start.2 = (bf16[1,2,2,3,32,256]{5,4,3,2,1,0:T(8,128)(2,1)S(1)}, bf16[1,2,2,3,32,256]{5,4,3,2,1,0:T(8,128)(2,1)S(1)}, u32[]{:S(2)}, u32[]{:S(2)}) collective-permute-start(bf16[1,2,2,3,32,256]{5,4,3,2,1,0:T(8,128)(2,1)S(1)} %maximum_bitcast_fusion), channel_id=1, source_target_pairs={{0,16},{8,24},{16,0},{24,8},{1,17},{9,25},{17,1},{25,9},{2,18},{10... | collective-permute-start | bytes 589832 | tf_op jit(solution)/shard_map/ppermute | solution.py:149
  17.2 1.3 %collective-permute-start.3 = (bf16[6,32,256]{2,1,0:T(8,128)(2,1)}, bf16[6,32,256]{2,1,0:T(8,128)(2,1)S(1)}, u32[]{:S(2)}, u32[]{:S(2)}) collective-permute-start(bf16[6,32,256]{2,1,0:T(8,128)(2,1)} %bitcast.95), channel_id=1, source_target_pairs={{0,4},{1,5},{2,6},{3,7},{4,0},{5,1},{6,2},{7,3},{8,12},{9,13},{10,... | collective-permute-start | bytes 294920 | tf_op jit(solution)/shard_map/ppermute | solution.py:149
  18.6 3.8 %collective-permute-done.2 = bf16[1,2,2,3,32,256]{5,4,3,2,1,0:T(8,128)(2,1)S(1)} collective-permute-done((bf16[1,2,2,3,32,256]{5,4,3,2,1,0:T(8,128)(2,1)S(1)}, bf16[1,2,2,3,32,256]{5,4,3,2,1,0:T(8,128)(2,1)S(1)}, u32[]{:S(2)}, u32[]{:S(2)}) %collective-permute-start.2) | collective-permute-done | bytes 196640 | tf_op jit(solution)/shard_map/ppermute | solution.py:149
  22.4 3.2 %collective-permute-done.3.other1 = bf16[6,32,256]{2,1,0:T(8,128)(2,1)S(1)} collective-permute-done((bf16[6,32,256]{2,1,0:T(8,128)(2,1)}, bf16[6,32,256]{2,1,0:T(8,128)(2,1)S(1)}, u32[]{:S(2)}, u32[]{:S(2)}) %collective-permute-start.3) | collective-permute-done | bytes 98336 | tf_op jit(solution)/shard_map/ppermute | solution.py:149
  25.6 0.1 collective-permute-start.4
  25.7 1.6 %collective-permute-done.4 = bf16[2,2,2,3,32,256]{5,4,3,2,1,0:T(8,128)(2,1)S(1)} collective-permute-done((bf16[2,2,2,3,32,256]{5,4,3,2,1,0:T(8,128)(2,1)S(1)}, bf16[2,2,2,3,32,256]{5,4,3,2,1,0:T(8,128)(2,1)S(1)}, u32[]{:S(2)}, u32[]{:S(2)}) %collective-permute-start.4) | collective-permute-done | bytes 393248 | tf_op jit(solution)/shard_map/ppermute | solution.py:149
  27.3 0.0 copy-start.3
  27.3 0.0 copy-start.4
  27.4 0.0 copy-start.7
  27.4 0.1 pad_maximum_fusion.pieces
  27.5 6.3 %collective-permute-done.5.other2 = bf16[6,32,256]{2,1,0:T(8,128)(2,1)S(1)} collective-permute-done((bf16[6,32,256]{2,1,0:T(8,128)(2,1)}, bf16[6,32,256]{2,1,0:T(8,128)(2,1)S(1)}, u32[]{:S(2)}, u32[]{:S(2)}) %collective-permute-start.5) | collective-permute-done | bytes 98336 | tf_op jit(solution)/shard_map/ppermute | solution.py:149
  33.8 5.5 %products.1 = (f32[4,6,32,256]{3,2,1,0:T(8,128)S(1)}, f32[4,6,32,256]{3,2,1,0:T(8,128)S(1)}, bf16[4,6,32,256]{3,2,1,0:T(8,128)(2,1)S(1)}, bf16[4,6,32,256]{3,2,1,0:T(8,128)(2,1)S(1)}) custom-call(s32[18]{0:T(128)S(1)} %copy-done.5, s32[12]{0:T(128)S(1)} %copy-done.6, f32[256,256]{1,0:T(8,128)S(1)} %copy-done.1, f32[256,256]{1,0:T(8,128)S(1)} %copy-done.2, ...), custom_call_target="tpu_custom_call" | custom-call | tf_op jit(solution)/shard_map/products/pallas_call | solution.py:200
  39.3 0.1 collective-permute-start.8
  39.4 0.9 %collective-permute-start.6 = (bf16[4,6,32,256]{3,2,1,0:T(8,128)(2,1)S(1)}, bf16[4,6,32,256]{3,2,1,0:T(8,128)(2,1)S(1)}, u32[]{:S(2)}, u32[]{:S(2)}) collective-permute-start(bf16[4,6,32,256]{3,2,1,0:T(8,128)(2,1)S(1)} %get-tuple-element.29), channel_id=1, source_target_pairs={{0,1},{1,0},{2,3},{3,2},{4,5},{5,4},{6,7},{7,6},{8,9},{9,8},{10,11... | collective-permute-start | bytes 1179656 | tf_op jit(solution)/shard_map/ppermute | solution.py:149
  40.3 3.3 %prepare.1 = (bf16[2,2,6,32,256]{4,3,2,1,0:T(8,128)(2,1)S(1)}, f32[256,256]{1,0:T(8,128)S(1)}, f32[3,32,256]{2,1,0:T(8,128)S(1)}) custom-call(s32[18]{0:T(128)S(1)} %copy-done.5, s32[12]{0:T(128)S(1)} %copy-done.6, bf16[6,32,256]{2,1,0:T(8,128)(2,1)S(1)} %bitcast.96, bf16[6,32,256]{2,1,0:T(8,128)(2,1)S(1)} %bitcast.93, ...), custom_call_target="tpu_custom_call" | custom-call | flops 1006632960 | bytes 524288 | tf_op jit(solution)/shard_map/prepare/pallas_call | solution.py:215
  43.6 6.9 %collective-permute-done.8 = bf16[4,6,32,256]{3,2,1,0:T(8,128)(2,1)} collective-permute-done((bf16[4,6,32,256]{3,2,1,0:T(8,128)(2,1)S(1)}, bf16[4,6,32,256]{3,2,1,0:T(8,128)(2,1)}, u32[]{:S(2)}, u32[]{:S(2)}) %collective-permute-start.8) | collective-permute-done | bytes 393248 | tf_op jit(solution)/shard_map/ppermute | solution.py:149
  50.6 1.1 %convert_add_fusion = f32[4,6,32,256]{3,2,1,0:T(8,128)S(1)} fusion(f32[4,6,32,256]{3,2,1,0:T(8,128)S(1)} %get-tuple-element.30, bf16[4,6,32,256]{3,2,1,0:T(8,128)(2,1)} %collective-permute-done.8), kind=kLoop, calls=%fused_computation.1 | loop fusion | flops 393216 | bytes 1966080 | tf_op jit(solution)/shard_map/add | solution.py:234
  51.7 0.9 %collective-permute-start.9 = (bf16[2,6,32,256]{3,2,1,0:T(8,128)(2,1)S(1)}, bf16[2,6,32,256]{3,2,1,0:T(8,128)(2,1)S(1)}, u32[]{:S(2)}, u32[]{:S(2)}) collective-permute-start(bf16[2,6,32,256]{3,2,1,0:T(8,128)(2,1)S(1)} %fusion.1), channel_id=1, source_target_pairs={{0,1},{1,0},{2,3},{3,2},{4,5},{5,4},{6,7},{7,6},{8,9},{9,8},{10,11... | collective-permute-start | bytes 589832 | tf_op jit(solution)/shard_map/ppermute | solution.py:149
  52.6 0.1 convert_add_fusion.1
  52.8 0.4 collective-permute-start.7
  53.1 4.7 %collective-permute-done.9 = bf16[2,6,32,256]{3,2,1,0:T(8,128)(2,1)S(1)} collective-permute-done((bf16[2,6,32,256]{3,2,1,0:T(8,128)(2,1)S(1)}, bf16[2,6,32,256]{3,2,1,0:T(8,128)(2,1)S(1)}, u32[]{:S(2)}, u32[]{:S(2)}) %collective-permute-start.9) | collective-permute-done | bytes 196640 | tf_op jit(solution)/shard_map/ppermute | solution.py:149
  57.9 0.7 collective-permute-done.7
  58.7 1.0 %sums.1 = f32[3,8,32,256]{3,2,1,0:T(8,128)S(1)} custom-call(bf16[2,2,6,32,256]{4,3,2,1,0:T(8,128)(2,1)S(1)} %get-tuple-element.28.rows, f32[6,32,256]{2,1,0:T(8,128)S(1)} %get-tuple-element.34.mine1.kept1, f32[6,32,256]{2,1,0:T(8,128)S(1)} %get-tuple-element.53.theirs1, f32[6,32,256]{2,1,0:T(8,128)S(1)} %get-tuple-element.36.mine2.kept2, ...), custom_call_target="tpu_custom_call" | custom-call | tf_op jit(solution)/shard_map/sums/pallas_call | solution.py:242
  59.7 1.2 %collective-permute-start.10 = (bf16[3,4,32,256]{3,2,1,0:T(8,128)(2,1)S(1)}, bf16[3,4,32,256]{3,2,1,0:T(8,128)(2,1)S(1)}, u32[]{:S(2)}, u32[]{:S(2)}) collective-permute-start(bf16[3,4,32,256]{3,2,1,0:T(8,128)(2,1)S(1)} %fusion.2), channel_id=1, source_target_pairs={{0,1},{1,0},{2,3},{3,2},{4,5},{5,4},{6,7},{7,6},{8,9},{9,8},{10,11... | collective-permute-start | bytes 589832 | tf_op jit(solution)/shard_map/ppermute | solution.py:149
  61.0 0.7 collective-permute-start.13
  61.7 3.8 %collective-permute-done.10 = bf16[3,4,32,256]{3,2,1,0:T(8,128)(2,1)S(1)} collective-permute-done((bf16[3,4,32,256]{3,2,1,0:T(8,128)(2,1)S(1)}, bf16[3,4,32,256]{3,2,1,0:T(8,128)(2,1)S(1)}, u32[]{:S(2)}, u32[]{:S(2)}) %collective-permute-start.10) | collective-permute-done | bytes 196640 | tf_op jit(solution)/shard_map/ppermute | solution.py:149
  65.6 0.7 collective-permute-start.11
  66.2 1.8 %collective-permute-start.12 = (bf16[1,6,32,256]{3,2,1,0:T(8,128)(2,1)S(1)}, bf16[1,6,32,256]{3,2,1,0:T(8,128)(2,1)S(1)}, u32[]{:S(2)}, u32[]{:S(2)}) collective-permute-start(bf16[1,6,32,256]{3,2,1,0:T(8,128)(2,1)S(1)} %dynamic-slice_convert_fusion.1), channel_id=1, source_target_pairs={{0,4},{1,5},{2,6},{3,7},{4,0},{5,1},{6,2},{7,3},{8,12},{9,13},{10,... | collective-permute-start | bytes 294920 | tf_op jit(solution)/shard_map/ppermute | solution.py:149
  68.1 2.7 %collective-permute-done.11 = bf16[3,2,32,256]{3,2,0,1:T(8,128)(2,1)S(1)} collective-permute-done((bf16[3,2,32,256]{3,2,0,1:T(8,128)(2,1)S(1)}, bf16[3,2,32,256]{3,2,0,1:T(8,128)(2,1)S(1)}, u32[]{:S(2)}, u32[]{:S(2)}) %collective-permute-start.11) | collective-permute-done | bytes 98336 | tf_op jit(solution)/shard_map/ppermute | solution.py:149
  70.8 2.6 %collective-permute-done.12 = bf16[1,6,32,256]{3,2,1,0:T(8,128)(2,1)S(1)} collective-permute-done((bf16[1,6,32,256]{3,2,1,0:T(8,128)(2,1)S(1)}, bf16[1,6,32,256]{3,2,1,0:T(8,128)(2,1)S(1)}, u32[]{:S(2)}, u32[]{:S(2)}) %collective-permute-start.12) | collective-permute-done | bytes 98336 | tf_op jit(solution)/shard_map/ppermute | solution.py:149
  73.4 0.5 collective-permute-start.14
  73.9 5.0 %collective-permute-done.14 = bf16[3,1,32,256]{3,2,0,1:T(8,128)(2,1)S(1)} collective-permute-done((bf16[3,1,32,256]{3,2,0,1:T(8,128)(2,1)S(1)}, bf16[3,1,32,256]{3,2,0,1:T(8,128)(2,1)S(1)}, u32[]{:S(2)}, u32[]{:S(2)}) %collective-permute-start.14) | collective-permute-done | bytes 49184 | tf_op jit(solution)/shard_map/ppermute | solution.py:149
  78.9 0.1 collective-permute-start.15
  79.0 1.2 %collective-permute-start.16 = (bf16[3,32,256]{2,1,0:T(8,128)(2,1)S(1)}, bf16[3,32,256]{2,1,0:T(8,128)(2,1)S(1)}, u32[]{:S(2)}, u32[]{:S(2)}) collective-permute-start(bf16[3,32,256]{2,1,0:T(8,128)(2,1)S(1)} %bitcast_convert_fusion.3), channel_id=1, source_target_pairs={{0,16},{8,24},{16,0},{24,8},{1,17},{9,25},{17,1},{25,9},{2,18},{10... | collective-permute-start | bytes 147464 | tf_op jit(solution)/shard_map/ppermute | solution.py:149
  80.2 0.7 collective-permute-start.17
  80.9 1.8 %columns.1 = (f32[6,32,256]{2,1,0:T(8,128)}, f32[6,32,256]{2,1,0:T(8,128)}) custom-call(s32[18]{0:T(128)S(1)} %copy-done.5, s32[12]{0:T(128)S(1)} %copy-done.6, f32[6,32,256]{2,1,0:T(8,128)S(1)} %get-tuple-element.34.mine1.kept1, bf16[6,32,256]{2,1,0:T(8,128)(2,1)S(1)} %bitcast.98, f32[6,32,256]{2,1,0:T(8,128)S(1)} %get-tuple-element.36.mine2.kept2, ...), custom_call_target="tpu_custom_call" | custom-call | tf_op jit(solution)/shard_map/columns/pallas_call | solution.py:259
  82.6 0.5 collective-permute-done.16
  83.1 0.7 collective-permute-done.17
  83.9 0.6 slice_bitcast_fusion
  (35 shorter events, 0.6 us)
Async XLA Ops:
  2.4 31.4 %copy-start = (bf16[6,1,3,1,256,256]{5,4,3,2,1,0:T(8,128)(2,1)S(1)}, bf16[6,1,3,1,256,256]{5,4,3,2,1,0:T(8,128)(2,1)}, u32[]{:S(2)}) copy-start(bf16[6,1,3,1,256,256]{5,4,3,2,1,0:T(8,128)(2,1)} %param.8) | copy-start | bytes 7077892
  2.4 31.4 %copy-start.1 = (f32[256,256]{1,0:T(8,128)S(1)}, f32[256,256]{1,0:T(8,128)}, u32[]{:S(2)}) copy-start(f32[256,256]{1,0:T(8,128)} %inv1.3) | copy-start | bytes 786436
  2.4 31.4 %copy-start.2 = (f32[256,256]{1,0:T(8,128)S(1)}, f32[256,256]{1,0:T(8,128)}, u32[]{:S(2)}) copy-start(f32[256,256]{1,0:T(8,128)} %inv2.3) | copy-start | bytes 786436
  2.4 31.4 %copy-start.5 = (s32[18]{0:T(128)S(1)}, s32[18]{0:T(128)}, u32[]{:S(2)}) copy-start(s32[18]{0:T(128)} %struct1.5) | copy-start | bytes 220
  2.4 31.4 %copy-start.6 = (s32[12]{0:T(128)S(1)}, s32[12]{0:T(128)}, u32[]{:S(2)}) copy-start(s32[12]{0:T(128)} %struct2.5) | copy-start | bytes 148
  2.4 7.6 %collective-permute-start = (bf16[2,3,32,256]{3,2,1,0:T(8,128)(2,1)S(1)}, bf16[2,3,32,256]{3,2,1,0:T(8,128)(2,1)S(1)}, u32[]{:S(2)}, u32[]{:S(2)}) collective-permute-start(bf16[2,3,32,256]{3,2,1,0:T(8,128)(2,1)S(1)} %pad_maximum_fusion.2), channel_id=1, source_target_pairs={{0,0},{1,4},{2,8},{3,12},{4,16},{5,20},{6,24},{7,28},{8,1},{9,5},{... | collective-permute-start | bytes 294920 | tf_op jit(solution)/shard_map/ppermute | solution.py:183
  3.3 10.6 %collective-permute-start.1 = (bf16[2,3,32,256]{3,2,1,0:T(8,128)(2,1)S(1)}, bf16[2,3,32,256]{3,2,1,0:T(8,128)(2,1)S(1)}, u32[]{:S(2)}, u32[]{:S(2)}) collective-permute-start(bf16[2,3,32,256]{3,2,1,0:T(8,128)(2,1)S(1)} %pad_maximum_fusion.3), channel_id=1, source_target_pairs={{0,4},{1,0},{2,12},{3,8},{4,20},{5,16},{6,28},{7,24},{8,5},{9,1},{... | collective-permute-start | bytes 294920 | tf_op jit(solution)/shard_map/ppermute | solution.py:183
  13.9 8.5 %collective-permute-start.2 = (bf16[1,2,2,3,32,256]{5,4,3,2,1,0:T(8,128)(2,1)S(1)}, bf16[1,2,2,3,32,256]{5,4,3,2,1,0:T(8,128)(2,1)S(1)}, u32[]{:S(2)}, u32[]{:S(2)}) collective-permute-start(bf16[1,2,2,3,32,256]{5,4,3,2,1,0:T(8,128)(2,1)S(1)} %maximum_bitcast_fusion), channel_id=1, source_target_pairs={{0,16},{8,24},{16,0},{24,8},{1,17},{9,25},{17,1},{25,9},{2,18},{10... | collective-permute-start | bytes 589832 | tf_op jit(solution)/shard_map/ppermute | solution.py:149
  17.2 8.3 %collective-permute-start.3 = (bf16[6,32,256]{2,1,0:T(8,128)(2,1)}, bf16[6,32,256]{2,1,0:T(8,128)(2,1)S(1)}, u32[]{:S(2)}, u32[]{:S(2)}) collective-permute-start(bf16[6,32,256]{2,1,0:T(8,128)(2,1)} %bitcast.95), channel_id=1, source_target_pairs={{0,4},{1,5},{2,6},{3,7},{4,0},{5,1},{6,2},{7,3},{8,12},{9,13},{10,... | collective-permute-start | bytes 294920 | tf_op jit(solution)/shard_map/ppermute | solution.py:149
  25.6 1.7 %collective-permute-start.4 = (bf16[2,2,2,3,32,256]{5,4,3,2,1,0:T(8,128)(2,1)S(1)}, bf16[2,2,2,3,32,256]{5,4,3,2,1,0:T(8,128)(2,1)S(1)}, u32[]{:S(2)}, u32[]{:S(2)}) collective-permute-start(bf16[2,2,2,3,32,256]{5,4,3,2,1,0:T(8,128)(2,1)S(1)} %pad_maximum_fusion.1), channel_id=1, source_target_pairs={{0,8},{8,0},{16,24},{24,16},{1,9},{9,1},{17,25},{25,17},{2,10},{10... | collective-permute-start | bytes 1179656 | tf_op jit(solution)/shard_map/ppermute | solution.py:149
  25.7 8.1 %collective-permute-start.5 = (bf16[6,32,256]{2,1,0:T(8,128)(2,1)}, bf16[6,32,256]{2,1,0:T(8,128)(2,1)S(1)}, u32[]{:S(2)}, u32[]{:S(2)}) collective-permute-start(bf16[6,32,256]{2,1,0:T(8,128)(2,1)} %bitcast.92), channel_id=1, source_target_pairs={{0,4},{1,5},{2,6},{3,7},{4,0},{5,1},{6,2},{7,3},{8,12},{9,13},{10,... | collective-permute-start | bytes 294920 | tf_op jit(solution)/shard_map/ppermute | solution.py:149
  27.3 13.0 %copy-start.3 = (bf16[6,1,32,256]{3,2,1,0:T(8,128)(2,1)S(1)}, bf16[6,1,32,256]{3,2,1,0:T(8,128)(2,1)}, u32[]{:S(2)}) copy-start(bf16[6,1,32,256]{3,2,1,0:T(8,128)(2,1)} %param.10) | copy-start | bytes 294916
  27.3 12.9 %copy-start.4 = (bf16[6,1,32,256]{3,2,1,0:T(8,128)(2,1)S(1)}, bf16[6,1,32,256]{3,2,1,0:T(8,128)(2,1)}, u32[]{:S(2)}) copy-start(bf16[6,1,32,256]{3,2,1,0:T(8,128)(2,1)} %param.9) | copy-start | bytes 294916
  27.4 12.9 %copy-start.7 = (bf16[256,256]{1,0:T(8,128)(2,1)S(1)}, bf16[256,256]{1,0:T(8,128)(2,1)}, u32[]{:S(2)}) copy-start(bf16[256,256]{1,0:T(8,128)(2,1)} %link.1) | copy-start | bytes 393220
  39.3 11.2 %collective-permute-start.8 = (bf16[4,6,32,256]{3,2,1,0:T(8,128)(2,1)S(1)}, bf16[4,6,32,256]{3,2,1,0:T(8,128)(2,1)}, u32[]{:S(2)}, u32[]{:S(2)}) collective-permute-start(bf16[4,6,32,256]{3,2,1,0:T(8,128)(2,1)S(1)} %get-tuple-element.31), channel_id=1, source_target_pairs={{0,2},{1,3},{2,0},{3,1},{4,6},{5,7},{6,4},{7,5},{8,10},{9,11},{10,... | collective-permute-start | bytes 1179656 | tf_op jit(solution)/shard_map/ppermute | solution.py:149
  39.4 13.2 %collective-permute-start.6 = (bf16[4,6,32,256]{3,2,1,0:T(8,128)(2,1)S(1)}, bf16[4,6,32,256]{3,2,1,0:T(8,128)(2,1)S(1)}, u32[]{:S(2)}, u32[]{:S(2)}) collective-permute-start(bf16[4,6,32,256]{3,2,1,0:T(8,128)(2,1)S(1)} %get-tuple-element.29), channel_id=1, source_target_pairs={{0,1},{1,0},{2,3},{3,2},{4,5},{5,4},{6,7},{7,6},{8,9},{9,8},{10,11... | collective-permute-start | bytes 1179656 | tf_op jit(solution)/shard_map/ppermute | solution.py:149
  51.7 6.1 %collective-permute-start.9 = (bf16[2,6,32,256]{3,2,1,0:T(8,128)(2,1)S(1)}, bf16[2,6,32,256]{3,2,1,0:T(8,128)(2,1)S(1)}, u32[]{:S(2)}, u32[]{:S(2)}) collective-permute-start(bf16[2,6,32,256]{3,2,1,0:T(8,128)(2,1)S(1)} %fusion.1), channel_id=1, source_target_pairs={{0,1},{1,0},{2,3},{3,2},{4,5},{5,4},{6,7},{7,6},{8,9},{9,8},{10,11... | collective-permute-start | bytes 589832 | tf_op jit(solution)/shard_map/ppermute | solution.py:149
  52.8 5.8 %collective-permute-start.7 = (bf16[2,6,32,256]{3,2,1,0:T(8,128)(2,1)S(1)}, bf16[2,6,32,256]{3,2,1,0:T(8,128)(2,1)S(1)}, u32[]{:S(2)}, u32[]{:S(2)}) collective-permute-start(bf16[2,6,32,256]{3,2,1,0:T(8,128)(2,1)S(1)} %fusion), channel_id=1, source_target_pairs={{0,2},{1,3},{2,0},{3,1},{4,6},{5,7},{6,4},{7,5},{8,10},{9,11},{10,... | collective-permute-start | bytes 589832 | tf_op jit(solution)/shard_map/ppermute | solution.py:149
  59.7 5.7 %collective-permute-start.10 = (bf16[3,4,32,256]{3,2,1,0:T(8,128)(2,1)S(1)}, bf16[3,4,32,256]{3,2,1,0:T(8,128)(2,1)S(1)}, u32[]{:S(2)}, u32[]{:S(2)}) collective-permute-start(bf16[3,4,32,256]{3,2,1,0:T(8,128)(2,1)S(1)} %fusion.2), channel_id=1, source_target_pairs={{0,1},{1,0},{2,3},{3,2},{4,5},{5,4},{6,7},{7,6},{8,9},{9,8},{10,11... | collective-permute-start | bytes 589832 | tf_op jit(solution)/shard_map/ppermute | solution.py:149
  61.0 9.8 %collective-permute-start.13 = (bf16[1,6,32,256]{3,2,1,0:T(8,128)(2,1)S(1)}, bf16[1,6,32,256]{3,2,1,0:T(8,128)(2,1)S(1)}, u32[]{:S(2)}, u32[]{:S(2)}) collective-permute-start(bf16[1,6,32,256]{3,2,1,0:T(8,128)(2,1)S(1)} %dynamic-slice_convert_fusion), channel_id=1, source_target_pairs={{0,4},{1,5},{2,6},{3,7},{4,0},{5,1},{6,2},{7,3},{8,12},{9,13},{10,... | collective-permute-start | bytes 294920 | tf_op jit(solution)/shard_map/ppermute | solution.py:149
  65.6 5.2 %collective-permute-start.11 = (bf16[3,2,32,256]{3,2,0,1:T(8,128)(2,1)S(1)}, bf16[3,2,32,256]{3,2,0,1:T(8,128)(2,1)S(1)}, u32[]{:S(2)}, u32[]{:S(2)}) collective-permute-start(bf16[3,2,32,256]{3,2,0,1:T(8,128)(2,1)S(1)} %fusion.3), channel_id=1, source_target_pairs={{0,2},{1,3},{2,0},{3,1},{4,6},{5,7},{6,4},{7,5},{8,10},{9,11},{10,... | collective-permute-start | bytes 294920 | tf_op jit(solution)/shard_map/ppermute | solution.py:149
  66.2 7.2 %collective-permute-start.12 = (bf16[1,6,32,256]{3,2,1,0:T(8,128)(2,1)S(1)}, bf16[1,6,32,256]{3,2,1,0:T(8,128)(2,1)S(1)}, u32[]{:S(2)}, u32[]{:S(2)}) collective-permute-start(bf16[1,6,32,256]{3,2,1,0:T(8,128)(2,1)S(1)} %dynamic-slice_convert_fusion.1), channel_id=1, source_target_pairs={{0,4},{1,5},{2,6},{3,7},{4,0},{5,1},{6,2},{7,3},{8,12},{9,13},{10,... | collective-permute-start | bytes 294920 | tf_op jit(solution)/shard_map/ppermute | solution.py:149
  73.4 5.5 %collective-permute-start.14 = (bf16[3,1,32,256]{3,2,0,1:T(8,128)(2,1)S(1)}, bf16[3,1,32,256]{3,2,0,1:T(8,128)(2,1)S(1)}, u32[]{:S(2)}, u32[]{:S(2)}) collective-permute-start(bf16[3,1,32,256]{3,2,0,1:T(8,128)(2,1)S(1)} %dynamic-slice_convert_fusion.2), channel_id=1, source_target_pairs={{0,4},{1,5},{2,6},{3,7},{4,0},{5,1},{6,2},{7,3},{8,12},{9,13},{10,... | collective-permute-start | bytes 147464 | tf_op jit(solution)/shard_map/ppermute | solution.py:149
  78.9 3.7 %collective-permute-start.15 = (bf16[3,32,256]{2,1,0:T(8,128)(2,1)S(1)}, bf16[3,32,256]{2,1,0:T(8,128)(2,1)S(1)}, u32[]{:S(2)}, u32[]{:S(2)}) collective-permute-start(bf16[3,32,256]{2,1,0:T(8,128)(2,1)S(1)} %bitcast_convert_fusion.3), channel_id=1, source_target_pairs={{0,8},{8,0},{16,24},{24,16},{1,9},{9,1},{17,25},{25,17},{2,10},{10... | collective-permute-start | bytes 147464 | tf_op jit(solution)/shard_map/ppermute | solution.py:149
  79.0 4.2 %collective-permute-start.16 = (bf16[3,32,256]{2,1,0:T(8,128)(2,1)S(1)}, bf16[3,32,256]{2,1,0:T(8,128)(2,1)S(1)}, u32[]{:S(2)}, u32[]{:S(2)}) collective-permute-start(bf16[3,32,256]{2,1,0:T(8,128)(2,1)S(1)} %bitcast_convert_fusion.3), channel_id=1, source_target_pairs={{0,16},{8,24},{16,0},{24,8},{1,17},{9,25},{17,1},{25,9},{2,18},{10... | collective-permute-start | bytes 147464 | tf_op jit(solution)/shard_map/ppermute | solution.py:149
  80.2 3.7 %collective-permute-start.17 = (bf16[3,32,256]{2,1,0:T(8,128)(2,1)S(1)}, bf16[3,32,256]{2,1,0:T(8,128)(2,1)S(1)}, u32[]{:S(2)}, u32[]{:S(2)}) collective-permute-start(bf16[3,32,256]{2,1,0:T(8,128)(2,1)S(1)} %bitcast_convert_fusion.3), channel_id=1, source_target_pairs={{0,24},{8,16},{16,8},{24,0},{1,25},{9,17},{17,9},{25,1},{2,26},{10... | collective-permute-start | bytes 147464 | tf_op jit(solution)/shard_map/ppermute | solution.py:149

commit v2 on v1

--- a/solution.py
+++ b/solution.py
@@ -46,56 +46,65 @@
     return found == 1
 
 
+def slice_of(row, turn, n_row):
+    half = n_row // 2
+    return 2 * (turn * half + lax.rem(row, half)) + row // half
+
+
+def place_of(piece, n_row):
+    half = n_row // 2
+    return (piece % 2) * half + piece // 2 % half, piece // 2 // half
+
+
 def product_kernel(n_row, n_col, first_bits, struct1, struct2, inv1, inv2, stored, pieces, *rest):
     cycle = n_col // n_row
     keeps, sends = rest[:2], rest[2:4]
-    held, loose, factor, sems = rest[4:]
-    row_blocks = held.shape[0]
+    loose, factor = rest[4:]
+    row_blocks = stored.shape[0]
     _, col_blocks, _, slab, width = loose.shape
     here_row, here_col = lax.axis_index("row"), lax.axis_index("col")
-    copies = [pltpu.make_async_copy(stored.at[a], held.at[a], sems.at[a]) for a in range(row_blocks)]
-    for copy in copies:
-        copy.start()
 
     group = here_col // n_row
     for m in range(n_row):
+        row = here_row ^ m
         for s in range(cycle):
-            slot = (here_row ^ m) * cycle + lax.rem(s - group + cycle, cycle)
+            slot = slice_of(row, lax.rem(s - group + cycle, cycle), n_row)
             for p in range(2):
                 for b in range(col_blocks):
-                    loose[p, b, slot] = pieces[m, s, p, b].astype(jnp.float32)
+                    loose[p, b, slot] = pieces[m, s, p, b].astype(loose.dtype)
     for p, (struct, inverse) in enumerate(((struct1, inv1), (struct2, inv2))):
 
         def look(place, found):
             return tuple(f | (struct[place] == b * n_col + here_col).astype(jnp.int32) for b, f in enumerate(found))
 
         found = lax.fori_loop(0, struct.shape[0], look, (jnp.int32(0),) * col_blocks)
-        blocks = loose[p].reshape(col_blocks * n_col * slab, width).astype(jnp.bfloat16)
+        blocks = loose[p].reshape(col_blocks * width, width).astype(jnp.bfloat16)
         product = split_dot(blocks, inverse[...])
         for b in range(col_blocks):
-            block = product[b * width : (b + 1) * width]
-            factor[b, :, p * width : (p + 1) * width] = jnp.where(found[b] == 1, block, 0.0).astype(jnp.bfloat16)
-
-    for a in range(row_blocks):
-        copies[a].wait()
-        total = jnp.dot(held[a, 0], factor[0], preferred_element_type=jnp.float32)
-        for b in range(1, col_blocks):
-            total += jnp.dot(held[a, b], factor[b], preferred_element_type=jnp.float32)
-        for p in range(2):
-            bit = first_bits[p]
-            upper = ((here_col >> bit) & 1) == 1
-            for j in range(n_col // 2):
-                low = ((j >> bit) << (bit + 1)) | (j & ((1 << bit) - 1))
-                high = low | (1 << bit)
-                x = total[low * slab : (low + 1) * slab, p * width : (p + 1) * width]
-                y = total[high * slab : (high + 1) * slab, p * width : (p + 1) * width]
-                keeps[p][j, a] = jnp.where(upper, y, x)
-                sends[p][j, a] = jnp.where(upper, x, y).astype(jnp.bfloat16)
-
-
-def prepare_kernel(n_row, struct1, struct2, mine1, mine2, other1, other2, link, inv1, inv2, after, rows, linked, out, whole):
+            place = slice(b * width, (b + 1) * width)
+            factor[place, p * width : (p + 1) * width] = jnp.where(found[b] == 1, product[place], 0.0).astype(jnp.bfloat16)
+
+    step = 2 if row_blocks % 2 == 0 else 1
+    for a in range(0, row_blocks, step):
+        wide = [jnp.concatenate([stored[a + i, b] for b in range(col_blocks)], axis=1) for i in range(step)]
+        totals = jnp.dot(jnp.concatenate(wide, axis=0), factor[...], preferred_element_type=jnp.float32)
+        for i in range(step):
+            total = totals[i * width : (i + 1) * width]
+            for p in range(2):
+                bit = first_bits[p]
+                upper = ((here_col >> bit) & 1) == 1
+                for j in range(n_col // 2):
+                    low = ((j >> bit) << (bit + 1)) | (j & ((1 << bit) - 1))
+                    high = low | (1 << bit)
+                    x = total[low * slab : (low + 1) * slab, p * width : (p + 1) * width]
+                    y = total[high * slab : (high + 1) * slab, p * width : (p + 1) * width]
+                    keeps[p][j, a + i] = jnp.where(upper, y, x)
+                    sends[p][j, a + i] = jnp.where(upper, x, y).astype(jnp.bfloat16)
+
+
+def prepare_kernel(n_row, struct1, struct2, mine1, mine2, other, link, inv1, inv2, after, rows, linked, out, whole):
     blocks, slab, width = mine1.shape
-    for p, (struct, inverse, parts) in enumerate(((struct1, inv1, (mine1, other1)), (struct2, inv2, (mine2, other2)))):
+    for p, (struct, inverse, parts) in enumerate(((struct1, inv1, (mine1, other.at[0])), (struct2, inv2, (mine2, other.at[1])))):
         keep = listed(struct, blocks, n_row)
         for i, part in enumerate(parts):
             flat = part[...].astype(jnp.float32).reshape(blocks * slab, width).astype(jnp.bfloat16)
@@ -164,64 +173,60 @@
     n_bits = n_col.bit_length() - 1
     f32, bf16 = jnp.float32, jnp.bfloat16
     shape = jax.ShapeDtypeStruct
-    big = pltpu.CompilerParams(vmem_limit_bytes=24 * 1024 * 1024)
+    big = pltpu.CompilerParams(vmem_limit_bytes=12 * 1024 * 1024)
     stored = stored_inverse.reshape(row_blocks, col_blocks, width, width)
     panel = (row_blocks, slab, width)
 
     panels = [panel_first.reshape(panel), panel_second.reshape(panel)]
 
-    turns = [p.reshape(col_blocks, cycle, slab, width) for p in panels]
+    turns = jnp.stack(panels).reshape(2, col_blocks, cycle, slab, width)
+    _, turn = place_of(here_col, n_row)
     got = []
     for s in range(cycle):
         moves = []
         for r in range(n_row):
             for c in range(n_col):
-                j = (s - c) % cycle
-                moves.append((r * n_col + c, (c // cycle) * n_col + r + j * n_row))
-        pick = (s - here_col) % cycle
-        part = jnp.stack([lax.dynamic_index_in_dim(t, pick, 1, keepdims=False) for t in turns])
+                row, t = place_of(c, n_row)
+                moves.append((r * n_col + c, row * n_col + r + (s - t) % cycle * n_row))
+        part = lax.dynamic_index_in_dim(turns, (s - turn) % cycle, 2, keepdims=False)
         got.append(lax.ppermute(part, ("row", "col"), moves))
     pieces = jnp.stack(got)[None]
-    others = [swapped(p, "col", n_col, n_col // 2) for p in panels]
 
     order = [0]
     bit = n_row // 2
     while bit:
-        if bit == 1:
-            pieces, others[0] = lax.optimization_barrier((pieces, others[0]))
         pieces = jnp.concatenate([pieces, swapped(pieces, "row", n_row, bit)])
         order += [o ^ bit for o in order]
         bit //= 2
     pieces = jnp.stack([pieces[order.index(m)] for m in range(n_row)])
-    pieces, others[1] = lax.optimization_barrier((pieces, others[1]))
 
     orders = (list(range(n_bits)), [1, 0] + list(range(2, n_bits)))
     half = (n_col // 2,) + panel
     split = pl.pallas_call(
         functools.partial(product_kernel, n_row, n_col, (orders[0][0], orders[1][0])),
         out_shape=[shape(half, f32)] * 2 + [shape(half, bf16)] * 2,
-        in_specs=[SMEM, SMEM, VMEM, VMEM, HBM, VMEM],
+        in_specs=[SMEM, SMEM] + [VMEM] * 4,
         out_specs=[VMEM] * 4,
         scratch_shapes=[
-            pltpu.VMEM(stored.shape, bf16),
-            pltpu.VMEM((2, col_blocks, n_col, slab, width), f32),
-            pltpu.VMEM((col_blocks, width, 2 * width), bf16),
-            pltpu.SemaphoreType.DMA((row_blocks,)),
+            pltpu.VMEM((2, col_blocks, n_col, slab, width), bf16 if slab % 16 == 0 else f32),
+            pltpu.VMEM((col_blocks * width, 2 * width), bf16),
         ],
         compiler_params=big,
         name="products",
     )(struct_first, struct_second, inv_first, inv_second, stored, pieces)
 
+    panels, pieces = lax.optimization_barrier((panels, pieces))
+    other = swapped(jnp.stack(panels), "col", n_col, n_col // 2)
     rows, linked, consts = pl.pallas_call(
         functools.partial(prepare_kernel, n_row),
         out_shape=[shape((2, 2) + panel, bf16), shape((width, width), f32), shape((3, slab, width), f32)],
-        in_specs=[SMEM, SMEM] + [VMEM] * 7 + [ANY],
+        in_specs=[SMEM, SMEM] + [VMEM] * 6 + [ANY],
         out_specs=[VMEM] * 3,
         scratch_shapes=[pltpu.VMEM((3, width, width), f32)],
         compiler_params=big,
         name="prepare",
         cost_estimate=pl.CostEstimate(flops=6 * 10 * width**3, bytes_accessed=8 * width**2, transcendentals=0),
-    )(struct_first, struct_second, *panels, *others, panel_link, inv_first, inv_second, split[0])
+    )(struct_first, struct_second, *panels, other, panel_link, inv_first, inv_second, split[0])
 
     last = []
     for p in range(2):
@@ -252,10 +257,12 @@
         done += [keep, swapped(send, "col", n_col, n_col // 2).reshape(panel)]
     for bit in range(n_bits):
         if bit == n_bits - 1:
-            sums, done = lax.optimization_barrier((sums, done))
+            sums, done[1] = lax.optimization_barrier((sums, done[1]))
         keep, send = halves(sums.reshape(3, -1, 2, slab, width), 2, (here_col >> bit) & 1)
         sums = keep + swapped(send, "col", n_col, 1 << bit).astype(f32)
 
+    total = sums.reshape(3, slab, width)
+    total, done[3] = lax.optimization_barrier((total, done[3]))
     column_first, column_second = pl.pallas_call(
         functools.partial(column_kernel, n_row),
         out_shape=[shape(panel, f32)] * 2,
@@ -265,7 +272,6 @@
         name="columns",
     )(struct_first, struct_second, *done, linked)
 
-    total = sums.reshape(3, slab, width)
     send = total.astype(bf16)
     for m in range(1, n_row):
         total = total + swapped(send, "row", n_row, m).astype(f32)

time: 84.8 us -> 85.8 us (1.012)
  the two profiles are of different devices: /device:TPU:0 before, /device:TPU:13 now
where the time goes in v2:
time: 85.8 us; the launch traced here: 85.5 us
  waiting for transfers between devices  35 us (41%)
  starting transfers between devices  32.2 us (38%)
  Pallas kernels  10 us (12%)
  local copies, waits for them, and re-layouts  5.6 us (7%)
  other arithmetic  1.66 us (2%)
  between operations  1.01 us (1%)
    ppermute x15, waiting for transfers between devices, swapped(): return lax.ppermute(value, axis, [(i, i ^ mask) for i in range(size)])  30.6 us
    ppermute x15, starting transfers between devices, swapped(): return lax.ppermute(value, axis, [(i, i ^ mask) for i in range(size)])  25.9 us
    ppermute x2, starting transfers between devices, body(): got.append(lax.ppermute(part, ('row', 'col'), moves))  6.27 us
    unnamed x28, local copies, waits for them, and re-layouts  4.71 us
    ppermute x2, waiting for transfers between devices, body(): got.append(lax.ppermute(part, ('row', 'col'), moves))  4.39 us
    pallas_call x1, Pallas kernels, body(): pl.pallas_call(functools.partial(product_kernel, n_row, n_col, (orders[0]...  3.87 us
    pallas_call x1, Pallas kernels, body(): pl.pallas_call(functools.partial(prepare_kernel, n_row), out_shape=[shape...  3.34 us
    pallas_call x1, Pallas kernels, body(): pl.pallas_call(functools.partial(column_kernel, n_row), out_shape=[shape(...  1.78 us
  transfers between devices with their start and end apart: 17, of which 11 were waited for; matrix products, arithmetic and copies ran while one was open for 1% of the time, Pallas kernels for 6%

profile of v2, /device:TPU:13, one launch (start us, length us, event | category | flops | bytes accessed | tf_op | source)
XLA Modules:
  0.0 85.5 jit_solution(15599386949846453437)
XLA Ops:
  0.7 0.0 copy-start.6
  0.7 0.0 copy-start.8
  0.8 1.1 %fusion.7 = (bf16[2,3,32,256]{3,2,1,0:T(8,128)(2,1)S(1)}, bf16[2,3,32,256]{3,2,1,0:T(8,128)(2,1)S(1)}) fusion(s32[]{:T(128)S(6)} %select_n.61, bf16[1,3,2,32,256]{4,3,2,1,0:T(8,128)(2,1)} %bitcast.78, bf16[1,3,2,32,256]{4,3,2,1,0:T(8,128)(2,1)} %bitcast.81, s32[]{:T(128)S(6)} %select_n.63), kind=kLoop, calls=%fused_computation.31 | loop fusion | flops 98304 | bytes 393224 | tf_op jit(solution)/shard_map/jit(dynamic_index_in_dim)/squeeze | solution.py:191
  1.8 3.1 %collective-permute-start = (bf16[2,3,32,256]{3,2,1,0:T(8,128)(2,1)S(1)}, bf16[2,3,32,256]{3,2,1,0:T(8,128)(2,1)S(1)}, u32[]{:S(2)}, u32[]{:S(2)}) collective-permute-start(bf16[2,3,32,256]{3,2,1,0:T(8,128)(2,1)S(1)} %get-tuple-element.51), channel_id=1, source_target_pairs={{0,0},{1,16},{2,8},{3,24},{4,4},{5,20},{6,12},{7,28},{8,1},{9,17},... | collective-permute-start | bytes 294920 | tf_op jit(solution)/shard_map/ppermute | solution.py:192
  4.9 3.2 %collective-permute-start.1 = (bf16[2,3,32,256]{3,2,1,0:T(8,128)(2,1)S(1)}, bf16[2,3,32,256]{3,2,1,0:T(8,128)(2,1)S(1)}, u32[]{:S(2)}, u32[]{:S(2)}) collective-permute-start(bf16[2,3,32,256]{3,2,1,0:T(8,128)(2,1)S(1)} %get-tuple-element.52), channel_id=1, source_target_pairs={{0,4},{1,20},{2,12},{3,28},{4,0},{5,16},{6,8},{7,24},{8,5},{9,21},... | collective-permute-start | bytes 294920 | tf_op jit(solution)/shard_map/ppermute | solution.py:192
  8.1 0.0 collective-permute-done
  8.1 4.4 %collective-permute-done.1 = bf16[2,3,32,256]{3,2,1,0:T(8,128)(2,1)S(1)} collective-permute-done((bf16[2,3,32,256]{3,2,1,0:T(8,128)(2,1)S(1)}, bf16[2,3,32,256]{3,2,1,0:T(8,128)(2,1)S(1)}, u32[]{:S(2)}, u32[]{:S(2)}) %collective-permute-start.1) | collective-permute-done | bytes 98336 | tf_op jit(solution)/shard_map/ppermute | solution.py:192
  12.5 0.1 collective-permute-start.2
  12.6 6.2 %collective-permute-done.2 = bf16[1,2,2,3,32,256]{5,4,3,2,1,0:T(8,128)(2,1)S(1)} collective-permute-done((bf16[1,2,2,3,32,256]{5,4,3,2,1,0:T(8,128)(2,1)S(1)}, bf16[1,2,2,3,32,256]{5,4,3,2,1,0:T(8,128)(2,1)S(1)}, u32[]{:S(2)}, u32[]{:S(2)}) %collective-permute-start.2) | collective-permute-done | bytes 196640 | tf_op jit(solution)/shard_map/ppermute | solution.py:158
  18.8 1.2 %collective-permute-start.3 = (bf16[2,2,2,3,32,256]{5,4,3,2,1,0:T(8,128)(2,1)S(1)}, bf16[2,2,2,3,32,256]{5,4,3,2,1,0:T(8,128)(2,1)S(1)}, u32[]{:S(2)}, u32[]{:S(2)}) collective-permute-start(bf16[2,2,2,3,32,256]{5,4,3,2,1,0:T(8,128)(2,1)S(1)} %pad_maximum_fusion.1), channel_id=1, source_target_pairs={{0,8},{8,0},{16,24},{24,16},{1,9},{9,1},{17,25},{25,17},{2,10},{10... | collective-permute-start | bytes 1179656 | tf_op jit(solution)/shard_map/ppermute | solution.py:158
  20.0 1.3 %collective-permute-done.3 = bf16[2,2,2,3,32,256]{5,4,3,2,1,0:T(8,128)(2,1)S(1)} collective-permute-done((bf16[2,2,2,3,32,256]{5,4,3,2,1,0:T(8,128)(2,1)S(1)}, bf16[2,2,2,3,32,256]{5,4,3,2,1,0:T(8,128)(2,1)S(1)}, u32[]{:S(2)}, u32[]{:S(2)}) %collective-permute-start.3) | collective-permute-done | bytes 393248 | tf_op jit(solution)/shard_map/ppermute | solution.py:158
  21.4 0.0 copy-start.4
  21.4 0.0 copy-start.5
  21.4 0.1 pad_maximum_fusion.pieces
  21.5 0.0 copy-start.13
  21.6 3.9 %products.1 = (f32[4,6,32,256]{3,2,1,0:T(8,128)S(1)}, f32[4,6,32,256]{3,2,1,0:T(8,128)S(1)}, bf16[4,6,32,256]{3,2,1,0:T(8,128)(2,1)}, bf16[4,6,32,256]{3,2,1,0:T(8,128)(2,1)S(1)}) custom-call(s32[18]{0:T(128)S(1)} %copy-done.10, s32[12]{0:T(128)S(1)} %copy-done.11, f32[256,256]{1,0:T(8,128)S(1)} %copy-done.6, f32[256,256]{1,0:T(8,128)S(1)} %copy-done.8, ...), custom_call_target="tpu_custom_call" | custom-call | tf_op jit(solution)/shard_map/products/pallas_call | solution.py:205
  25.4 0.9 %copy-done.1 = f32[4,6,32,256]{3,2,1,0:T(8,128)} copy-done((f32[4,6,32,256]{3,2,1,0:T(8,128)}, f32[4,6,32,256]{3,2,1,0:T(8,128)S(1)}, u32[]{:S(2)}) %copy-start.1) | copy-done | bytes 786456
  26.3 0.7 copy-done.12
  27.1 3.8 %collective-permute-start.6 = (bf16[2,6,32,256]{3,2,1,0:T(8,128)(2,1)S(1)}, bf16[2,6,32,256]{3,2,1,0:T(8,128)(2,1)S(1)}, u32[]{:S(2)}, u32[]{:S(2)}) collective-permute-start(bf16[2,6,32,256]{3,2,1,0:T(8,128)(2,1)S(1)} %pad_maximum_fusion.2), channel_id=1, source_target_pairs={{0,4},{1,5},{2,6},{3,7},{4,0},{5,1},{6,2},{7,3},{8,12},{9,13},{10,... | collective-permute-start | bytes 589832 | tf_op jit(solution)/shard_map/ppermute | solution.py:158
  30.9 0.4 collective-permute-start.7
  31.4 8.3 %collective-permute-done.6.other = bf16[2,6,32,256]{3,2,1,0:T(8,128)(2,1)S(1)} collective-permute-done((bf16[2,6,32,256]{3,2,1,0:T(8,128)(2,1)S(1)}, bf16[2,6,32,256]{3,2,1,0:T(8,128)(2,1)S(1)}, u32[]{:S(2)}, u32[]{:S(2)}) %collective-permute-start.6) | collective-permute-done | bytes 196640 | tf_op jit(solution)/shard_map/ppermute | solution.py:158
  39.7 1.1 %copy-done.2 = f32[4,6,32,256]{3,2,1,0:T(8,128)S(1)} copy-done((f32[4,6,32,256]{3,2,1,0:T(8,128)S(1)}, f32[4,6,32,256]{3,2,1,0:T(8,128)}, u32[]{:S(2)}) %copy-start.2) | copy-done | bytes 786456
  40.8 0.9 %copy-done.7 = f32[256,256]{1,0:T(8,128)S(1)} copy-done((f32[256,256]{1,0:T(8,128)S(1)}, f32[256,256]{1,0:T(8,128)}, u32[]{:S(2)}) %copy-start.7) | copy-done | bytes 262168
  41.7 0.9 %copy-done.9 = f32[256,256]{1,0:T(8,128)S(1)} copy-done((f32[256,256]{1,0:T(8,128)S(1)}, f32[256,256]{1,0:T(8,128)}, u32[]{:S(2)}) %copy-start.9) | copy-done | bytes 262168
  42.7 3.3 %prepare.1 = (bf16[2,2,6,32,256]{4,3,2,1,0:T(8,128)(2,1)S(1)}, f32[256,256]{1,0:T(8,128)S(1)}, f32[3,32,256]{2,1,0:T(8,128)S(1)}) custom-call(s32[18]{0:T(128)S(1)} %copy-done.10, s32[12]{0:T(128)S(1)} %copy-done.11, bf16[6,32,256]{2,1,0:T(8,128)(2,1)S(1)} %bitcast.80, bf16[6,32,256]{2,1,0:T(8,128)(2,1)S(1)} %bitcast.83, ...), custom_call_target="tpu_custom_call" | custom-call | flops 1006632960 | bytes 524288 | tf_op jit(solution)/shard_map/prepare/pallas_call | solution.py:220
  46.0 0.0 collective-permute-done.4
  46.1 0.1 convert_add_fusion.1
  46.2 1.0 %collective-permute-start.5 = (bf16[2,6,32,256]{3,2,1,0:T(8,128)(2,1)S(1)}, bf16[2,6,32,256]{3,2,1,0:T(8,128)(2,1)S(1)}, u32[]{:S(2)}, u32[]{:S(2)}) collective-permute-start(bf16[2,6,32,256]{3,2,1,0:T(8,128)(2,1)S(1)} %fusion), channel_id=1, source_target_pairs={{0,2},{1,3},{2,0},{3,1},{4,6},{5,7},{6,4},{7,5},{8,10},{9,11},{10,... | collective-permute-start | bytes 589832 | tf_op jit(solution)/shard_map/ppermute | solution.py:158
  47.2 0.1 convert_add_fusion
  47.4 1.5 %collective-permute-start.8 = (bf16[2,6,32,256]{3,2,1,0:T(8,128)(2,1)S(1)}, bf16[2,6,32,256]{3,2,1,0:T(8,128)(2,1)S(1)}, u32[]{:S(2)}, u32[]{:S(2)}) collective-permute-start(bf16[2,6,32,256]{3,2,1,0:T(8,128)(2,1)S(1)} %fusion.1), channel_id=1, source_target_pairs={{0,1},{1,0},{2,3},{3,2},{4,5},{5,4},{6,7},{7,6},{8,9},{9,8},{10,11... | collective-permute-start | bytes 589832 | tf_op jit(solution)/shard_map/ppermute | solution.py:158
  48.9 3.2 %collective-permute-done.5 = bf16[2,6,32,256]{3,2,1,0:T(8,128)(2,1)S(1)} collective-permute-done((bf16[2,6,32,256]{3,2,1,0:T(8,128)(2,1)S(1)}, bf16[2,6,32,256]{3,2,1,0:T(8,128)(2,1)S(1)}, u32[]{:S(2)}, u32[]{:S(2)}) %collective-permute-start.5) | collective-permute-done | bytes 196640 | tf_op jit(solution)/shard_map/ppermute | solution.py:158
  52.2 0.2 collective-permute-done.8
  52.5 1.0 %sums.1 = f32[3,8,32,256]{3,2,1,0:T(8,128)S(1)} custom-call(bf16[2,2,6,32,256]{4,3,2,1,0:T(8,128)(2,1)S(1)} %get-tuple-element.24.rows, f32[6,32,256]{2,1,0:T(8,128)S(1)} %get-tuple-element.48.mine1.kept1, f32[6,32,256]{2,1,0:T(8,128)S(1)} %get-tuple-element.47.theirs1, f32[6,32,256]{2,1,0:T(8,128)S(1)} %get-tuple-element.46.mine2.kept2, ...), custom_call_target="tpu_custom_call" | custom-call | tf_op jit(solution)/shard_map/sums/pallas_call | solution.py:247
  53.6 2.1 %collective-permute-start.9 = (bf16[3,4,32,256]{3,2,1,0:T(8,128)(2,1)S(1)}, bf16[3,4,32,256]{3,2,1,0:T(8,128)(2,1)S(1)}, u32[]{:S(2)}, u32[]{:S(2)}) collective-permute-start(bf16[3,4,32,256]{3,2,1,0:T(8,128)(2,1)S(1)} %fusion.2), channel_id=1, source_target_pairs={{0,1},{1,0},{2,3},{3,2},{4,5},{5,4},{6,7},{7,6},{8,9},{9,8},{10,11... | collective-permute-start | bytes 589832 | tf_op jit(solution)/shard_map/ppermute | solution.py:158
  55.7 3.1 %collective-permute-done.9 = bf16[3,4,32,256]{3,2,1,0:T(8,128)(2,1)S(1)} collective-permute-done((bf16[3,4,32,256]{3,2,1,0:T(8,128)(2,1)S(1)}, bf16[3,4,32,256]{3,2,1,0:T(8,128)(2,1)S(1)}, u32[]{:S(2)}, u32[]{:S(2)}) %collective-permute-start.9) | collective-permute-done | bytes 196640 | tf_op jit(solution)/shard_map/ppermute | solution.py:158
  58.9 0.5 collective-permute-start.10
  59.4 3.1 %collective-permute-start.11 = (bf16[1,6,32,256]{3,2,1,0:T(8,128)(2,1)S(1)}, bf16[1,6,32,256]{3,2,1,0:T(8,128)(2,1)S(1)}, u32[]{:S(2)}, u32[]{:S(2)}) collective-permute-start(bf16[1,6,32,256]{3,2,1,0:T(8,128)(2,1)S(1)} %dynamic-slice_convert_fusion.1), channel_id=1, source_target_pairs={{0,4},{1,5},{2,6},{3,7},{4,0},{5,1},{6,2},{7,3},{8,12},{9,13},{10,... | collective-permute-start | bytes 294920 | tf_op jit(solution)/shard_map/ppermute | solution.py:158
  62.5 2.9 %collective-permute-done.11 = bf16[1,6,32,256]{3,2,1,0:T(8,128)(2,1)S(1)} collective-permute-done((bf16[1,6,32,256]{3,2,1,0:T(8,128)(2,1)S(1)}, bf16[1,6,32,256]{3,2,1,0:T(8,128)(2,1)S(1)}, u32[]{:S(2)}, u32[]{:S(2)}) %collective-permute-start.11) | collective-permute-done | bytes 98336 | tf_op jit(solution)/shard_map/ppermute | solution.py:158
  65.5 2.6 %collective-permute-start.12 = (bf16[3,1,32,256]{3,2,0,1:T(8,128)(2,1)S(1)}, bf16[3,1,32,256]{3,2,0,1:T(8,128)(2,1)S(1)}, u32[]{:S(2)}, u32[]{:S(2)}) collective-permute-start(bf16[3,1,32,256]{3,2,0,1:T(8,128)(2,1)S(1)} %dynamic-slice_convert_fusion.2), channel_id=1, source_target_pairs={{0,4},{1,5},{2,6},{3,7},{4,0},{5,1},{6,2},{7,3},{8,12},{9,13},{10,... | collective-permute-start | bytes 147464 | tf_op jit(solution)/shard_map/ppermute | solution.py:158
  68.1 0.1 collective-permute-start.13
  68.2 2.2 %collective-permute-done.12 = bf16[3,1,32,256]{3,2,0,1:T(8,128)(2,1)S(1)} collective-permute-done((bf16[3,1,32,256]{3,2,0,1:T(8,128)(2,1)S(1)}, bf16[3,1,32,256]{3,2,0,1:T(8,128)(2,1)S(1)}, u32[]{:S(2)}, u32[]{:S(2)}) %collective-permute-start.12) | collective-permute-done | bytes 49184 | tf_op jit(solution)/shard_map/ppermute | solution.py:158
  70.4 2.2 %collective-permute-done.13 = bf16[1,6,32,256]{3,2,1,0:T(8,128)(2,1)S(1)} collective-permute-done((bf16[1,6,32,256]{3,2,1,0:T(8,128)(2,1)S(1)}, bf16[1,6,32,256]{3,2,1,0:T(8,128)(2,1)S(1)}, u32[]{:S(2)}, u32[]{:S(2)}) %collective-permute-start.13) | collective-permute-done | bytes 98336 | tf_op jit(solution)/shard_map/ppermute | solution.py:158
  72.6 7.9 %collective-permute-start.16 = (bf16[3,32,256]{2,1,0:T(8,128)(2,1)S(1)}, bf16[3,32,256]{2,1,0:T(8,128)(2,1)S(1)}, u32[]{:S(2)}, u32[]{:S(2)}) collective-permute-start(bf16[3,32,256]{2,1,0:T(8,128)(2,1)S(1)} %convert_element_type.98), channel_id=1, source_target_pairs={{0,24},{8,16},{16,8},{24,0},{1,25},{9,17},{17,9},{25,1},{2,26},{10... | collective-permute-start | bytes 147464 | tf_op jit(solution)/shard_map/ppermute | solution.py:158
  80.5 1.6 %collective-permute-start.15 = (bf16[3,32,256]{2,1,0:T(8,128)(2,1)S(1)}, bf16[3,32,256]{2,1,0:T(8,128)(2,1)S(1)}, u32[]{:S(2)}, u32[]{:S(2)}) collective-permute-start(bf16[3,32,256]{2,1,0:T(8,128)(2,1)S(1)} %convert_element_type.98), channel_id=1, source_target_pairs={{0,16},{8,24},{16,0},{24,8},{1,17},{9,25},{17,1},{25,9},{2,18},{10... | collective-permute-start | bytes 147464 | tf_op jit(solution)/shard_map/ppermute | solution.py:158
  82.1 1.8 %columns.1 = (f32[6,32,256]{2,1,0:T(8,128)}, f32[6,32,256]{2,1,0:T(8,128)}) custom-call(s32[18]{0:T(128)S(1)} %copy-done.10, s32[12]{0:T(128)S(1)} %copy-done.11, f32[6,32,256]{2,1,0:T(8,128)S(1)} %get-tuple-element.48.mine1.kept1, bf16[6,32,256]{2,1,0:T(8,128)(2,1)S(1)} %bitcast.84, f32[6,32,256]{2,1,0:T(8,128)S(1)} %get-tuple-element.46.mine2.kept2, ...), custom_call_target="tpu_custom_call" | custom-call | tf_op jit(solution)/shard_map/columns/pallas_call | solution.py:266
  83.9 0.0 collective-permute-done.16
  83.9 1.0 %collective-permute-done.15 = bf16[3,32,256]{2,1,0:T(8,128)(2,1)S(1)} collective-permute-done((bf16[3,32,256]{2,1,0:T(8,128)(2,1)S(1)}, bf16[3,32,256]{2,1,0:T(8,128)(2,1)S(1)}, u32[]{:S(2)}, u32[]{:S(2)}) %collective-permute-start.15) | collective-permute-done | bytes 49184 | tf_op jit(solution)/shard_map/ppermute | solution.py:158
  84.9 0.6 slice_bitcast_fusion
  (43 shorter events, 0.6 us)
Async XLA Ops:
  0.6 20.9 %copy-start.11 = (s32[12]{0:T(128)S(1)}, s32[12]{0:T(128)}, u32[]{:S(2)}) copy-start(s32[12]{0:T(128)} %struct2.5) | copy-start | bytes 148
  0.6 20.9 %copy-start.10 = (s32[18]{0:T(128)S(1)}, s32[18]{0:T(128)}, u32[]{:S(2)}) copy-start(s32[18]{0:T(128)} %struct1.5) | copy-start | bytes 220
  0.7 20.9 %copy-start = (bf16[6,1,3,1,256,256]{5,4,3,2,1,0:T(8,128)(2,1)S(1)}, bf16[6,1,3,1,256,256]{5,4,3,2,1,0:T(8,128)(2,1)}, u32[]{:S(2)}) copy-start(bf16[6,1,3,1,256,256]{5,4,3,2,1,0:T(8,128)(2,1)} %param.8) | copy-start | bytes 7077892
  0.7 20.8 %copy-start.6 = (f32[256,256]{1,0:T(8,128)S(1)}, f32[256,256]{1,0:T(8,128)}, u32[]{:S(2)}) copy-start(f32[256,256]{1,0:T(8,128)} %inv1.3) | copy-start | bytes 786436
  0.7 20.8 %copy-start.8 = (f32[256,256]{1,0:T(8,128)S(1)}, f32[256,256]{1,0:T(8,128)}, u32[]{:S(2)}) copy-start(f32[256,256]{1,0:T(8,128)} %inv2.3) | copy-start | bytes 786436
  1.8 6.3 %collective-permute-start = (bf16[2,3,32,256]{3,2,1,0:T(8,128)(2,1)S(1)}, bf16[2,3,32,256]{3,2,1,0:T(8,128)(2,1)S(1)}, u32[]{:S(2)}, u32[]{:S(2)}) collective-permute-start(bf16[2,3,32,256]{3,2,1,0:T(8,128)(2,1)S(1)} %get-tuple-element.51), channel_id=1, source_target_pairs={{0,0},{1,16},{2,8},{3,24},{4,4},{5,20},{6,12},{7,28},{8,1},{9,17},... | collective-permute-start | bytes 294920 | tf_op jit(solution)/shard_map/ppermute | solution.py:192
  4.9 7.6 %collective-permute-start.1 = (bf16[2,3,32,256]{3,2,1,0:T(8,128)(2,1)S(1)}, bf16[2,3,32,256]{3,2,1,0:T(8,128)(2,1)S(1)}, u32[]{:S(2)}, u32[]{:S(2)}) collective-permute-start(bf16[2,3,32,256]{3,2,1,0:T(8,128)(2,1)S(1)} %get-tuple-element.52), channel_id=1, source_target_pairs={{0,4},{1,20},{2,12},{3,28},{4,0},{5,16},{6,8},{7,24},{8,5},{9,21},... | collective-permute-start | bytes 294920 | tf_op jit(solution)/shard_map/ppermute | solution.py:192
  12.5 6.3 %collective-permute-start.2 = (bf16[1,2,2,3,32,256]{5,4,3,2,1,0:T(8,128)(2,1)S(1)}, bf16[1,2,2,3,32,256]{5,4,3,2,1,0:T(8,128)(2,1)S(1)}, u32[]{:S(2)}, u32[]{:S(2)}) collective-permute-start(bf16[1,2,2,3,32,256]{5,4,3,2,1,0:T(8,128)(2,1)S(1)} %maximum_bitcast_fusion), channel_id=1, source_target_pairs={{0,16},{8,24},{16,0},{24,8},{1,17},{9,25},{17,1},{25,9},{2,18},{10... | collective-permute-start | bytes 589832 | tf_op jit(solution)/shard_map/ppermute | solution.py:158
  18.8 2.5 %collective-permute-start.3 = (bf16[2,2,2,3,32,256]{5,4,3,2,1,0:T(8,128)(2,1)S(1)}, bf16[2,2,2,3,32,256]{5,4,3,2,1,0:T(8,128)(2,1)S(1)}, u32[]{:S(2)}, u32[]{:S(2)}) collective-permute-start(bf16[2,2,2,3,32,256]{5,4,3,2,1,0:T(8,128)(2,1)S(1)} %pad_maximum_fusion.1), channel_id=1, source_target_pairs={{0,8},{8,0},{16,24},{24,16},{1,9},{9,1},{17,25},{25,17},{2,10},{10... | collective-permute-start | bytes 1179656 | tf_op jit(solution)/shard_map/ppermute | solution.py:158
  21.4 5.7 %copy-start.4 = (bf16[6,1,32,256]{3,2,1,0:T(8,128)(2,1)S(1)}, bf16[6,1,32,256]{3,2,1,0:T(8,128)(2,1)}, u32[]{:S(2)}) copy-start(bf16[6,1,32,256]{3,2,1,0:T(8,128)(2,1)} %param.9) | copy-start | bytes 294916
  21.4 5.7 %copy-start.5 = (bf16[6,1,32,256]{3,2,1,0:T(8,128)(2,1)S(1)}, bf16[6,1,32,256]{3,2,1,0:T(8,128)(2,1)}, u32[]{:S(2)}) copy-start(bf16[6,1,32,256]{3,2,1,0:T(8,128)(2,1)} %param.10) | copy-start | bytes 294916
  21.5 18.2 %copy-start.13 = (bf16[256,256]{1,0:T(8,128)(2,1)S(1)}, bf16[256,256]{1,0:T(8,128)(2,1)}, u32[]{:S(2)}) copy-start(bf16[256,256]{1,0:T(8,128)(2,1)} %link.1) | copy-start | bytes 393220
  25.4 0.9 %copy-start.1 = (f32[4,6,32,256]{3,2,1,0:T(8,128)}, f32[4,6,32,256]{3,2,1,0:T(8,128)S(1)}, u32[]{:S(2)}) copy-start(f32[4,6,32,256]{3,2,1,0:T(8,128)S(1)} %get-tuple-element.20.after) | copy-start | bytes 2359300
  26.3 0.7 copy-start.12
  27.1 19.0 %collective-permute-start.4 = (bf16[4,6,32,256]{3,2,1,0:T(8,128)(2,1)}, bf16[4,6,32,256]{3,2,1,0:T(8,128)(2,1)S(1)}, u32[]{:S(2)}, u32[]{:S(2)}) collective-permute-start(bf16[4,6,32,256]{3,2,1,0:T(8,128)(2,1)} %get-tuple-element.21), channel_id=1, source_target_pairs={{0,1},{1,0},{2,3},{3,2},{4,5},{5,4},{6,7},{7,6},{8,9},{9,8},{10,11... | collective-permute-start | bytes 1179656 | tf_op jit(solution)/shard_map/ppermute | solution.py:158
  27.1 12.5 %collective-permute-start.6 = (bf16[2,6,32,256]{3,2,1,0:T(8,128)(2,1)S(1)}, bf16[2,6,32,256]{3,2,1,0:T(8,128)(2,1)S(1)}, u32[]{:S(2)}, u32[]{:S(2)}) collective-permute-start(bf16[2,6,32,256]{3,2,1,0:T(8,128)(2,1)S(1)} %pad_maximum_fusion.2), channel_id=1, source_target_pairs={{0,4},{1,5},{2,6},{3,7},{4,0},{5,1},{6,2},{7,3},{8,12},{9,13},{10,... | collective-permute-start | bytes 589832 | tf_op jit(solution)/shard_map/ppermute | solution.py:158
  30.9 16.3 %collective-permute-start.7 = (bf16[4,6,32,256]{3,2,1,0:T(8,128)(2,1)}, bf16[4,6,32,256]{3,2,1,0:T(8,128)(2,1)S(1)}, u32[]{:S(2)}, u32[]{:S(2)}) collective-permute-start(bf16[4,6,32,256]{3,2,1,0:T(8,128)(2,1)} %copy-done.12), channel_id=1, source_target_pairs={{0,2},{1,3},{2,0},{3,1},{4,6},{5,7},{6,4},{7,5},{8,10},{9,11},{10,... | collective-permute-start | bytes 1179656 | tf_op jit(solution)/shard_map/ppermute | solution.py:158
  39.7 1.1 %copy-start.2 = (f32[4,6,32,256]{3,2,1,0:T(8,128)S(1)}, f32[4,6,32,256]{3,2,1,0:T(8,128)}, u32[]{:S(2)}) copy-start(f32[4,6,32,256]{3,2,1,0:T(8,128)} %copy-done.1) | copy-start | bytes 2359300
  40.8 0.9 %copy-start.7 = (f32[256,256]{1,0:T(8,128)S(1)}, f32[256,256]{1,0:T(8,128)}, u32[]{:S(2)}) copy-start(f32[256,256]{1,0:T(8,128)} %inv1.3) | copy-start | bytes 786436
  41.7 0.9 %copy-start.9 = (f32[256,256]{1,0:T(8,128)S(1)}, f32[256,256]{1,0:T(8,128)}, u32[]{:S(2)}) copy-start(f32[256,256]{1,0:T(8,128)} %inv2.3) | copy-start | bytes 786436
  42.7 3.4 %copy-start.3 = (f32[4,6,32,256]{3,2,1,0:T(8,128)S(1)}, f32[4,6,32,256]{3,2,1,0:T(8,128)}, u32[]{:S(2)}) copy-start(f32[4,6,32,256]{3,2,1,0:T(8,128)} %copy-done.1) | copy-start | bytes 2359300
  46.2 5.9 %collective-permute-start.5 = (bf16[2,6,32,256]{3,2,1,0:T(8,128)(2,1)S(1)}, bf16[2,6,32,256]{3,2,1,0:T(8,128)(2,1)S(1)}, u32[]{:S(2)}, u32[]{:S(2)}) collective-permute-start(bf16[2,6,32,256]{3,2,1,0:T(8,128)(2,1)S(1)} %fusion), channel_id=1, source_target_pairs={{0,2},{1,3},{2,0},{3,1},{4,6},{5,7},{6,4},{7,5},{8,10},{9,11},{10,... | collective-permute-start | bytes 589832 | tf_op jit(solution)/shard_map/ppermute | solution.py:158
  47.4 5.1 %collective-permute-start.8 = (bf16[2,6,32,256]{3,2,1,0:T(8,128)(2,1)S(1)}, bf16[2,6,32,256]{3,2,1,0:T(8,128)(2,1)S(1)}, u32[]{:S(2)}, u32[]{:S(2)}) collective-permute-start(bf16[2,6,32,256]{3,2,1,0:T(8,128)(2,1)S(1)} %fusion.1), channel_id=1, source_target_pairs={{0,1},{1,0},{2,3},{3,2},{4,5},{5,4},{6,7},{7,6},{8,9},{9,8},{10,11... | collective-permute-start | bytes 589832 | tf_op jit(solution)/shard_map/ppermute | solution.py:158
  53.6 5.2 %collective-permute-start.9 = (bf16[3,4,32,256]{3,2,1,0:T(8,128)(2,1)S(1)}, bf16[3,4,32,256]{3,2,1,0:T(8,128)(2,1)S(1)}, u32[]{:S(2)}, u32[]{:S(2)}) collective-permute-start(bf16[3,4,32,256]{3,2,1,0:T(8,128)(2,1)S(1)} %fusion.2), channel_id=1, source_target_pairs={{0,1},{1,0},{2,3},{3,2},{4,5},{5,4},{6,7},{7,6},{8,9},{9,8},{10,11... | collective-permute-start | bytes 589832 | tf_op jit(solution)/shard_map/ppermute | solution.py:158
  58.9 3.6 %collective-permute-start.10 = (bf16[3,2,32,256]{3,2,0,1:T(8,128)(2,1)S(1)}, bf16[3,2,32,256]{3,2,0,1:T(8,128)(2,1)S(1)}, u32[]{:S(2)}, u32[]{:S(2)}) collective-permute-start(bf16[3,2,32,256]{3,2,0,1:T(8,128)(2,1)S(1)} %fusion.3), channel_id=1, source_target_pairs={{0,2},{1,3},{2,0},{3,1},{4,6},{5,7},{6,4},{7,5},{8,10},{9,11},{10,... | collective-permute-start | bytes 294920 | tf_op jit(solution)/shard_map/ppermute | solution.py:158
  59.4 6.1 %collective-permute-start.11 = (bf16[1,6,32,256]{3,2,1,0:T(8,128)(2,1)S(1)}, bf16[1,6,32,256]{3,2,1,0:T(8,128)(2,1)S(1)}, u32[]{:S(2)}, u32[]{:S(2)}) collective-permute-start(bf16[1,6,32,256]{3,2,1,0:T(8,128)(2,1)S(1)} %dynamic-slice_convert_fusion.1), channel_id=1, source_target_pairs={{0,4},{1,5},{2,6},{3,7},{4,0},{5,1},{6,2},{7,3},{8,12},{9,13},{10,... | collective-permute-start | bytes 294920 | tf_op jit(solution)/shard_map/ppermute | solution.py:158
  65.5 4.9 %collective-permute-start.12 = (bf16[3,1,32,256]{3,2,0,1:T(8,128)(2,1)S(1)}, bf16[3,1,32,256]{3,2,0,1:T(8,128)(2,1)S(1)}, u32[]{:S(2)}, u32[]{:S(2)}) collective-permute-start(bf16[3,1,32,256]{3,2,0,1:T(8,128)(2,1)S(1)} %dynamic-slice_convert_fusion.2), channel_id=1, source_target_pairs={{0,4},{1,5},{2,6},{3,7},{4,0},{5,1},{6,2},{7,3},{8,12},{9,13},{10,... | collective-permute-start | bytes 147464 | tf_op jit(solution)/shard_map/ppermute | solution.py:158
  68.1 4.5 %collective-permute-start.13 = (bf16[1,6,32,256]{3,2,1,0:T(8,128)(2,1)S(1)}, bf16[1,6,32,256]{3,2,1,0:T(8,128)(2,1)S(1)}, u32[]{:S(2)}, u32[]{:S(2)}) collective-permute-start(bf16[1,6,32,256]{3,2,1,0:T(8,128)(2,1)S(1)} %dynamic-slice_convert_fusion), channel_id=1, source_target_pairs={{0,4},{1,5},{2,6},{3,7},{4,0},{5,1},{6,2},{7,3},{8,12},{9,13},{10,... | collective-permute-start | bytes 294920 | tf_op jit(solution)/shard_map/ppermute | solution.py:158
  72.6 11.3 %collective-permute-start.16 = (bf16[3,32,256]{2,1,0:T(8,128)(2,1)S(1)}, bf16[3,32,256]{2,1,0:T(8,128)(2,1)S(1)}, u32[]{:S(2)}, u32[]{:S(2)}) collective-permute-start(bf16[3,32,256]{2,1,0:T(8,128)(2,1)S(1)} %convert_element_type.98), channel_id=1, source_target_pairs={{0,24},{8,16},{16,8},{24,0},{1,25},{9,17},{17,9},{25,1},{2,26},{10... | collective-permute-start | bytes 147464 | tf_op jit(solution)/shard_map/ppermute | solution.py:158
  80.5 4.3 %collective-permute-start.15 = (bf16[3,32,256]{2,1,0:T(8,128)(2,1)S(1)}, bf16[3,32,256]{2,1,0:T(8,128)(2,1)S(1)}, u32[]{:S(2)}, u32[]{:S(2)}) collective-permute-start(bf16[3,32,256]{2,1,0:T(8,128)(2,1)S(1)} %convert_element_type.98), channel_id=1, source_target_pairs={{0,16},{8,24},{16,0},{24,8},{1,17},{9,25},{17,1},{25,9},{2,18},{10... | collective-permute-start | bytes 147464 | tf_op jit(solution)/shard_map/ppermute | solution.py:158
  82.1 2.7 %collective-permute-start.14 = (bf16[3,32,256]{2,1,0:T(8,128)(2,1)S(1)}, bf16[3,32,256]{2,1,0:T(8,128)(2,1)S(1)}, u32[]{:S(2)}, u32[]{:S(2)}) collective-permute-start(bf16[3,32,256]{2,1,0:T(8,128)(2,1)S(1)} %convert_element_type.98), channel_id=1, source_target_pairs={{0,8},{8,0},{16,24},{24,16},{1,9},{9,1},{17,25},{25,17},{2,10},{10... | collective-permute-start | bytes 147464 | tf_op jit(solution)/shard_map/ppermute | solution.py:158

commit v3 on v2

--- a/solution.py
+++ b/solution.py
@@ -102,14 +102,17 @@
                     sends[p][j, a + i] = jnp.where(upper, x, y).astype(jnp.bfloat16)
 
 
-def prepare_kernel(n_row, struct1, struct2, mine1, mine2, other, link, inv1, inv2, after, rows, linked, out, whole):
+def factor_rows(panel, inverse, keep):
+    blocks, slab, width = panel.shape
+    flat = panel[...].astype(jnp.float32).reshape(blocks * slab, width).astype(jnp.bfloat16)
+    product = split_dot(flat, inverse[...]).reshape(blocks, slab, width)
+    return jnp.where(keep, product, 0.0)
+
+
+def prepare_kernel(n_row, struct1, struct2, mine1, mine2, link, inv1, inv2, after, rows, linked, out, whole):
     blocks, slab, width = mine1.shape
-    for p, (struct, inverse, parts) in enumerate(((struct1, inv1, (mine1, other.at[0])), (struct2, inv2, (mine2, other.at[1])))):
-        keep = listed(struct, blocks, n_row)
-        for i, part in enumerate(parts):
-            flat = part[...].astype(jnp.float32).reshape(blocks * slab, width).astype(jnp.bfloat16)
-            product = split_dot(flat, inverse[...]).reshape(blocks, slab, width)
-            rows[p, i] = jnp.where(keep, product, 0.0).astype(jnp.bfloat16)
+    for p, (struct, mine, inverse) in enumerate(((struct1, mine1, inv1), (struct2, mine2, inv2))):
+        rows[p] = factor_rows(mine, inverse, listed(struct, blocks, n_row)).astype(jnp.bfloat16)
     linked[...] = exact_dot(link[...].astype(jnp.float32), inv2[...])
     link = linked[...]
     gram1 = exact_dot(inv1[...], inv1[...], 0)
@@ -121,20 +124,21 @@
     out[...] = whole[:, place, :]
 
 
-def sum_kernel(rows, mine1, theirs1, mine2, theirs2, linked, after, out):
+def sum_kernel(n_row, struct1, struct2, rows, other1, other2, inv1, inv2, mine1, theirs1, mine2, theirs2, linked, after, out):
     blocks, slab, width = mine1.shape
     flat = (blocks * slab, width)
 
     def both(a, b):
         return jnp.concatenate([a.reshape(flat), b.reshape(flat)], axis=0)
 
-    def factor(p):
-        return rows[p].astype(jnp.float32).reshape(2 * blocks * slab, width).astype(jnp.bfloat16)
+    def factor(p, struct, other, inverse):
+        theirs = factor_rows(other, inverse, listed(struct, blocks, n_row))
+        return both(rows[p].astype(jnp.float32), theirs).astype(jnp.bfloat16)
 
     link = linked[...]
     sum1 = both(mine1[...], theirs1[...])
-    u2 = factor(1)
-    first = split_dot(factor(0), sum1, 0)
+    u2 = factor(1, struct2, other2, inv2)
+    first = split_dot(factor(0, struct1, other1, inv1), sum1, 0)
     cross = split_dot(u2, sum1, 0)
     top = cross.T - split_dot(first, link)
     second = split_dot(u2, both(mine2[...], theirs2[...]), 0) - split_dot(cross, link) - split_dot(link, top, 0)
@@ -158,10 +162,9 @@
     return lax.ppermute(value, axis, [(i, i ^ mask) for i in range(size)])
 
 
-def halves(value, axis, mine):
-    kept = lax.dynamic_index_in_dim(value, mine, axis, keepdims=False)
-    sent = lax.dynamic_index_in_dim(value, 1 - mine, axis, keepdims=False)
-    return kept, sent.astype(jnp.bfloat16)
+def halves(value, axis, ways):
+    kept, sent = (lax.dynamic_index_in_dim(value, way, axis, keepdims=False) for way in ways)
+    return kept, sent
 
 
 def body(stored_inverse, panel_first, panel_second, panel_link, inv_first, inv_second, struct_first, struct_second):
@@ -178,9 +181,13 @@
     panel = (row_blocks, slab, width)
 
     panels = [panel_first.reshape(panel), panel_second.reshape(panel)]
+    _, turn = place_of(here_col, n_row)
+    picks = [((s - turn + cycle) % cycle).astype(jnp.uint32) for s in range(cycle)]
+    ways = [(here_col >> bit) & 1 for bit in range(n_bits)]
+    ways = [(way.astype(jnp.uint32), (1 - way).astype(jnp.uint32)) for way in ways]
+    panels, picks, ways = lax.optimization_barrier((panels, picks, ways))
 
     turns = jnp.stack(panels).reshape(2, col_blocks, cycle, slab, width)
-    _, turn = place_of(here_col, n_row)
     got = []
     for s in range(cycle):
         moves = []
@@ -188,7 +195,7 @@
             for c in range(n_col):
                 row, t = place_of(c, n_row)
                 moves.append((r * n_col + c, row * n_col + r + (s - t) % cycle * n_row))
-        part = lax.dynamic_index_in_dim(turns, (s - turn) % cycle, 2, keepdims=False)
+        part = lax.dynamic_index_in_dim(turns, picks[s], 2, keepdims=False)
         got.append(lax.ppermute(part, ("row", "col"), moves))
     pieces = jnp.stack(got)[None]
 
@@ -215,18 +222,19 @@
         name="products",
     )(struct_first, struct_second, inv_first, inv_second, stored, pieces)
 
-    panels, pieces = lax.optimization_barrier((panels, pieces))
-    other = swapped(jnp.stack(panels), "col", n_col, n_col // 2)
     rows, linked, consts = pl.pallas_call(
         functools.partial(prepare_kernel, n_row),
-        out_shape=[shape((2, 2) + panel, bf16), shape((width, width), f32), shape((3, slab, width), f32)],
-        in_specs=[SMEM, SMEM] + [VMEM] * 6 + [ANY],
+        out_shape=[shape((2,) + panel, bf16), shape((width, width), f32), shape((3, slab, width), f32)],
+        in_specs=[SMEM, SMEM] + [VMEM] * 5 + [ANY],
         out_specs=[VMEM] * 3,
         scratch_shapes=[pltpu.VMEM((3, width, width), f32)],
         compiler_params=big,
         name="prepare",
         cost_estimate=pl.CostEstimate(flops=6 * 10 * width**3, bytes_accessed=8 * width**2, transcendentals=0),
-    )(struct_first, struct_second, *panels, other, panel_link, inv_first, inv_second, split[0])
+    )(struct_first, struct_second, *panels, panel_link, inv_first, inv_second, split[0])
+
+    panels, consts = lax.optimization_barrier((panels, consts))
+    others = [swapped(p, "col", n_col, n_col // 2) for p in panels]
 
     last = []
     for p in range(2):
@@ -237,32 +245,28 @@
             low = 1 << left.index(bit)
             left.remove(bit)
             total = (keep + came.astype(f32)).reshape((-1, 2, low) + panel)
-            keep, send = halves(total, 1, (here_col >> bit) & 1)
-            keep, send = keep.reshape((-1,) + panel), send.reshape((-1,) + panel)
+            keep, theirs = halves(total, 1, ways[bit])
+            keep, theirs = keep.reshape((-1,) + panel), theirs.reshape((-1,) + panel)
             if left:
-                came = swapped(send, "col", n_col, 1 << bit)
-        theirs = lax.dynamic_index_in_dim(total, 1 - ((here_col >> bit) & 1), 1, keepdims=False)
-        last.append((keep.reshape(panel), theirs.reshape(panel), send))
+                came = swapped(theirs.astype(bf16), "col", n_col, 1 << bit)
+        last.append((keep[0], theirs[0]))
 
     sums = pl.pallas_call(
-        sum_kernel,
+        functools.partial(sum_kernel, n_row),
         out_shape=shape((3, n_col, slab, width), f32),
-        in_specs=[VMEM] * 6 + [ANY],
+        in_specs=[SMEM, SMEM] + [VMEM] * 10 + [ANY],
         out_specs=VMEM,
         compiler_params=big,
         name="sums",
-    )(rows, last[0][0], last[0][1], last[1][0], last[1][1], linked, consts)
-    done = []
-    for keep, _, send in last:
-        done += [keep, swapped(send, "col", n_col, n_col // 2).reshape(panel)]
+    )(struct_first, struct_second, rows, *others, inv_first, inv_second, last[0][0], last[0][1], last[1][0], last[1][1], linked, consts)
+    done = [swapped(theirs.astype(bf16), "col", n_col, n_col // 2) for _, theirs in last]
     for bit in range(n_bits):
-        if bit == n_bits - 1:
-            sums, done[1] = lax.optimization_barrier((sums, done[1]))
-        keep, send = halves(sums.reshape(3, -1, 2, slab, width), 2, (here_col >> bit) & 1)
-        sums = keep + swapped(send, "col", n_col, 1 << bit).astype(f32)
+        if bit >= n_bits - 2:
+            sums, done[bit - n_bits + 2] = lax.optimization_barrier((sums, done[bit - n_bits + 2]))
+        keep, send = halves(sums.reshape(3, -1, 2, slab, width), 2, ways[bit])
+        sums = keep + swapped(send.astype(bf16), "col", n_col, 1 << bit).astype(f32)
 
     total = sums.reshape(3, slab, width)
-    total, done[3] = lax.optimization_barrier((total, done[3]))
     column_first, column_second = pl.pallas_call(
         functools.partial(column_kernel, n_row),
         out_shape=[shape(panel, f32)] * 2,
@@ -270,7 +274,7 @@
         out_specs=[VMEM] * 2,
         compiler_params=big,
         name="columns",
-    )(struct_first, struct_second, *done, linked)
+    )(struct_first, struct_second, last[0][0], done[0], last[1][0], done[1], linked)
 
     send = total.astype(bf16)
     for m in range(1, n_row):

time: 85.8 us -> 77.6 us (0.904)
  the two profiles are of different devices: /device:TPU:13 before, /device:TPU:0 now
where the time goes in v3:
time: 77.6 us; the launch traced here: 77.5 us
  starting transfers between devices  31.7 us (41%)
  waiting for transfers between devices  31.7 us (41%)
  Pallas kernels  10.5 us (14%)
  other arithmetic  1.72 us (2%)
  between operations  1.02 us (1%)
  local copies, waits for them, and re-layouts  0.82 us (1%)
    ppermute x16, waiting for transfers between devices, swapped(): return lax.ppermute(value, axis, [(i, i ^ mask) for i in range(size)])  29 us
    ppermute x16, starting transfers between devices, swapped(): return lax.ppermute(value, axis, [(i, i ^ mask) for i in range(size)])  26.9 us
    ppermute x2, starting transfers between devices, body(): got.append(lax.ppermute(part, ('row', 'col'), moves))  4.76 us
    pallas_call x1, Pallas kernels, body(): pl.pallas_call(functools.partial(product_kernel, n_row, n_col, (orders[0]...  3.29 us
    pallas_call x1, Pallas kernels, body(): pl.pallas_call(functools.partial(prepare_kernel, n_row), out_shape=[shape...  3.2 us
    ppermute x2, waiting for transfers between devices, body(): got.append(lax.ppermute(part, ('row', 'col'), moves))  2.69 us
    pallas_call x1, Pallas kernels, body(): pl.pallas_call(functools.partial(sum_kernel, n_row), out_shape=shape((3,...  2.28 us
    pallas_call x1, Pallas kernels, body(): pl.pallas_call(functools.partial(column_kernel, n_row), out_shape=[shape(...  1.78 us
  transfers between devices with their start and end apart: 18, of which 13 were waited for; matrix products, arithmetic and copies ran while one was open for 1% of the time, Pallas kernels for 6%

profile of v3, /device:TPU:0, one launch (start us, length us, event | category | flops | bytes accessed | tf_op | source)
XLA Modules:
  0.0 77.5 jit_solution(7443436021381431142)
XLA Ops:
  0.8 1.0 %fusion.7 = (bf16[2,3,32,256]{3,2,1,0:T(8,128)(2,1)S(1)}, bf16[2,3,32,256]{3,2,1,0:T(8,128)(2,1)S(1)}) fusion(u32[]{:T(128)S(6)} %convert_element_type.92, bf16[1,3,2,32,256]{4,3,2,1,0:T(8,128)(2,1)} %bitcast.79, bf16[1,3,2,32,256]{4,3,2,1,0:T(8,128)(2,1)} %bitcast.82, u32[]{:T(128)S(6)} %convert_element_type.93), kind=kLoop, calls=%fused_computation.28 | loop fusion | flops 98304 | bytes 393224 | tf_op jit(solution)/shard_map/jit(dynamic_index_in_dim)/squeeze | solution.py:198
  1.8 0.7 collective-permute-start
  2.5 4.1 %collective-permute-start.1 = (bf16[2,3,32,256]{3,2,1,0:T(8,128)(2,1)S(1)}, bf16[2,3,32,256]{3,2,1,0:T(8,128)(2,1)S(1)}, u32[]{:S(2)}, u32[]{:S(2)}) collective-permute-start(bf16[2,3,32,256]{3,2,1,0:T(8,128)(2,1)S(1)} %get-tuple-element.76), channel_id=1, source_target_pairs={{0,4},{1,20},{2,12},{3,28},{4,0},{5,16},{6,8},{7,24},{8,5},{9,21},... | collective-permute-start | bytes 294920 | tf_op jit(solution)/shard_map/ppermute | solution.py:199
  6.6 0.0 collective-permute-done
  6.6 2.7 %collective-permute-done.1 = bf16[2,3,32,256]{3,2,1,0:T(8,128)(2,1)S(1)} collective-permute-done((bf16[2,3,32,256]{3,2,1,0:T(8,128)(2,1)S(1)}, bf16[2,3,32,256]{3,2,1,0:T(8,128)(2,1)S(1)}, u32[]{:S(2)}, u32[]{:S(2)}) %collective-permute-start.1) | collective-permute-done | bytes 98336 | tf_op jit(solution)/shard_map/ppermute | solution.py:199
  9.3 9.0 %collective-permute-start.2 = (bf16[1,2,2,3,32,256]{5,4,3,2,1,0:T(8,128)(2,1)S(1)}, bf16[1,2,2,3,32,256]{5,4,3,2,1,0:T(8,128)(2,1)S(1)}, u32[]{:S(2)}, u32[]{:S(2)}) collective-permute-start(bf16[1,2,2,3,32,256]{5,4,3,2,1,0:T(8,128)(2,1)S(1)} %maximum_bitcast_fusion), channel_id=1, source_target_pairs={{0,16},{8,24},{16,0},{24,8},{1,17},{9,25},{17,1},{25,9},{2,18},{10... | collective-permute-start | bytes 589832 | tf_op jit(solution)/shard_map/ppermute | solution.py:162
  18.3 3.9 %collective-permute-done.2 = bf16[1,2,2,3,32,256]{5,4,3,2,1,0:T(8,128)(2,1)S(1)} collective-permute-done((bf16[1,2,2,3,32,256]{5,4,3,2,1,0:T(8,128)(2,1)S(1)}, bf16[1,2,2,3,32,256]{5,4,3,2,1,0:T(8,128)(2,1)S(1)}, u32[]{:S(2)}, u32[]{:S(2)}) %collective-permute-start.2) | collective-permute-done | bytes 196640 | tf_op jit(solution)/shard_map/ppermute | solution.py:162
  22.3 0.1 collective-permute-start.3
  22.4 1.7 %collective-permute-done.3 = bf16[2,2,2,3,32,256]{5,4,3,2,1,0:T(8,128)(2,1)S(1)} collective-permute-done((bf16[2,2,2,3,32,256]{5,4,3,2,1,0:T(8,128)(2,1)S(1)}, bf16[2,2,2,3,32,256]{5,4,3,2,1,0:T(8,128)(2,1)S(1)}, u32[]{:S(2)}, u32[]{:S(2)}) %collective-permute-start.3) | collective-permute-done | bytes 393248 | tf_op jit(solution)/shard_map/ppermute | solution.py:162
  24.1 0.0 copy-start.3
  24.1 0.0 copy-start.4
  24.1 0.0 copy-start.7
  24.1 0.1 pad_maximum_fusion.pieces
  24.3 3.3 %products.1 = (f32[4,6,32,256]{3,2,1,0:T(8,128)S(1)}, f32[4,6,32,256]{3,2,1,0:T(8,128)S(1)}, bf16[4,6,32,256]{3,2,1,0:T(8,128)(2,1)S(1)}, bf16[4,6,32,256]{3,2,1,0:T(8,128)(2,1)S(1)}) custom-call(s32[18]{0:T(128)S(1)} %copy-done.5, s32[12]{0:T(128)S(1)} %copy-done.6, f32[256,256]{1,0:T(8,128)S(1)} %copy-done.1, f32[256,256]{1,0:T(8,128)S(1)} %copy-done.2, ...), custom_call_target="tpu_custom_call" | custom-call | tf_op jit(solution)/shard_map/products/pallas_call | solution.py:212
  27.6 0.1 collective-permute-start.8
  27.7 1.6 %collective-permute-start.4 = (bf16[4,6,32,256]{3,2,1,0:T(8,128)(2,1)S(1)}, bf16[4,6,32,256]{3,2,1,0:T(8,128)(2,1)S(1)}, u32[]{:S(2)}, u32[]{:S(2)}) collective-permute-start(bf16[4,6,32,256]{3,2,1,0:T(8,128)(2,1)S(1)} %get-tuple-element.36), channel_id=1, source_target_pairs={{0,1},{1,0},{2,3},{3,2},{4,5},{5,4},{6,7},{7,6},{8,9},{9,8},{10,11... | collective-permute-start | bytes 1179656 | tf_op jit(solution)/shard_map/ppermute | solution.py:162
  29.3 3.2 %prepare.1 = (bf16[2,6,32,256]{3,2,1,0:T(8,128)(2,1)S(1)}, f32[256,256]{1,0:T(8,128)S(1)}, f32[3,32,256]{2,1,0:T(8,128)S(1)}) custom-call(s32[18]{0:T(128)S(1)} %copy-done.5, s32[12]{0:T(128)S(1)} %copy-done.6, bf16[6,32,256]{2,1,0:T(8,128)(2,1)S(1)} %bitcast.80, bf16[6,32,256]{2,1,0:T(8,128)(2,1)S(1)} %bitcast.83, bf16[256,256]{1,0:T(8,128)(2,1)S(1)} %copy-done.7, ...), custom_call_target="tpu_custom_call" | custom-call | flops 1006632960 | bytes 524288 | tf_op jit(solution)/shard_map/prepare/pallas_call | solution.py:225
  32.5 4.0 %collective-permute-start.6 = (bf16[6,32,256]{2,1,0:T(8,128)(2,1)S(1)}, bf16[6,32,256]{2,1,0:T(8,128)(2,1)S(1)}, u32[]{:S(2)}, u32[]{:S(2)}) collective-permute-start(bf16[6,32,256]{2,1,0:T(8,128)(2,1)S(1)} %bitcast.81), channel_id=1, source_target_pairs={{0,4},{1,5},{2,6},{3,7},{4,0},{5,1},{6,2},{7,3},{8,12},{9,13},{10,... | collective-permute-start | bytes 294920 | tf_op jit(solution)/shard_map/ppermute | solution.py:162
  36.5 0.1 collective-permute-start.7
  36.6 5.7 %collective-permute-done.8 = bf16[4,6,32,256]{3,2,1,0:T(8,128)(2,1)S(1)} collective-permute-done((bf16[4,6,32,256]{3,2,1,0:T(8,128)(2,1)S(1)}, bf16[4,6,32,256]{3,2,1,0:T(8,128)(2,1)S(1)}, u32[]{:S(2)}, u32[]{:S(2)}) %collective-permute-start.8) | collective-permute-done | bytes 393248 | tf_op jit(solution)/shard_map/ppermute | solution.py:162
  42.3 0.1 convert_add_fusion
  42.4 1.2 %collective-permute-start.9 = (bf16[2,6,32,256]{3,2,1,0:T(8,128)(2,1)S(1)}, bf16[2,6,32,256]{3,2,1,0:T(8,128)(2,1)S(1)}, u32[]{:S(2)}, u32[]{:S(2)}) collective-permute-start(bf16[2,6,32,256]{3,2,1,0:T(8,128)(2,1)S(1)} %fusion.1), channel_id=1, source_target_pairs={{0,1},{1,0},{2,3},{3,2},{4,5},{5,4},{6,7},{7,6},{8,9},{9,8},{10,11... | collective-permute-start | bytes 589832 | tf_op jit(solution)/shard_map/ppermute | solution.py:162
  43.7 0.0 collective-permute-done.4
  43.7 0.1 convert_add_fusion.1
  43.9 0.1 collective-permute-start.5
  43.9 4.6 %collective-permute-done.9 = bf16[2,6,32,256]{3,2,1,0:T(8,128)(2,1)S(1)} collective-permute-done((bf16[2,6,32,256]{3,2,1,0:T(8,128)(2,1)S(1)}, bf16[2,6,32,256]{3,2,1,0:T(8,128)(2,1)S(1)}, u32[]{:S(2)}, u32[]{:S(2)}) %collective-permute-start.9) | collective-permute-done | bytes 196640 | tf_op jit(solution)/shard_map/ppermute | solution.py:162
  48.6 1.2 %collective-permute-done.5 = bf16[2,6,32,256]{3,2,1,0:T(8,128)(2,1)S(1)} collective-permute-done((bf16[2,6,32,256]{3,2,1,0:T(8,128)(2,1)S(1)}, bf16[2,6,32,256]{3,2,1,0:T(8,128)(2,1)S(1)}, u32[]{:S(2)}, u32[]{:S(2)}) %collective-permute-start.5) | collective-permute-done | bytes 196640 | tf_op jit(solution)/shard_map/ppermute | solution.py:162
  49.9 0.0 collective-permute-done.6.other1
  49.9 0.0 collective-permute-done.7.other2
  50.0 2.3 %sums.1 = f32[3,8,32,256]{3,2,1,0:T(8,128)S(1)} custom-call(s32[18]{0:T(128)S(1)} %copy-done.5, s32[12]{0:T(128)S(1)} %copy-done.6, bf16[2,6,32,256]{3,2,1,0:T(8,128)(2,1)S(1)} %get-tuple-element.40.rows, bf16[6,32,256]{2,1,0:T(8,128)(2,1)S(1)} %collective-permute-done.6.other1, bf16[6,32,256]{2,1,0:T(8,128)(2,1)S(1)} %collective-permute-done.7.other2, ...), custom_call_target="tpu_custom_call" | custom-call | tf_op jit(solution)/shard_map/sums/pallas_call | solution.py:254
  52.3 0.9 %collective-permute-start.10 = (bf16[3,4,32,256]{3,2,1,0:T(8,128)(2,1)S(1)}, bf16[3,4,32,256]{3,2,1,0:T(8,128)(2,1)S(1)}, u32[]{:S(2)}, u32[]{:S(2)}) collective-permute-start(bf16[3,4,32,256]{3,2,1,0:T(8,128)(2,1)S(1)} %fusion.2), channel_id=1, source_target_pairs={{0,1},{1,0},{2,3},{3,2},{4,5},{5,4},{6,7},{7,6},{8,9},{9,8},{10,11... | collective-permute-start | bytes 589832 | tf_op jit(solution)/shard_map/ppermute | solution.py:162
  53.1 1.0 %collective-permute-start.11 = (bf16[6,32,256]{2,1,0:T(8,128)(2,1)S(1)}, bf16[6,32,256]{2,1,0:T(8,128)(2,1)S(1)}, u32[]{:S(2)}, u32[]{:S(2)}) collective-permute-start(bf16[6,32,256]{2,1,0:T(8,128)(2,1)S(1)} %get-tuple-element.69), channel_id=1, source_target_pairs={{0,4},{1,5},{2,6},{3,7},{4,0},{5,1},{6,2},{7,3},{8,12},{9,13},{10,... | collective-permute-start | bytes 294920 | tf_op jit(solution)/shard_map/ppermute | solution.py:162
  54.2 3.8 %collective-permute-done.10 = bf16[3,4,32,256]{3,2,1,0:T(8,128)(2,1)S(1)} collective-permute-done((bf16[3,4,32,256]{3,2,1,0:T(8,128)(2,1)S(1)}, bf16[3,4,32,256]{3,2,1,0:T(8,128)(2,1)S(1)}, u32[]{:S(2)}, u32[]{:S(2)}) %collective-permute-start.10) | collective-permute-done | bytes 196640 | tf_op jit(solution)/shard_map/ppermute | solution.py:162
  58.1 1.3 %collective-permute-done.11.came1 = bf16[6,32,256]{2,1,0:T(8,128)(2,1)S(1)} collective-permute-done((bf16[6,32,256]{2,1,0:T(8,128)(2,1)S(1)}, bf16[6,32,256]{2,1,0:T(8,128)(2,1)S(1)}, u32[]{:S(2)}, u32[]{:S(2)}) %collective-permute-start.11) | collective-permute-done | bytes 98336 | tf_op jit(solution)/shard_map/ppermute | solution.py:162
  59.4 0.1 collective-permute-start.12
  59.4 2.8 %collective-permute-start.13 = (bf16[6,32,256]{2,1,0:T(8,128)(2,1)S(1)}, bf16[6,32,256]{2,1,0:T(8,128)(2,1)S(1)}, u32[]{:S(2)}, u32[]{:S(2)}) collective-permute-start(bf16[6,32,256]{2,1,0:T(8,128)(2,1)S(1)} %get-tuple-element.67), channel_id=1, source_target_pairs={{0,4},{1,5},{2,6},{3,7},{4,0},{5,1},{6,2},{7,3},{8,12},{9,13},{10,... | collective-permute-start | bytes 294920 | tf_op jit(solution)/shard_map/ppermute | solution.py:162
  62.3 1.8 %collective-permute-done.12 = bf16[3,2,32,256]{3,2,0,1:T(8,128)(2,1)S(1)} collective-permute-done((bf16[3,2,32,256]{3,2,0,1:T(8,128)(2,1)S(1)}, bf16[3,2,32,256]{3,2,0,1:T(8,128)(2,1)S(1)}, u32[]{:S(2)}, u32[]{:S(2)}) %collective-permute-start.12) | collective-permute-done | bytes 98336 | tf_op jit(solution)/shard_map/ppermute | solution.py:162
  64.1 1.0 %collective-permute-done.13.came2 = bf16[6,32,256]{2,1,0:T(8,128)(2,1)S(1)} collective-permute-done((bf16[6,32,256]{2,1,0:T(8,128)(2,1)S(1)}, bf16[6,32,256]{2,1,0:T(8,128)(2,1)S(1)}, u32[]{:S(2)}, u32[]{:S(2)}) %collective-permute-start.13) | collective-permute-done | bytes 98336 | tf_op jit(solution)/shard_map/ppermute | solution.py:162
  65.1 3.4 %collective-permute-start.14 = (bf16[3,1,32,256]{3,2,0,1:T(8,128)(2,1)S(1)}, bf16[3,1,32,256]{3,2,0,1:T(8,128)(2,1)S(1)}, u32[]{:S(2)}, u32[]{:S(2)}) collective-permute-start(bf16[3,1,32,256]{3,2,0,1:T(8,128)(2,1)S(1)} %dynamic-slice_convert_fusion), channel_id=1, source_target_pairs={{0,4},{1,5},{2,6},{3,7},{4,0},{5,1},{6,2},{7,3},{8,12},{9,13},{10,... | collective-permute-start | bytes 147464 | tf_op jit(solution)/shard_map/ppermute | solution.py:162
  68.5 2.1 %collective-permute-done.14 = bf16[3,1,32,256]{3,2,0,1:T(8,128)(2,1)S(1)} collective-permute-done((bf16[3,1,32,256]{3,2,0,1:T(8,128)(2,1)S(1)}, bf16[3,1,32,256]{3,2,0,1:T(8,128)(2,1)S(1)}, u32[]{:S(2)}, u32[]{:S(2)}) %collective-permute-start.14) | collective-permute-done | bytes 49184 | tf_op jit(solution)/shard_map/ppermute | solution.py:162
  70.6 0.1 collective-permute-start.15
  70.7 2.4 %collective-permute-start.16 = (bf16[3,32,256]{2,1,0:T(8,128)(2,1)S(1)}, bf16[3,32,256]{2,1,0:T(8,128)(2,1)S(1)}, u32[]{:S(2)}, u32[]{:S(2)}) collective-permute-start(bf16[3,32,256]{2,1,0:T(8,128)(2,1)S(1)} %bitcast_convert_fusion.3), channel_id=1, source_target_pairs={{0,16},{8,24},{16,0},{24,8},{1,17},{9,25},{17,1},{25,9},{2,18},{10... | collective-permute-start | bytes 147464 | tf_op jit(solution)/shard_map/ppermute | solution.py:162
  73.1 0.1 collective-permute-start.17
  73.2 1.8 %columns.1 = (f32[6,32,256]{2,1,0:T(8,128)}, f32[6,32,256]{2,1,0:T(8,128)}) custom-call(s32[18]{0:T(128)S(1)} %copy-done.5, s32[12]{0:T(128)S(1)} %copy-done.6, f32[6,32,256]{2,1,0:T(8,128)S(1)} %get-tuple-element.72.mine1.kept1, bf16[6,32,256]{2,1,0:T(8,128)(2,1)S(1)} %collective-permute-done.11.came1, f32[6,32,256]{2,1,0:T(8,128)S(1)} %get-tuple-element.71.mine2.kept2, ...), custom_call_target="tpu_custom_call" | custom-call | tf_op jit(solution)/shard_map/columns/pallas_call | solution.py:270
  74.9 0.0 collective-permute-done.15
  74.9 0.5 collective-permute-done.16
  75.4 1.4 %collective-permute-done.17 = bf16[3,32,256]{2,1,0:T(8,128)(2,1)S(1)} collective-permute-done((bf16[3,32,256]{2,1,0:T(8,128)(2,1)S(1)}, bf16[3,32,256]{2,1,0:T(8,128)(2,1)S(1)}, u32[]{:S(2)}, u32[]{:S(2)}) %collective-permute-start.17) | collective-permute-done | bytes 49184 | tf_op jit(solution)/shard_map/ppermute | solution.py:162
  76.8 0.6 slice_bitcast_fusion
  (29 shorter events, 0.5 us)
Async XLA Ops:
  0.6 23.6 %copy-start = (bf16[6,1,3,1,256,256]{5,4,3,2,1,0:T(8,128)(2,1)S(1)}, bf16[6,1,3,1,256,256]{5,4,3,2,1,0:T(8,128)(2,1)}, u32[]{:S(2)}) copy-start(bf16[6,1,3,1,256,256]{5,4,3,2,1,0:T(8,128)(2,1)} %param.8) | copy-start | bytes 7077892
  0.6 23.6 %copy-start.1 = (f32[256,256]{1,0:T(8,128)S(1)}, f32[256,256]{1,0:T(8,128)}, u32[]{:S(2)}) copy-start(f32[256,256]{1,0:T(8,128)} %inv1.5) | copy-start | bytes 786436
  0.7 23.6 %copy-start.2 = (f32[256,256]{1,0:T(8,128)S(1)}, f32[256,256]{1,0:T(8,128)}, u32[]{:S(2)}) copy-start(f32[256,256]{1,0:T(8,128)} %inv2.5) | copy-start | bytes 786436
  0.7 23.6 %copy-start.5 = (s32[18]{0:T(128)S(1)}, s32[18]{0:T(128)}, u32[]{:S(2)}) copy-start(s32[18]{0:T(128)} %struct1.7) | copy-start | bytes 220
  0.7 23.6 %copy-start.6 = (s32[12]{0:T(128)S(1)}, s32[12]{0:T(128)}, u32[]{:S(2)}) copy-start(s32[12]{0:T(128)} %struct2.7) | copy-start | bytes 148
  1.8 4.8 %collective-permute-start = (bf16[2,3,32,256]{3,2,1,0:T(8,128)(2,1)S(1)}, bf16[2,3,32,256]{3,2,1,0:T(8,128)(2,1)S(1)}, u32[]{:S(2)}, u32[]{:S(2)}) collective-permute-start(bf16[2,3,32,256]{3,2,1,0:T(8,128)(2,1)S(1)} %get-tuple-element.75), channel_id=1, source_target_pairs={{0,0},{1,16},{2,8},{3,24},{4,4},{5,20},{6,12},{7,28},{8,1},{9,17},... | collective-permute-start | bytes 294920 | tf_op jit(solution)/shard_map/ppermute | solution.py:199
  2.5 6.8 %collective-permute-start.1 = (bf16[2,3,32,256]{3,2,1,0:T(8,128)(2,1)S(1)}, bf16[2,3,32,256]{3,2,1,0:T(8,128)(2,1)S(1)}, u32[]{:S(2)}, u32[]{:S(2)}) collective-permute-start(bf16[2,3,32,256]{3,2,1,0:T(8,128)(2,1)S(1)} %get-tuple-element.76), channel_id=1, source_target_pairs={{0,4},{1,20},{2,12},{3,28},{4,0},{5,16},{6,8},{7,24},{8,5},{9,21},... | collective-permute-start | bytes 294920 | tf_op jit(solution)/shard_map/ppermute | solution.py:199
  9.3 13.0 %collective-permute-start.2 = (bf16[1,2,2,3,32,256]{5,4,3,2,1,0:T(8,128)(2,1)S(1)}, bf16[1,2,2,3,32,256]{5,4,3,2,1,0:T(8,128)(2,1)S(1)}, u32[]{:S(2)}, u32[]{:S(2)}) collective-permute-start(bf16[1,2,2,3,32,256]{5,4,3,2,1,0:T(8,128)(2,1)S(1)} %maximum_bitcast_fusion), channel_id=1, source_target_pairs={{0,16},{8,24},{16,0},{24,8},{1,17},{9,25},{17,1},{25,9},{2,18},{10... | collective-permute-start | bytes 589832 | tf_op jit(solution)/shard_map/ppermute | solution.py:162
  22.3 1.8 %collective-permute-start.3 = (bf16[2,2,2,3,32,256]{5,4,3,2,1,0:T(8,128)(2,1)S(1)}, bf16[2,2,2,3,32,256]{5,4,3,2,1,0:T(8,128)(2,1)S(1)}, u32[]{:S(2)}, u32[]{:S(2)}) collective-permute-start(bf16[2,2,2,3,32,256]{5,4,3,2,1,0:T(8,128)(2,1)S(1)} %pad_maximum_fusion.1), channel_id=1, source_target_pairs={{0,8},{8,0},{16,24},{24,16},{1,9},{9,1},{17,25},{25,17},{2,10},{10... | collective-permute-start | bytes 1179656 | tf_op jit(solution)/shard_map/ppermute | solution.py:162
  24.1 5.2 %copy-start.3 = (bf16[6,1,32,256]{3,2,1,0:T(8,128)(2,1)S(1)}, bf16[6,1,32,256]{3,2,1,0:T(8,128)(2,1)}, u32[]{:S(2)}) copy-start(bf16[6,1,32,256]{3,2,1,0:T(8,128)(2,1)} %param.9) | copy-start | bytes 294916
  24.1 5.1 %copy-start.4 = (bf16[6,1,32,256]{3,2,1,0:T(8,128)(2,1)S(1)}, bf16[6,1,32,256]{3,2,1,0:T(8,128)(2,1)}, u32[]{:S(2)}) copy-start(bf16[6,1,32,256]{3,2,1,0:T(8,128)(2,1)} %param.10) | copy-start | bytes 294916
  24.1 5.1 %copy-start.7 = (bf16[256,256]{1,0:T(8,128)(2,1)S(1)}, bf16[256,256]{1,0:T(8,128)(2,1)}, u32[]{:S(2)}) copy-start(bf16[256,256]{1,0:T(8,128)(2,1)} %link.1) | copy-start | bytes 393220
  27.6 14.7 %collective-permute-start.8 = (bf16[4,6,32,256]{3,2,1,0:T(8,128)(2,1)S(1)}, bf16[4,6,32,256]{3,2,1,0:T(8,128)(2,1)S(1)}, u32[]{:S(2)}, u32[]{:S(2)}) collective-permute-start(bf16[4,6,32,256]{3,2,1,0:T(8,128)(2,1)S(1)} %get-tuple-element.46), channel_id=1, source_target_pairs={{0,2},{1,3},{2,0},{3,1},{4,6},{5,7},{6,4},{7,5},{8,10},{9,11},{10,... | collective-permute-start | bytes 1179656 | tf_op jit(solution)/shard_map/ppermute | solution.py:162
  27.7 16.0 %collective-permute-start.4 = (bf16[4,6,32,256]{3,2,1,0:T(8,128)(2,1)S(1)}, bf16[4,6,32,256]{3,2,1,0:T(8,128)(2,1)S(1)}, u32[]{:S(2)}, u32[]{:S(2)}) collective-permute-start(bf16[4,6,32,256]{3,2,1,0:T(8,128)(2,1)S(1)} %get-tuple-element.36), channel_id=1, source_target_pairs={{0,1},{1,0},{2,3},{3,2},{4,5},{5,4},{6,7},{7,6},{8,9},{9,8},{10,11... | collective-permute-start | bytes 1179656 | tf_op jit(solution)/shard_map/ppermute | solution.py:162
  32.5 17.5 %collective-permute-start.6 = (bf16[6,32,256]{2,1,0:T(8,128)(2,1)S(1)}, bf16[6,32,256]{2,1,0:T(8,128)(2,1)S(1)}, u32[]{:S(2)}, u32[]{:S(2)}) collective-permute-start(bf16[6,32,256]{2,1,0:T(8,128)(2,1)S(1)} %bitcast.81), channel_id=1, source_target_pairs={{0,4},{1,5},{2,6},{3,7},{4,0},{5,1},{6,2},{7,3},{8,12},{9,13},{10,... | collective-permute-start | bytes 294920 | tf_op jit(solution)/shard_map/ppermute | solution.py:162
  36.5 13.5 %collective-permute-start.7 = (bf16[6,32,256]{2,1,0:T(8,128)(2,1)S(1)}, bf16[6,32,256]{2,1,0:T(8,128)(2,1)S(1)}, u32[]{:S(2)}, u32[]{:S(2)}) collective-permute-start(bf16[6,32,256]{2,1,0:T(8,128)(2,1)S(1)} %bitcast.84), channel_id=1, source_target_pairs={{0,4},{1,5},{2,6},{3,7},{4,0},{5,1},{6,2},{7,3},{8,12},{9,13},{10,... | collective-permute-start | bytes 294920 | tf_op jit(solution)/shard_map/ppermute | solution.py:162
  42.4 6.1 %collective-permute-start.9 = (bf16[2,6,32,256]{3,2,1,0:T(8,128)(2,1)S(1)}, bf16[2,6,32,256]{3,2,1,0:T(8,128)(2,1)S(1)}, u32[]{:S(2)}, u32[]{:S(2)}) collective-permute-start(bf16[2,6,32,256]{3,2,1,0:T(8,128)(2,1)S(1)} %fusion.1), channel_id=1, source_target_pairs={{0,1},{1,0},{2,3},{3,2},{4,5},{5,4},{6,7},{7,6},{8,9},{9,8},{10,11... | collective-permute-start | bytes 589832 | tf_op jit(solution)/shard_map/ppermute | solution.py:162
  43.9 6.0 %collective-permute-start.5 = (bf16[2,6,32,256]{3,2,1,0:T(8,128)(2,1)S(1)}, bf16[2,6,32,256]{3,2,1,0:T(8,128)(2,1)S(1)}, u32[]{:S(2)}, u32[]{:S(2)}) collective-permute-start(bf16[2,6,32,256]{3,2,1,0:T(8,128)(2,1)S(1)} %fusion), channel_id=1, source_target_pairs={{0,2},{1,3},{2,0},{3,1},{4,6},{5,7},{6,4},{7,5},{8,10},{9,11},{10,... | collective-permute-start | bytes 589832 | tf_op jit(solution)/shard_map/ppermute | solution.py:162
  52.3 5.7 %collective-permute-start.10 = (bf16[3,4,32,256]{3,2,1,0:T(8,128)(2,1)S(1)}, bf16[3,4,32,256]{3,2,1,0:T(8,128)(2,1)S(1)}, u32[]{:S(2)}, u32[]{:S(2)}) collective-permute-start(bf16[3,4,32,256]{3,2,1,0:T(8,128)(2,1)S(1)} %fusion.2), channel_id=1, source_target_pairs={{0,1},{1,0},{2,3},{3,2},{4,5},{5,4},{6,7},{7,6},{8,9},{9,8},{10,11... | collective-permute-start | bytes 589832 | tf_op jit(solution)/shard_map/ppermute | solution.py:162
  53.1 6.2 %collective-permute-start.11 = (bf16[6,32,256]{2,1,0:T(8,128)(2,1)S(1)}, bf16[6,32,256]{2,1,0:T(8,128)(2,1)S(1)}, u32[]{:S(2)}, u32[]{:S(2)}) collective-permute-start(bf16[6,32,256]{2,1,0:T(8,128)(2,1)S(1)} %get-tuple-element.69), channel_id=1, source_target_pairs={{0,4},{1,5},{2,6},{3,7},{4,0},{5,1},{6,2},{7,3},{8,12},{9,13},{10,... | collective-permute-start | bytes 294920 | tf_op jit(solution)/shard_map/ppermute | solution.py:162
  59.4 4.7 %collective-permute-start.12 = (bf16[3,2,32,256]{3,2,0,1:T(8,128)(2,1)S(1)}, bf16[3,2,32,256]{3,2,0,1:T(8,128)(2,1)S(1)}, u32[]{:S(2)}, u32[]{:S(2)}) collective-permute-start(bf16[3,2,32,256]{3,2,0,1:T(8,128)(2,1)S(1)} %fusion.3), channel_id=1, source_target_pairs={{0,2},{1,3},{2,0},{3,1},{4,6},{5,7},{6,4},{7,5},{8,10},{9,11},{10,... | collective-permute-start | bytes 294920 | tf_op jit(solution)/shard_map/ppermute | solution.py:162
  59.4 5.7 %collective-permute-start.13 = (bf16[6,32,256]{2,1,0:T(8,128)(2,1)S(1)}, bf16[6,32,256]{2,1,0:T(8,128)(2,1)S(1)}, u32[]{:S(2)}, u32[]{:S(2)}) collective-permute-start(bf16[6,32,256]{2,1,0:T(8,128)(2,1)S(1)} %get-tuple-element.67), channel_id=1, source_target_pairs={{0,4},{1,5},{2,6},{3,7},{4,0},{5,1},{6,2},{7,3},{8,12},{9,13},{10,... | collective-permute-start | bytes 294920 | tf_op jit(solution)/shard_map/ppermute | solution.py:162
  65.1 5.5 %collective-permute-start.14 = (bf16[3,1,32,256]{3,2,0,1:T(8,128)(2,1)S(1)}, bf16[3,1,32,256]{3,2,0,1:T(8,128)(2,1)S(1)}, u32[]{:S(2)}, u32[]{:S(2)}) collective-permute-start(bf16[3,1,32,256]{3,2,0,1:T(8,128)(2,1)S(1)} %dynamic-slice_convert_fusion), channel_id=1, source_target_pairs={{0,4},{1,5},{2,6},{3,7},{4,0},{5,1},{6,2},{7,3},{8,12},{9,13},{10,... | collective-permute-start | bytes 147464 | tf_op jit(solution)/shard_map/ppermute | solution.py:162
  70.6 4.4 %collective-permute-start.15 = (bf16[3,32,256]{2,1,0:T(8,128)(2,1)S(1)}, bf16[3,32,256]{2,1,0:T(8,128)(2,1)S(1)}, u32[]{:S(2)}, u32[]{:S(2)}) collective-permute-start(bf16[3,32,256]{2,1,0:T(8,128)(2,1)S(1)} %bitcast_convert_fusion.3), channel_id=1, source_target_pairs={{0,8},{8,0},{16,24},{24,16},{1,9},{9,1},{17,25},{25,17},{2,10},{10... | collective-permute-start | bytes 147464 | tf_op jit(solution)/shard_map/ppermute | solution.py:162
  70.7 4.8 %collective-permute-start.16 = (bf16[3,32,256]{2,1,0:T(8,128)(2,1)S(1)}, bf16[3,32,256]{2,1,0:T(8,128)(2,1)S(1)}, u32[]{:S(2)}, u32[]{:S(2)}) collective-permute-start(bf16[3,32,256]{2,1,0:T(8,128)(2,1)S(1)} %bitcast_convert_fusion.3), channel_id=1, source_target_pairs={{0,16},{8,24},{16,0},{24,8},{1,17},{9,25},{17,1},{25,9},{2,18},{10... | collective-permute-start | bytes 147464 | tf_op jit(solution)/shard_map/ppermute | solution.py:162
  73.1 3.7 %collective-permute-start.17 = (bf16[3,32,256]{2,1,0:T(8,128)(2,1)S(1)}, bf16[3,32,256]{2,1,0:T(8,128)(2,1)S(1)}, u32[]{:S(2)}, u32[]{:S(2)}) collective-permute-start(bf16[3,32,256]{2,1,0:T(8,128)(2,1)S(1)} %bitcast_convert_fusion.3), channel_id=1, source_target_pairs={{0,24},{8,16},{16,8},{24,0},{1,25},{9,17},{17,9},{25,1},{2,26},{10... | collective-permute-start | bytes 147464 | tf_op jit(solution)/shard_map/ppermute | solution.py:162

commit v4 on v3

--- a/solution.py
+++ b/solution.py
@@ -47,13 +47,11 @@
 
 
 def slice_of(row, turn, n_row):
-    half = n_row // 2
-    return 2 * (turn * half + lax.rem(row, half)) + row // half
+    return turn * n_row + row
 
 
 def place_of(piece, n_row):
-    half = n_row // 2
-    return (piece % 2) * half + piece // 2 % half, piece // 2 // half
+    return piece % n_row, piece // n_row
 
 
 def product_kernel(n_row, n_col, first_bits, struct1, struct2, inv1, inv2, stored, pieces, *rest):
@@ -124,28 +122,19 @@
     out[...] = whole[:, place, :]
 
 
-def sum_kernel(n_row, struct1, struct2, rows, other1, other2, inv1, inv2, mine1, theirs1, mine2, theirs2, linked, after, out):
-    blocks, slab, width = mine1.shape
+def sum_kernel(rows, kept1, came1, kept2, came2, linked, after, out):
+    blocks, slab, width = kept1.shape
     flat = (blocks * slab, width)
-
-    def both(a, b):
-        return jnp.concatenate([a.reshape(flat), b.reshape(flat)], axis=0)
-
-    def factor(p, struct, other, inverse):
-        theirs = factor_rows(other, inverse, listed(struct, blocks, n_row))
-        return both(rows[p].astype(jnp.float32), theirs).astype(jnp.bfloat16)
-
+    sum1 = (kept1[...] + came1[...].astype(jnp.float32)).reshape(flat)
+    sum2 = (kept2[...] + came2[...].astype(jnp.float32)).reshape(flat)
+    u1, u2 = (rows[p].astype(jnp.float32).reshape(flat).astype(jnp.bfloat16) for p in range(2))
     link = linked[...]
-    sum1 = both(mine1[...], theirs1[...])
-    u2 = factor(1, struct2, other2, inv2)
-    first = split_dot(factor(0, struct1, other1, inv1), sum1, 0)
+    first = split_dot(u1, sum1, 0)
     cross = split_dot(u2, sum1, 0)
     top = cross.T - split_dot(first, link)
-    second = split_dot(u2, both(mine2[...], theirs2[...]), 0) - split_dot(cross, link) - split_dot(link, top, 0)
-    n_col = width // slab
-    out[0] = first.reshape(n_col, slab, width)
-    out[1] = top.reshape(n_col, slab, width)
-    out[2] = second.reshape(n_col, slab, width)
+    second = split_dot(u2, sum2, 0) - split_dot(cross, link) - split_dot(link, top, 0)
+    for i, part in enumerate((first, top, second)):
+        out[:, i] = part.reshape(width // slab, slab, width).astype(out.dtype)
 
 
 def column_kernel(n_row, struct1, struct2, kept1, came1, kept2, came2, linked, column1, column2):
@@ -207,7 +196,7 @@
         bit //= 2
     pieces = jnp.stack([pieces[order.index(m)] for m in range(n_row)])
 
-    orders = (list(range(n_bits)), [1, 0] + list(range(2, n_bits)))
+    orders = (list(range(1, n_bits)) + [0], list(range(n_bits)))
     half = (n_col // 2,) + panel
     split = pl.pallas_call(
         functools.partial(product_kernel, n_row, n_col, (orders[0][0], orders[1][0])),
@@ -233,40 +222,29 @@
         cost_estimate=pl.CostEstimate(flops=6 * 10 * width**3, bytes_accessed=8 * width**2, transcendentals=0),
     )(struct_first, struct_second, *panels, panel_link, inv_first, inv_second, split[0])
 
-    panels, consts = lax.optimization_barrier((panels, consts))
-    others = [swapped(p, "col", n_col, n_col // 2) for p in panels]
-
     last = []
     for p in range(2):
-        keep, send = split[p], split[2 + p]
+        keep, came = split[p], swapped(split[2 + p], "col", n_col, 1 << orders[p][0])
         left = sorted(set(range(n_bits)) - {orders[p][0]})
-        came = swapped(send, "col", n_col, 1 << orders[p][0])
         for bit in orders[p][1:]:
             low = 1 << left.index(bit)
             left.remove(bit)
             total = (keep + came.astype(f32)).reshape((-1, 2, low) + panel)
-            keep, theirs = halves(total, 1, ways[bit])
-            keep, theirs = keep.reshape((-1,) + panel), theirs.reshape((-1,) + panel)
-            if left:
-                came = swapped(theirs.astype(bf16), "col", n_col, 1 << bit)
-        last.append((keep[0], theirs[0]))
+            keep, send = halves(total, 1, ways[bit])
+            keep = keep.reshape((-1,) + panel)
+            came = swapped(send.astype(bf16).reshape((-1,) + panel), "col", n_col, 1 << bit)
+        last += [keep[0], came[0]]
 
     sums = pl.pallas_call(
-        functools.partial(sum_kernel, n_row),
-        out_shape=shape((3, n_col, slab, width), f32),
-        in_specs=[SMEM, SMEM] + [VMEM] * 10 + [ANY],
+        sum_kernel,
+        out_shape=shape((n_col, 3, slab, width), bf16),
+        in_specs=[VMEM] * 6 + [ANY],
         out_specs=VMEM,
         compiler_params=big,
         name="sums",
-    )(struct_first, struct_second, rows, *others, inv_first, inv_second, last[0][0], last[0][1], last[1][0], last[1][1], linked, consts)
-    done = [swapped(theirs.astype(bf16), "col", n_col, n_col // 2) for _, theirs in last]
-    for bit in range(n_bits):
-        if bit >= n_bits - 2:
-            sums, done[bit - n_bits + 2] = lax.optimization_barrier((sums, done[bit - n_bits + 2]))
-        keep, send = halves(sums.reshape(3, -1, 2, slab, width), 2, ways[bit])
-        sums = keep + swapped(send.astype(bf16), "col", n_col, 1 << bit).astype(f32)
-
-    total = sums.reshape(3, slab, width)
+    )(rows, *last, linked, consts)
+    sums = lax.all_to_all(sums, "col", 0, 0, tiled=True)
+
     column_first, column_second = pl.pallas_call(
         functools.partial(column_kernel, n_row),
         out_shape=[shape(panel, f32)] * 2,
@@ -274,8 +252,9 @@
         out_specs=[VMEM] * 2,
         compiler_params=big,
         name="columns",
-    )(struct_first, struct_second, last[0][0], done[0], last[1][0], done[1], linked)
-
+    )(struct_first, struct_second, *last, linked)
+
+    total = jnp.sum(sums.astype(f32), axis=0)
     send = total.astype(bf16)
     for m in range(1, n_row):
         total = total + swapped(send, "row", n_row, m).astype(f32)

time: 77.6 us -> 80.5 us (1.037)
  blocking collectives: 0 us -> 13.9 us
  starting transfers between devices: 31.7 us -> 21.3 us
  Pallas kernels: 10.5 us -> 9.15 us
    all_to_all x0 -> x1, blocking collectives: none -> 13.9 us  [body(): sums = lax.all_to_all(sums, 'col', 0, 0, tiled=True)]
    ppermute x16 -> x11, starting transfers between devices: 26.9 us -> 16.5 us  [swapped(): return lax.ppermute(value, axis, [(i, i ^ mask) for i in range(size)])]
    pallas_call x1, Pallas kernels: 2.28 us -> 0.89 us  [body(): pl.pallas_call(sum_kernel, out_shape=shape((n_col, 3, slab, width), bf16)...]
    ppermute x16 -> x11, waiting for transfers between devices: 29 us -> 29.9 us  [swapped(): return lax.ppermute(value, axis, [(i, i ^ mask) for i in range(size)])]
  transfers between devices with their start and end apart: 18 -> 13, of which waited for: 13 -> 10; matrix products, arithmetic and copies ran while one was open for 1% -> 1% of each run, Pallas kernels for 6% -> 6%
where the time goes in v4:
time: 80.5 us; the launch traced here: 80.3 us
  waiting for transfers between devices  32.5 us (40%)
  starting transfers between devices  21.3 us (26%)
  blocking collectives  13.9 us (17%)
  Pallas kernels  9.15 us (11%)
  other arithmetic  1.63 us (2%)
  between operations  0.95 us (1%)
  local copies, waits for them, and re-layouts  0.84 us (1%)
    ppermute x11, waiting for transfers between devices, swapped(): return lax.ppermute(value, axis, [(i, i ^ mask) for i in range(size)])  29.9 us
    ppermute x11, starting transfers between devices, swapped(): return lax.ppermute(value, axis, [(i, i ^ mask) for i in range(size)])  16.5 us
    all_to_all x1, blocking collectives, body(): sums = lax.all_to_all(sums, 'col', 0, 0, tiled=True)  13.9 us
    ppermute x2, starting transfers between devices, body(): got.append(lax.ppermute(part, ('row', 'col'), moves))  4.77 us
    pallas_call x1, Pallas kernels, body(): pl.pallas_call(functools.partial(product_kernel, n_row, n_col, (orders[0]...  3.29 us
    pallas_call x1, Pallas kernels, body(): pl.pallas_call(functools.partial(prepare_kernel, n_row), out_shape=[shape...  3.2 us
    ppermute x2, waiting for transfers between devices, body(): got.append(lax.ppermute(part, ('row', 'col'), moves))  2.6 us
    pallas_call x1, Pallas kernels, body(): pl.pallas_call(functools.partial(column_kernel, n_row), out_shape=[shape(...  1.78 us
  transfers between devices with their start and end apart: 13, of which 10 were waited for; matrix products, arithmetic and copies ran while one was open for 1% of the time, Pallas kernels for 6%

profile of v4, /device:TPU:0, one launch (start us, length us, event | category | flops | bytes accessed | tf_op | source)
XLA Modules:
  0.0 80.3 jit_solution(5573063849670295137)
XLA Ops:
  0.6 0.0 copy-start
  0.6 0.0 copy-start.1
  0.7 1.0 %fusion.5 = (bf16[2,3,32,256]{3,2,1,0:T(8,128)(2,1)S(1)}, bf16[2,3,32,256]{3,2,1,0:T(8,128)(2,1)S(1)}) fusion(u32[]{:T(128)S(6)} %convert_element_type.81, bf16[1,3,2,32,256]{4,3,2,1,0:T(8,128)(2,1)} %bitcast.50, bf16[1,3,2,32,256]{4,3,2,1,0:T(8,128)(2,1)} %bitcast.52, u32[]{:T(128)S(6)} %convert_element_type.82), kind=kLoop, calls=%fused_computation.23 | loop fusion | flops 98304 | bytes 393224 | tf_op jit(solution)/shard_map/jit(dynamic_index_in_dim)/squeeze | solution.py:187
  1.8 0.7 collective-permute-start
  2.5 4.1 %collective-permute-start.1 = (bf16[2,3,32,256]{3,2,1,0:T(8,128)(2,1)S(1)}, bf16[2,3,32,256]{3,2,1,0:T(8,128)(2,1)S(1)}, u32[]{:S(2)}, u32[]{:S(2)}) collective-permute-start(bf16[2,3,32,256]{3,2,1,0:T(8,128)(2,1)S(1)} %get-tuple-element.56), channel_id=1, source_target_pairs={{0,4},{1,12},{2,20},{3,28},{4,0},{5,8},{6,16},{7,24},{8,5},{9,13},... | collective-permute-start | bytes 294920 | tf_op jit(solution)/shard_map/ppermute | solution.py:188
  6.6 0.0 collective-permute-done
  6.6 2.6 %collective-permute-done.1 = bf16[2,3,32,256]{3,2,1,0:T(8,128)(2,1)S(1)} collective-permute-done((bf16[2,3,32,256]{3,2,1,0:T(8,128)(2,1)S(1)}, bf16[2,3,32,256]{3,2,1,0:T(8,128)(2,1)S(1)}, u32[]{:S(2)}, u32[]{:S(2)}) %collective-permute-start.1) | collective-permute-done | bytes 98336 | tf_op jit(solution)/shard_map/ppermute | solution.py:188
  9.2 8.5 %collective-permute-start.2 = (bf16[1,2,2,3,32,256]{5,4,3,2,1,0:T(8,128)(2,1)S(1)}, bf16[1,2,2,3,32,256]{5,4,3,2,1,0:T(8,128)(2,1)S(1)}, u32[]{:S(2)}, u32[]{:S(2)}) collective-permute-start(bf16[1,2,2,3,32,256]{5,4,3,2,1,0:T(8,128)(2,1)S(1)} %maximum_bitcast_fusion), channel_id=1, source_target_pairs={{0,16},{8,24},{16,0},{24,8},{1,17},{9,25},{17,1},{25,9},{2,18},{10... | collective-permute-start | bytes 589832 | tf_op jit(solution)/shard_map/ppermute | solution.py:151
  17.7 4.9 %collective-permute-done.2 = bf16[1,2,2,3,32,256]{5,4,3,2,1,0:T(8,128)(2,1)S(1)} collective-permute-done((bf16[1,2,2,3,32,256]{5,4,3,2,1,0:T(8,128)(2,1)S(1)}, bf16[1,2,2,3,32,256]{5,4,3,2,1,0:T(8,128)(2,1)S(1)}, u32[]{:S(2)}, u32[]{:S(2)}) %collective-permute-start.2) | collective-permute-done | bytes 196640 | tf_op jit(solution)/shard_map/ppermute | solution.py:151
  22.7 0.1 collective-permute-start.3
  22.7 1.7 %collective-permute-done.3 = bf16[2,2,2,3,32,256]{5,4,3,2,1,0:T(8,128)(2,1)S(1)} collective-permute-done((bf16[2,2,2,3,32,256]{5,4,3,2,1,0:T(8,128)(2,1)S(1)}, bf16[2,2,2,3,32,256]{5,4,3,2,1,0:T(8,128)(2,1)S(1)}, u32[]{:S(2)}, u32[]{:S(2)}) %collective-permute-start.3) | collective-permute-done | bytes 393248 | tf_op jit(solution)/shard_map/ppermute | solution.py:151
  24.5 0.0 copy-start.3
  24.5 0.0 copy-start.4
  24.5 0.0 copy-start.7
  24.5 0.1 pad_maximum_fusion.pieces
  24.6 0.0 copy-done
  24.6 0.0 copy-done.1
  24.6 0.0 copy-done.2
  24.7 0.0 copy-done.5
  24.7 0.0 copy-done.6
  24.7 3.3 %products.1 = (f32[4,6,32,256]{3,2,1,0:T(8,128)S(1)}, f32[4,6,32,256]{3,2,1,0:T(8,128)S(1)}, bf16[4,6,32,256]{3,2,1,0:T(8,128)(2,1)S(1)}, bf16[4,6,32,256]{3,2,1,0:T(8,128)(2,1)S(1)}) custom-call(s32[18]{0:T(128)S(1)} %copy-done.5, s32[12]{0:T(128)S(1)} %copy-done.6, f32[256,256]{1,0:T(8,128)S(1)} %copy-done.1, f32[256,256]{1,0:T(8,128)S(1)} %copy-done.2, ...), custom_call_target="tpu_custom_call" | custom-call | tf_op jit(solution)/shard_map/products/pallas_call | solution.py:201
  28.0 0.1 collective-permute-start.7
  28.0 0.6 collective-permute-start.4
  28.7 0.0 copy-done.7
  28.7 3.2 %prepare.1 = (bf16[2,6,32,256]{3,2,1,0:T(8,128)(2,1)S(1)}, f32[256,256]{1,0:T(8,128)S(1)}, f32[3,32,256]{2,1,0:T(8,128)S(1)}) custom-call(s32[18]{0:T(128)S(1)} %copy-done.5, s32[12]{0:T(128)S(1)} %copy-done.6, bf16[6,32,256]{2,1,0:T(8,128)(2,1)S(1)} %bitcast.51, bf16[6,32,256]{2,1,0:T(8,128)(2,1)S(1)} %bitcast.53, bf16[256,256]{1,0:T(8,128)(2,1)S(1)} %copy-done.7, ...), custom_call_target="tpu_custom_call" | custom-call | flops 1006632960 | bytes 524288 | tf_op jit(solution)/shard_map/prepare/pallas_call | solution.py:214
  31.9 7.3 %collective-permute-done.7 = bf16[4,6,32,256]{3,2,1,0:T(8,128)(2,1)S(1)} collective-permute-done((bf16[4,6,32,256]{3,2,1,0:T(8,128)(2,1)S(1)}, bf16[4,6,32,256]{3,2,1,0:T(8,128)(2,1)S(1)}, u32[]{:S(2)}, u32[]{:S(2)}) %collective-permute-start.7) | collective-permute-done | bytes 393248 | tf_op jit(solution)/shard_map/ppermute | solution.py:151
  39.2 0.1 convert_add_fusion
  39.4 0.6 collective-permute-start.8
  40.0 0.0 collective-permute-done.4
  40.0 0.1 convert_add_fusion.1
  40.2 3.9 %collective-permute-start.5 = (bf16[2,6,32,256]{3,2,1,0:T(8,128)(2,1)S(1)}, bf16[2,6,32,256]{3,2,1,0:T(8,128)(2,1)S(1)}, u32[]{:S(2)}, u32[]{:S(2)}) collective-permute-start(bf16[2,6,32,256]{3,2,1,0:T(8,128)(2,1)S(1)} %fusion), channel_id=1, source_target_pairs={{0,4},{1,5},{2,6},{3,7},{4,0},{5,1},{6,2},{7,3},{8,12},{9,13},{10,... | collective-permute-start | bytes 589832 | tf_op jit(solution)/shard_map/ppermute | solution.py:151
  44.1 5.2 %collective-permute-done.8 = bf16[2,6,32,256]{3,2,1,0:T(8,128)(2,1)S(1)} collective-permute-done((bf16[2,6,32,256]{3,2,1,0:T(8,128)(2,1)S(1)}, bf16[2,6,32,256]{3,2,1,0:T(8,128)(2,1)S(1)}, u32[]{:S(2)}, u32[]{:S(2)}) %collective-permute-start.8) | collective-permute-done | bytes 196640 | tf_op jit(solution)/shard_map/ppermute | solution.py:151
  49.4 0.4 collective-permute-start.9
  49.8 5.3 %collective-permute-done.5 = bf16[2,6,32,256]{3,2,1,0:T(8,128)(2,1)S(1)} collective-permute-done((bf16[2,6,32,256]{3,2,1,0:T(8,128)(2,1)S(1)}, bf16[2,6,32,256]{3,2,1,0:T(8,128)(2,1)S(1)}, u32[]{:S(2)}, u32[]{:S(2)}) %collective-permute-start.5) | collective-permute-done | bytes 196640 | tf_op jit(solution)/shard_map/ppermute | solution.py:151
  55.2 0.3 collective-permute-start.6
  55.6 1.1 %collective-permute-done.9 = bf16[1,6,32,256]{3,2,1,0:T(8,128)(2,1)S(1)} collective-permute-done((bf16[1,6,32,256]{3,2,1,0:T(8,128)(2,1)S(1)}, bf16[1,6,32,256]{3,2,1,0:T(8,128)(2,1)S(1)}, u32[]{:S(2)}, u32[]{:S(2)}) %collective-permute-start.9) | collective-permute-done | bytes 98336 | tf_op jit(solution)/shard_map/ppermute | solution.py:151
  56.7 3.3 %collective-permute-done.6 = bf16[1,6,32,256]{3,2,1,0:T(8,128)(2,1)S(1)} collective-permute-done((bf16[1,6,32,256]{3,2,1,0:T(8,128)(2,1)S(1)}, bf16[1,6,32,256]{3,2,1,0:T(8,128)(2,1)S(1)}, u32[]{:S(2)}, u32[]{:S(2)}) %collective-permute-start.6) | collective-permute-done | bytes 98336 | tf_op jit(solution)/shard_map/ppermute | solution.py:151
  59.9 0.9 %sums.1 = bf16[8,3,32,256]{3,2,1,0:T(8,128)(2,1)S(1)} custom-call(bf16[2,6,32,256]{3,2,1,0:T(8,128)(2,1)S(1)} %get-tuple-element.42.rows, f32[6,32,256]{2,1,0:T(8,128)S(1)} %dynamic-slice_bitcast_fusion.1.kept1, bf16[6,32,256]{2,1,0:T(8,128)(2,1)S(1)} %bitcast.48, f32[6,32,256]{2,1,0:T(8,128)S(1)} %dynamic-slice_bitcast_fusion.kept2, ...), custom_call_target="tpu_custom_call" | custom-call | tf_op jit(solution)/shard_map/sums/pallas_call | solution.py:238
  60.8 13.9 %all_to_all.5 = bf16[8,3,32,256]{3,2,1,0:T(8,128)(2,1)S(1)} all-to-all(bf16[8,3,32,256]{3,2,1,0:T(8,128)(2,1)S(1)} %sums.1), channel_id=1, replica_groups=mesh['row'=4,'col'=8] {'col'}, dimensions={0} | all-to-all | bytes 786432 | tf_op jit(solution)/shard_map/all_to_all | solution.py:246
  74.7 0.1 convert_reduce_fusion
  74.8 0.1 collective-permute-start.10
  74.9 0.4 collective-permute-start.11
  75.2 1.5 %collective-permute-start.12 = (bf16[3,32,256]{2,1,0:T(8,128)(2,1)S(1)}, bf16[3,32,256]{2,1,0:T(8,128)(2,1)S(1)}, u32[]{:S(2)}, u32[]{:S(2)}) collective-permute-start(bf16[3,32,256]{2,1,0:T(8,128)(2,1)S(1)} %convert_element_type.100), channel_id=1, source_target_pairs={{0,24},{8,16},{16,8},{24,0},{1,25},{9,17},{17,9},{25,1},{2,26},{10... | collective-permute-start | bytes 147464 | tf_op jit(solution)/shard_map/ppermute | solution.py:151
  76.7 1.8 %columns.1 = (f32[6,32,256]{2,1,0:T(8,128)}, f32[6,32,256]{2,1,0:T(8,128)}) custom-call(s32[18]{0:T(128)S(1)} %copy-done.5, s32[12]{0:T(128)S(1)} %copy-done.6, f32[6,32,256]{2,1,0:T(8,128)S(1)} %dynamic-slice_bitcast_fusion.1.kept1, bf16[6,32,256]{2,1,0:T(8,128)(2,1)S(1)} %bitcast.49, f32[6,32,256]{2,1,0:T(8,128)S(1)} %dynamic-slice_bitcast_fusion.kept2, ...), custom_call_target="tpu_custom_call" | custom-call | tf_op jit(solution)/shard_map/columns/pallas_call | solution.py:248
  78.5 0.0 collective-permute-done.10
  78.5 1.0 %collective-permute-done.11 = bf16[3,32,256]{2,1,0:T(8,128)(2,1)S(1)} collective-permute-done((bf16[3,32,256]{2,1,0:T(8,128)(2,1)S(1)}, bf16[3,32,256]{2,1,0:T(8,128)(2,1)S(1)}, u32[]{:S(2)}, u32[]{:S(2)}) %collective-permute-start.11) | collective-permute-done | bytes 49184 | tf_op jit(solution)/shard_map/ppermute | solution.py:151
  79.5 0.1 collective-permute-done.12
  79.7 0.6 slice_bitcast_fusion
  (18 shorter events, 0.4 us)
Async XLA Ops:
  0.6 24.0 %copy-start = (bf16[6,1,3,1,256,256]{5,4,3,2,1,0:T(8,128)(2,1)S(1)}, bf16[6,1,3,1,256,256]{5,4,3,2,1,0:T(8,128)(2,1)}, u32[]{:S(2)}) copy-start(bf16[6,1,3,1,256,256]{5,4,3,2,1,0:T(8,128)(2,1)} %param.8) | copy-start | bytes 7077892
  0.6 24.0 %copy-start.1 = (f32[256,256]{1,0:T(8,128)S(1)}, f32[256,256]{1,0:T(8,128)}, u32[]{:S(2)}) copy-start(f32[256,256]{1,0:T(8,128)} %inv1.3) | copy-start | bytes 786436
  0.7 24.0 %copy-start.2 = (f32[256,256]{1,0:T(8,128)S(1)}, f32[256,256]{1,0:T(8,128)}, u32[]{:S(2)}) copy-start(f32[256,256]{1,0:T(8,128)} %inv2.3) | copy-start | bytes 786436
  0.7 24.0 %copy-start.5 = (s32[18]{0:T(128)S(1)}, s32[18]{0:T(128)}, u32[]{:S(2)}) copy-start(s32[18]{0:T(128)} %struct1.5) | copy-start | bytes 220
  0.7 24.0 %copy-start.6 = (s32[12]{0:T(128)S(1)}, s32[12]{0:T(128)}, u32[]{:S(2)}) copy-start(s32[12]{0:T(128)} %struct2.5) | copy-start | bytes 148
  1.8 4.8 %collective-permute-start = (bf16[2,3,32,256]{3,2,1,0:T(8,128)(2,1)S(1)}, bf16[2,3,32,256]{3,2,1,0:T(8,128)(2,1)S(1)}, u32[]{:S(2)}, u32[]{:S(2)}) collective-permute-start(bf16[2,3,32,256]{3,2,1,0:T(8,128)(2,1)S(1)} %get-tuple-element.55), channel_id=1, source_target_pairs={{0,0},{1,8},{2,16},{3,24},{4,4},{5,12},{6,20},{7,28},{8,1},{9,9},{... | collective-permute-start | bytes 294920 | tf_op jit(solution)/shard_map/ppermute | solution.py:188
  2.5 6.7 %collective-permute-start.1 = (bf16[2,3,32,256]{3,2,1,0:T(8,128)(2,1)S(1)}, bf16[2,3,32,256]{3,2,1,0:T(8,128)(2,1)S(1)}, u32[]{:S(2)}, u32[]{:S(2)}) collective-permute-start(bf16[2,3,32,256]{3,2,1,0:T(8,128)(2,1)S(1)} %get-tuple-element.56), channel_id=1, source_target_pairs={{0,4},{1,12},{2,20},{3,28},{4,0},{5,8},{6,16},{7,24},{8,5},{9,13},... | collective-permute-start | bytes 294920 | tf_op jit(solution)/shard_map/ppermute | solution.py:188
  9.2 13.4 %collective-permute-start.2 = (bf16[1,2,2,3,32,256]{5,4,3,2,1,0:T(8,128)(2,1)S(1)}, bf16[1,2,2,3,32,256]{5,4,3,2,1,0:T(8,128)(2,1)S(1)}, u32[]{:S(2)}, u32[]{:S(2)}) collective-permute-start(bf16[1,2,2,3,32,256]{5,4,3,2,1,0:T(8,128)(2,1)S(1)} %maximum_bitcast_fusion), channel_id=1, source_target_pairs={{0,16},{8,24},{16,0},{24,8},{1,17},{9,25},{17,1},{25,9},{2,18},{10... | collective-permute-start | bytes 589832 | tf_op jit(solution)/shard_map/ppermute | solution.py:151
  22.7 1.8 %collective-permute-start.3 = (bf16[2,2,2,3,32,256]{5,4,3,2,1,0:T(8,128)(2,1)S(1)}, bf16[2,2,2,3,32,256]{5,4,3,2,1,0:T(8,128)(2,1)S(1)}, u32[]{:S(2)}, u32[]{:S(2)}) collective-permute-start(bf16[2,2,2,3,32,256]{5,4,3,2,1,0:T(8,128)(2,1)S(1)} %pad_maximum_fusion.1), channel_id=1, source_target_pairs={{0,8},{8,0},{16,24},{24,16},{1,9},{9,1},{17,25},{25,17},{2,10},{10... | collective-permute-start | bytes 1179656 | tf_op jit(solution)/shard_map/ppermute | solution.py:151
  24.5 4.2 %copy-start.3 = (bf16[6,1,32,256]{3,2,1,0:T(8,128)(2,1)S(1)}, bf16[6,1,32,256]{3,2,1,0:T(8,128)(2,1)}, u32[]{:S(2)}) copy-start(bf16[6,1,32,256]{3,2,1,0:T(8,128)(2,1)} %param.9) | copy-start | bytes 294916
  24.5 4.2 %copy-start.4 = (bf16[6,1,32,256]{3,2,1,0:T(8,128)(2,1)S(1)}, bf16[6,1,32,256]{3,2,1,0:T(8,128)(2,1)}, u32[]{:S(2)}) copy-start(bf16[6,1,32,256]{3,2,1,0:T(8,128)(2,1)} %param.10) | copy-start | bytes 294916
  24.5 4.2 %copy-start.7 = (bf16[256,256]{1,0:T(8,128)(2,1)S(1)}, bf16[256,256]{1,0:T(8,128)(2,1)}, u32[]{:S(2)}) copy-start(bf16[256,256]{1,0:T(8,128)(2,1)} %link.1) | copy-start | bytes 393220
  28.0 11.2 %collective-permute-start.7 = (bf16[4,6,32,256]{3,2,1,0:T(8,128)(2,1)S(1)}, bf16[4,6,32,256]{3,2,1,0:T(8,128)(2,1)S(1)}, u32[]{:S(2)}, u32[]{:S(2)}) collective-permute-start(bf16[4,6,32,256]{3,2,1,0:T(8,128)(2,1)S(1)} %get-tuple-element.35), channel_id=1, source_target_pairs={{0,1},{1,0},{2,3},{3,2},{4,5},{5,4},{6,7},{7,6},{8,9},{9,8},{10,11... | collective-permute-start | bytes 1179656 | tf_op jit(solution)/shard_map/ppermute | solution.py:151
  28.0 12.0 %collective-permute-start.4 = (bf16[4,6,32,256]{3,2,1,0:T(8,128)(2,1)S(1)}, bf16[4,6,32,256]{3,2,1,0:T(8,128)(2,1)S(1)}, u32[]{:S(2)}, u32[]{:S(2)}) collective-permute-start(bf16[4,6,32,256]{3,2,1,0:T(8,128)(2,1)S(1)} %get-tuple-element.29), channel_id=1, source_target_pairs={{0,2},{1,3},{2,0},{3,1},{4,6},{5,7},{6,4},{7,5},{8,10},{9,11},{10,... | collective-permute-start | bytes 1179656 | tf_op jit(solution)/shard_map/ppermute | solution.py:151
  39.4 9.9 %collective-permute-start.8 = (bf16[2,6,32,256]{3,2,1,0:T(8,128)(2,1)S(1)}, bf16[2,6,32,256]{3,2,1,0:T(8,128)(2,1)S(1)}, u32[]{:S(2)}, u32[]{:S(2)}) collective-permute-start(bf16[2,6,32,256]{3,2,1,0:T(8,128)(2,1)S(1)} %fusion.1), channel_id=1, source_target_pairs={{0,2},{1,3},{2,0},{3,1},{4,6},{5,7},{6,4},{7,5},{8,10},{9,11},{10,... | collective-permute-start | bytes 589832 | tf_op jit(solution)/shard_map/ppermute | solution.py:151
  40.2 15.0 %collective-permute-start.5 = (bf16[2,6,32,256]{3,2,1,0:T(8,128)(2,1)S(1)}, bf16[2,6,32,256]{3,2,1,0:T(8,128)(2,1)S(1)}, u32[]{:S(2)}, u32[]{:S(2)}) collective-permute-start(bf16[2,6,32,256]{3,2,1,0:T(8,128)(2,1)S(1)} %fusion), channel_id=1, source_target_pairs={{0,4},{1,5},{2,6},{3,7},{4,0},{5,1},{6,2},{7,3},{8,12},{9,13},{10,... | collective-permute-start | bytes 589832 | tf_op jit(solution)/shard_map/ppermute | solution.py:151
  49.4 7.3 %collective-permute-start.9 = (bf16[1,6,32,256]{3,2,1,0:T(8,128)(2,1)S(1)}, bf16[1,6,32,256]{3,2,1,0:T(8,128)(2,1)S(1)}, u32[]{:S(2)}, u32[]{:S(2)}) collective-permute-start(bf16[1,6,32,256]{3,2,1,0:T(8,128)(2,1)S(1)} %dynamic-slice_convert_fusion.1), channel_id=1, source_target_pairs={{0,4},{1,5},{2,6},{3,7},{4,0},{5,1},{6,2},{7,3},{8,12},{9,13},{10,... | collective-permute-start | bytes 294920 | tf_op jit(solution)/shard_map/ppermute | solution.py:151
  55.2 4.7 %collective-permute-start.6 = (bf16[1,6,32,256]{3,2,1,0:T(8,128)(2,1)S(1)}, bf16[1,6,32,256]{3,2,1,0:T(8,128)(2,1)S(1)}, u32[]{:S(2)}, u32[]{:S(2)}) collective-permute-start(bf16[1,6,32,256]{3,2,1,0:T(8,128)(2,1)S(1)} %dynamic-slice_convert_fusion.2), channel_id=1, source_target_pairs={{0,1},{1,0},{2,3},{3,2},{4,5},{5,4},{6,7},{7,6},{8,9},{9,8},{10,11... | collective-permute-start | bytes 294920 | tf_op jit(solution)/shard_map/ppermute | solution.py:151
  74.8 3.7 %collective-permute-start.10 = (bf16[3,32,256]{2,1,0:T(8,128)(2,1)S(1)}, bf16[3,32,256]{2,1,0:T(8,128)(2,1)S(1)}, u32[]{:S(2)}, u32[]{:S(2)}) collective-permute-start(bf16[3,32,256]{2,1,0:T(8,128)(2,1)S(1)} %convert_element_type.100), channel_id=1, source_target_pairs={{0,8},{8,0},{16,24},{24,16},{1,9},{9,1},{17,25},{25,17},{2,10},{10... | collective-permute-start | bytes 147464 | tf_op jit(solution)/shard_map/ppermute | solution.py:151
  74.9 4.6 %collective-permute-start.11 = (bf16[3,32,256]{2,1,0:T(8,128)(2,1)S(1)}, bf16[3,32,256]{2,1,0:T(8,128)(2,1)S(1)}, u32[]{:S(2)}, u32[]{:S(2)}) collective-permute-start(bf16[3,32,256]{2,1,0:T(8,128)(2,1)S(1)} %convert_element_type.100), channel_id=1, source_target_pairs={{0,16},{8,24},{16,0},{24,8},{1,17},{9,25},{17,1},{25,9},{2,18},{10... | collective-permute-start | bytes 147464 | tf_op jit(solution)/shard_map/ppermute | solution.py:151
  75.2 4.4 %collective-permute-start.12 = (bf16[3,32,256]{2,1,0:T(8,128)(2,1)S(1)}, bf16[3,32,256]{2,1,0:T(8,128)(2,1)S(1)}, u32[]{:S(2)}, u32[]{:S(2)}) collective-permute-start(bf16[3,32,256]{2,1,0:T(8,128)(2,1)S(1)} %convert_element_type.100), channel_id=1, source_target_pairs={{0,24},{8,16},{16,8},{24,0},{1,25},{9,17},{17,9},{25,1},{2,26},{10... | collective-permute-start | bytes 147464 | tf_op jit(solution)/shard_map/ppermute | solution.py:151

commit v5 on v4

--- a/solution.py
+++ b/solution.py
@@ -88,29 +88,28 @@
         totals = jnp.dot(jnp.concatenate(wide, axis=0), factor[...], preferred_element_type=jnp.float32)
         for i in range(step):
             total = totals[i * width : (i + 1) * width]
+            group, place = divmod(a + i, row_blocks // 2)
+            bit = first_bits[group]
+            upper = ((here_col >> bit) & 1) == 1
             for p in range(2):
-                bit = first_bits[p]
-                upper = ((here_col >> bit) & 1) == 1
                 for j in range(n_col // 2):
                     low = ((j >> bit) << (bit + 1)) | (j & ((1 << bit) - 1))
                     high = low | (1 << bit)
                     x = total[low * slab : (low + 1) * slab, p * width : (p + 1) * width]
                     y = total[high * slab : (high + 1) * slab, p * width : (p + 1) * width]
-                    keeps[p][j, a + i] = jnp.where(upper, y, x)
-                    sends[p][j, a + i] = jnp.where(upper, x, y).astype(jnp.bfloat16)
-
-
-def factor_rows(panel, inverse, keep):
-    blocks, slab, width = panel.shape
-    flat = panel[...].astype(jnp.float32).reshape(blocks * slab, width).astype(jnp.bfloat16)
-    product = split_dot(flat, inverse[...]).reshape(blocks, slab, width)
-    return jnp.where(keep, product, 0.0)
-
-
-def prepare_kernel(n_row, struct1, struct2, mine1, mine2, link, inv1, inv2, after, rows, linked, out, whole):
-    blocks, slab, width = mine1.shape
-    for p, (struct, mine, inverse) in enumerate(((struct1, mine1, inv1), (struct2, mine2, inv2))):
-        rows[p] = factor_rows(mine, inverse, listed(struct, blocks, n_row)).astype(jnp.bfloat16)
+                    keeps[group][j, p, place] = jnp.where(upper, y, x)
+                    sends[group][j, p, place] = jnp.where(upper, x, y).astype(jnp.bfloat16)
+
+
+def prepare_kernel(n_row, struct1, struct2, low, high, link, inv1, inv2, after, rows, linked, out, whole):
+    slices, _, half, slab, width = low.shape
+    for p, (struct, inverse) in enumerate(((struct1, inv1), (struct2, inv2))):
+        keep = listed(struct, 2 * half, n_row)
+        for group, part in enumerate((low, high)):
+            flat = part[:, p].astype(jnp.float32).reshape(slices * half * slab, width).astype(jnp.bfloat16)
+            product = split_dot(flat, inverse[...]).reshape(slices, half, slab, width)
+            mine = keep[group * half : (group + 1) * half][None]
+            rows[group, p] = jnp.where(mine, product, 0.0).astype(jnp.bfloat16)
     linked[...] = exact_dot(link[...].astype(jnp.float32), inv2[...])
     link = linked[...]
     gram1 = exact_dot(inv1[...], inv1[...], 0)
@@ -122,29 +121,44 @@
     out[...] = whole[:, place, :]
 
 
-def sum_kernel(rows, kept1, came1, kept2, came2, linked, after, out):
-    blocks, slab, width = kept1.shape
-    flat = (blocks * slab, width)
-    sum1 = (kept1[...] + came1[...].astype(jnp.float32)).reshape(flat)
-    sum2 = (kept2[...] + came2[...].astype(jnp.float32)).reshape(flat)
-    u1, u2 = (rows[p].astype(jnp.float32).reshape(flat).astype(jnp.bfloat16) for p in range(2))
+def sum_kernel(first_bits, masks, rows, total_low, total_high, linked, after, out):
+    _, _, half, slab, width = total_low.shape
+    here_col = lax.axis_index("col")
+
+    def gathered(p):
+        parts = []
+        for bit, own, total in zip(first_bits, masks, (total_low, total_high)):
+            for mask in own:
+                piece = here_col ^ mask
+                place = ((piece >> (bit + 1)) << bit) | (piece & ((1 << bit) - 1))
+                parts.append(total[place, p].reshape(half * slab, width))
+        return jnp.concatenate(parts, axis=0)
+
+    def factor(p):
+        parts = [rows[g, p].astype(jnp.float32).reshape(-1, width) for g in range(2)]
+        return jnp.concatenate(parts, axis=0).astype(jnp.bfloat16)
+
     link = linked[...]
-    first = split_dot(u1, sum1, 0)
+    sum1 = gathered(0)
+    u2 = factor(1)
+    first = split_dot(factor(0), sum1, 0)
     cross = split_dot(u2, sum1, 0)
     top = cross.T - split_dot(first, link)
-    second = split_dot(u2, sum2, 0) - split_dot(cross, link) - split_dot(link, top, 0)
+    second = split_dot(u2, gathered(1), 0) - split_dot(cross, link) - split_dot(link, top, 0)
     for i, part in enumerate((first, top, second)):
-        out[:, i] = part.reshape(width // slab, slab, width).astype(out.dtype)
-
-
-def column_kernel(n_row, struct1, struct2, kept1, came1, kept2, came2, linked, column1, column2):
+        out[i] = part.reshape(width // slab, slab, width)
+
+
+def column_kernel(n_row, struct1, struct2, kept_low, came_low, kept_high, came_high, linked, column1, column2):
     blocks, slab, width = column1.shape
-    sum1 = kept1[...] + came1[...].astype(jnp.float32)
-    sum2 = kept2[...] + came2[...].astype(jnp.float32)
-    col1 = jnp.where(listed(struct1, blocks, n_row), -sum1, 0.0)
+    sums = []
+    for p in range(2):
+        parts = [k[p] + c[p].astype(jnp.float32) for k, c in ((kept_low, came_low), (kept_high, came_high))]
+        sums.append(jnp.concatenate(parts, axis=0))
+    col1 = jnp.where(listed(struct1, blocks, n_row), -sums[0], 0.0)
     column1[...] = col1
-    carried = split_dot(col1.reshape(blocks * slab, width), linked[...]).reshape(sum2.shape)
-    column2[...] = jnp.where(listed(struct2, blocks, n_row), -(sum2 + carried), 0.0)
+    carried = split_dot(col1.reshape(blocks * slab, width), linked[...]).reshape(col1.shape)
+    column2[...] = jnp.where(listed(struct2, blocks, n_row), -(sums[1] + carried), 0.0)
 
 
 def swapped(value, axis, size, mask):
@@ -176,7 +190,8 @@
     ways = [(way.astype(jnp.uint32), (1 - way).astype(jnp.uint32)) for way in ways]
     panels, picks, ways = lax.optimization_barrier((panels, picks, ways))
 
-    turns = jnp.stack(panels).reshape(2, col_blocks, cycle, slab, width)
+    raw = jnp.stack(panels)
+    turns = raw.reshape(2, col_blocks, cycle, slab, width)
     got = []
     for s in range(cycle):
         moves = []
@@ -186,21 +201,34 @@
                 moves.append((r * n_col + c, row * n_col + r + (s - t) % cycle * n_row))
         part = lax.dynamic_index_in_dim(turns, picks[s], 2, keepdims=False)
         got.append(lax.ppermute(part, ("row", "col"), moves))
+    base, base_masks = raw[None], [0]
+    for bit in range(n_bits - 1, 1, -1):
+        base = jnp.concatenate([base, swapped(base, "col", n_col, 1 << bit)])
+        base_masks += [m ^ (1 << bit) for m in base_masks]
+    got, base = lax.optimization_barrier((got, base))
+    half = row_blocks // 2
+    low, high = base[:, :, :half], base[:, :, half:]
+    low = jnp.concatenate([low, swapped(low, "col", n_col, 2)])
+    high = jnp.concatenate([high, swapped(high, "col", n_col, 1)])
+    masks = (base_masks + [m ^ 2 for m in base_masks], base_masks + [m ^ 1 for m in base_masks])
+
     pieces = jnp.stack(got)[None]
-
     order = [0]
     bit = n_row // 2
     while bit:
+        if bit == 1:
+            pieces, low, high = lax.optimization_barrier((pieces, low, high))
         pieces = jnp.concatenate([pieces, swapped(pieces, "row", n_row, bit)])
         order += [o ^ bit for o in order]
         bit //= 2
     pieces = jnp.stack([pieces[order.index(m)] for m in range(n_row)])
 
-    orders = (list(range(1, n_bits)) + [0], list(range(n_bits)))
-    half = (n_col // 2,) + panel
+    orders = (list(range(n_bits)), [1, 0] + list(range(2, n_bits)))
+    block = (2, half, slab, width)
+    kept = (n_col // 2,) + block
     split = pl.pallas_call(
         functools.partial(product_kernel, n_row, n_col, (orders[0][0], orders[1][0])),
-        out_shape=[shape(half, f32)] * 2 + [shape(half, bf16)] * 2,
+        out_shape=[shape(kept, f32)] * 2 + [shape(kept, bf16)] * 2,
         in_specs=[SMEM, SMEM] + [VMEM] * 4,
         out_specs=[VMEM] * 4,
         scratch_shapes=[
@@ -213,37 +241,44 @@
 
     rows, linked, consts = pl.pallas_call(
         functools.partial(prepare_kernel, n_row),
-        out_shape=[shape((2,) + panel, bf16), shape((width, width), f32), shape((3, slab, width), f32)],
+        out_shape=[shape((2, 2, n_col // 2) + block[1:], bf16), shape((width, width), f32), shape((3, slab, width), f32)],
         in_specs=[SMEM, SMEM] + [VMEM] * 5 + [ANY],
         out_specs=[VMEM] * 3,
         scratch_shapes=[pltpu.VMEM((3, width, width), f32)],
         compiler_params=big,
         name="prepare",
         cost_estimate=pl.CostEstimate(flops=6 * 10 * width**3, bytes_accessed=8 * width**2, transcendentals=0),
-    )(struct_first, struct_second, *panels, panel_link, inv_first, inv_second, split[0])
-
-    last = []
-    for p in range(2):
-        keep, came = split[p], swapped(split[2 + p], "col", n_col, 1 << orders[p][0])
-        left = sorted(set(range(n_bits)) - {orders[p][0]})
-        for bit in orders[p][1:]:
-            low = 1 << left.index(bit)
-            left.remove(bit)
-            total = (keep + came.astype(f32)).reshape((-1, 2, low) + panel)
-            keep, send = halves(total, 1, ways[bit])
-            keep = keep.reshape((-1,) + panel)
-            came = swapped(send.astype(bf16).reshape((-1,) + panel), "col", n_col, 1 << bit)
-        last += [keep[0], came[0]]
+    )(struct_first, struct_second, low, high, panel_link, inv_first, inv_second, split[0])
+
+    def step(bit, keep, send):
+        return keep, swapped(send.astype(bf16), "col", n_col, 1 << bit)
+
+    state = [step(orders[g][0], split[g], split[2 + g]) for g in range(2)]
+    left = [sorted(set(range(n_bits)) - {order[0]}) for order in orders]
+    totals = []
+    for i in range(1, n_bits):
+        for g in range(2):
+            keep, came = state[g]
+            bit = orders[g][i]
+            low_size = 1 << left[g].index(bit)
+            left[g].remove(bit)
+            total = keep + came.astype(f32)
+            if i == 1:
+                totals.append(total)
+            keep, send = halves(total.reshape((-1, 2, low_size) + block), 1, ways[bit])
+            state[g] = step(bit, keep.reshape((-1,) + block), send.reshape((-1,) + block))
 
     sums = pl.pallas_call(
-        sum_kernel,
-        out_shape=shape((n_col, 3, slab, width), bf16),
-        in_specs=[VMEM] * 6 + [ANY],
+        functools.partial(sum_kernel, [order[0] for order in orders], masks),
+        out_shape=shape((3, n_col, slab, width), f32),
+        in_specs=[VMEM] * 4 + [ANY],
         out_specs=VMEM,
         compiler_params=big,
         name="sums",
-    )(rows, *last, linked, consts)
-    sums = lax.all_to_all(sums, "col", 0, 0, tiled=True)
+    )(rows, *totals, linked, consts)
+    for bit in range(n_bits):
+        keep, send = halves(sums.reshape(3, -1, 2, slab, width), 2, ways[bit])
+        sums = keep + swapped(send.astype(bf16), "col", n_col, 1 << bit).astype(f32)
 
     column_first, column_second = pl.pallas_call(
         functools.partial(column_kernel, n_row),
@@ -252,12 +287,11 @@
         out_specs=[VMEM] * 2,
         compiler_params=big,
         name="columns",
-    )(struct_first, struct_second, *last, linked)
-
-    total = jnp.sum(sums.astype(f32), axis=0)
-    send = total.astype(bf16)
-    for m in range(1, n_row):
-        total = total + swapped(send, "row", n_row, m).astype(f32)
+    )(struct_first, struct_second, state[0][0][0], state[0][1][0], state[1][0][0], state[1][1][0], linked)
+
+    total = sums.reshape(3, slab, width)
+    for bit in range(n_row.bit_length() - 1):
+        total = total + swapped(total, "row", n_row, 1 << bit)
     diag_first, link_block, diag_second = consts + total
     out = (row_blocks, 1, slab, width)
     return column_first.reshape(out), column_second.reshape(out), diag_first, link_block, diag_second

time: 80.5 us -> 75.6 us (0.939)
  blocking collectives: 13.9 us -> 0 us
  waiting for transfers between devices: 32.5 us -> 39.9 us
  other arithmetic: 1.63 us -> 2.53 us
    all_to_all x1 -> x0, blocking collectives: 13.9 us -> none  [body(): sums = lax.all_to_all(sums, 'col', 0, 0, tiled=True)]
    ppermute x11 -> x16, waiting for transfers between devices: 29.9 us -> 38.6 us  [swapped(): return lax.ppermute(value, axis, [(i, i ^ mask) for i in range(size)])]
    ppermute x2, starting transfers between devices: 4.77 us -> 0.75 us  [body(): got.append(lax.ppermute(part, ('row', 'col'), moves))]
    ppermute x11 -> x16, starting transfers between devices: 16.5 us -> 20.3 us  [swapped(): return lax.ppermute(value, axis, [(i, i ^ mask) for i in range(size)])]
    ppermute x2, waiting for transfers between devices: 2.6 us -> 1.24 us  [body(): got.append(lax.ppermute(part, ('row', 'col'), moves))]
    broadcast_in_dim x0 -> x1, other arithmetic: none -> 0.96 us  [body(): base, base_masks = (raw[None], [0])]
  transfers between devices with their start and end apart: 13 -> 18, of which waited for: 10 -> 16; matrix products, arithmetic and copies ran while one was open for 1% -> 2% of each run, Pallas kernels for 6% -> 9%
where the time goes in v5:
time: 75.6 us; the launch traced here: 75.3 us
  waiting for transfers between devices  39.9 us (53%)
  starting transfers between devices  21.1 us (28%)
  Pallas kernels  9.93 us (13%)
  other arithmetic  2.53 us (3%)
  between operations  0.99 us (1%)
  local copies, waits for them, and re-layouts  0.94 us (1%)
    ppermute x16, waiting for transfers between devices, swapped(): return lax.ppermute(value, axis, [(i, i ^ mask) for i in range(size)])  38.6 us
    ppermute x16, starting transfers between devices, swapped(): return lax.ppermute(value, axis, [(i, i ^ mask) for i in range(size)])  20.3 us
    pallas_call x1, Pallas kernels, body(): pl.pallas_call(functools.partial(prepare_kernel, n_row), out_shape=[shape...  3.67 us
    pallas_call x1, Pallas kernels, body(): pl.pallas_call(functools.partial(product_kernel, n_row, n_col, (orders[0]...  3.29 us
    pallas_call x1, Pallas kernels, body(): pl.pallas_call(functools.partial(column_kernel, n_row), out_shape=[shape(...  1.77 us
  transfers between devices with their start and end apart: 18, of which 16 were waited for; matrix products, arithmetic and copies ran while one was open for 2% of the time, Pallas kernels for 9%

profile of v5, /device:TPU:0, one launch (start us, length us, event | category | flops | bytes accessed | tf_op | source)
XLA Modules:
  0.0 75.3 jit_solution(16556215800729615557)
XLA Ops:
  0.7 1.0 %maximum_bitcast_fusion = bf16[1,2,6,32,256]{4,3,2,1,0:T(8,128)(2,1)S(1)} fusion(bf16[1,6,32,256]{3,2,1,0:T(8,128)(2,1)} %bitcast.82, bf16[1,6,32,256]{3,2,1,0:T(8,128)(2,1)} %bitcast.80), kind=kLoop, calls=%fused_computation.20 | loop fusion | flops 98304 | bytes 393216 | tf_op jit(solution)/shard_map/broadcast_in_dim | solution.py:204
  1.6 4.1 %collective-permute-start.2 = (bf16[1,2,6,32,256]{4,3,2,1,0:T(8,128)(2,1)S(1)}, bf16[1,2,6,32,256]{4,3,2,1,0:T(8,128)(2,1)S(1)}, u32[]{:S(2)}, u32[]{:S(2)}) collective-permute-start(bf16[1,2,6,32,256]{4,3,2,1,0:T(8,128)(2,1)S(1)} %maximum_bitcast_fusion), channel_id=1, source_target_pairs={{0,4},{1,5},{2,6},{3,7},{4,0},{5,1},{6,2},{7,3},{8,12},{9,13},{10,... | collective-permute-start | bytes 589832 | tf_op jit(solution)/shard_map/ppermute | solution.py:165
  5.7 0.9 %fusion.5 = (bf16[2,3,32,256]{3,2,1,0:T(8,128)(2,1)S(1)}, bf16[2,3,32,256]{3,2,1,0:T(8,128)(2,1)S(1)}) fusion(u32[]{:T(128)S(6)} %convert_element_type.85, bf16[1,3,2,32,256]{4,3,2,1,0:T(8,128)(2,1)} %bitcast.81, bf16[1,3,2,32,256]{4,3,2,1,0:T(8,128)(2,1)} %bitcast.83, u32[]{:T(128)S(6)} %convert_element_type.84), kind=kLoop, calls=%fused_computation.30 | loop fusion | flops 98304 | bytes 393224 | tf_op jit(solution)/shard_map/jit(dynamic_index_in_dim)/squeeze | solution.py:202
  6.6 0.1 collective-permute-start.1
  6.7 0.7 collective-permute-start
  7.4 10.5 %collective-permute-done.2 = bf16[1,2,6,32,256]{4,3,2,1,0:T(8,128)(2,1)S(1)} collective-permute-done((bf16[1,2,6,32,256]{4,3,2,1,0:T(8,128)(2,1)S(1)}, bf16[1,2,6,32,256]{4,3,2,1,0:T(8,128)(2,1)S(1)}, u32[]{:S(2)}, u32[]{:S(2)}) %collective-permute-start.2) | collective-permute-done | bytes 196640 | tf_op jit(solution)/shard_map/ppermute | solution.py:165
  17.9 1.2 %collective-permute-done.1 = bf16[2,3,32,256]{3,2,1,0:T(8,128)(2,1)S(1)} collective-permute-done((bf16[2,3,32,256]{3,2,1,0:T(8,128)(2,1)S(1)}, bf16[2,3,32,256]{3,2,1,0:T(8,128)(2,1)S(1)}, u32[]{:S(2)}, u32[]{:S(2)}) %collective-permute-start.1) | collective-permute-done | bytes 98336 | tf_op jit(solution)/shard_map/ppermute | solution.py:203
  19.2 3.6 %collective-permute-start.3 = (bf16[1,2,2,3,32,256]{5,4,3,2,1,0:T(8,128)(2,1)S(1)}, bf16[1,2,2,3,32,256]{5,4,3,2,1,0:T(8,128)(2,1)S(1)}, u32[]{:S(2)}, u32[]{:S(2)}) collective-permute-start(bf16[1,2,2,3,32,256]{5,4,3,2,1,0:T(8,128)(2,1)S(1)} %maximum_bitcast_fusion.1), channel_id=1, source_target_pairs={{0,16},{8,24},{16,0},{24,8},{1,17},{9,25},{17,1},{25,9},{2,18},{10... | collective-permute-start | bytes 589832 | tf_op jit(solution)/shard_map/ppermute | solution.py:165
  22.8 1.5 %collective-permute-start.5 = (bf16[2,2,3,32,256]{4,3,2,1,0:T(8,128)(2,1)S(1)}, bf16[2,2,3,32,256]{4,3,2,1,0:T(8,128)(2,1)S(1)}, u32[]{:S(2)}, u32[]{:S(2)}) collective-permute-start(bf16[2,2,3,32,256]{4,3,2,1,0:T(8,128)(2,1)S(1)} %get-tuple-element.69), channel_id=1, source_target_pairs={{0,1},{1,0},{2,3},{3,2},{4,5},{5,4},{6,7},{7,6},{8,9},{9,8},{10,11... | collective-permute-start | bytes 589832 | tf_op jit(solution)/shard_map/ppermute | solution.py:165
  24.3 4.2 %collective-permute-done.3 = bf16[1,2,2,3,32,256]{5,4,3,2,1,0:T(8,128)(2,1)S(1)} collective-permute-done((bf16[1,2,2,3,32,256]{5,4,3,2,1,0:T(8,128)(2,1)S(1)}, bf16[1,2,2,3,32,256]{5,4,3,2,1,0:T(8,128)(2,1)S(1)}, u32[]{:S(2)}, u32[]{:S(2)}) %collective-permute-start.3) | collective-permute-done | bytes 196640 | tf_op jit(solution)/shard_map/ppermute | solution.py:165
  28.5 0.0 copy-start
  28.5 0.0 copy-start.1
  28.5 0.0 copy-start.2
  28.5 0.0 copy-start.4
  28.5 1.6 %collective-permute-done.5 = bf16[2,2,3,32,256]{4,3,2,1,0:T(8,128)(2,1)S(1)} collective-permute-done((bf16[2,2,3,32,256]{4,3,2,1,0:T(8,128)(2,1)S(1)}, bf16[2,2,3,32,256]{4,3,2,1,0:T(8,128)(2,1)S(1)}, u32[]{:S(2)}, u32[]{:S(2)}) %collective-permute-start.5) | collective-permute-done | bytes 196640 | tf_op jit(solution)/shard_map/ppermute | solution.py:165
  30.2 0.4 collective-permute-done.4
  30.6 0.1 collective-permute-start.6
  30.8 1.7 %collective-permute-done.6 = bf16[2,2,2,3,32,256]{5,4,3,2,1,0:T(8,128)(2,1)S(1)} collective-permute-done((bf16[2,2,2,3,32,256]{5,4,3,2,1,0:T(8,128)(2,1)S(1)}, bf16[2,2,2,3,32,256]{5,4,3,2,1,0:T(8,128)(2,1)S(1)}, u32[]{:S(2)}, u32[]{:S(2)}) %collective-permute-start.6) | collective-permute-done | bytes 393248 | tf_op jit(solution)/shard_map/ppermute | solution.py:165
  32.5 0.0 copy-start.5
  32.5 0.1 pad_maximum_fusion.pieces
  32.6 3.3 %products.1 = (f32[4,2,3,32,256]{4,3,2,1,0:T(8,128)S(1)}, f32[4,2,3,32,256]{4,3,2,1,0:T(8,128)S(1)}, bf16[4,2,3,32,256]{4,3,2,1,0:T(8,128)(2,1)S(1)}, bf16[4,2,3,32,256]{4,3,2,1,0:T(8,128)(2,1)S(1)}) custom-call(s32[18]{0:T(128)S(1)} %copy-done.3, s32[12]{0:T(128)S(1)} %copy-done.4, f32[256,256]{1,0:T(8,128)S(1)} %copy-done.1, f32[256,256]{1,0:T(8,128)S(1)} %copy-done.2, ...), custom_call_target="tpu_custom_call" | custom-call | tf_op jit(solution)/shard_map/products/pallas_call | solution.py:229
  35.9 1.4 %collective-permute-start.7 = (bf16[4,2,3,32,256]{4,3,2,1,0:T(8,128)(2,1)S(1)}, bf16[4,2,3,32,256]{4,3,2,1,0:T(8,128)(2,1)S(1)}, u32[]{:S(2)}, u32[]{:S(2)}) collective-permute-start(bf16[4,2,3,32,256]{4,3,2,1,0:T(8,128)(2,1)S(1)} %get-tuple-element.39), channel_id=1, source_target_pairs={{0,1},{1,0},{2,3},{3,2},{4,5},{5,4},{6,7},{7,6},{8,9},{9,8},{10,11... | collective-permute-start | bytes 1179656 | tf_op jit(solution)/shard_map/ppermute | solution.py:165
  37.3 0.3 collective-permute-start.10
  37.6 3.7 %prepare.1 = (bf16[2,2,4,3,32,256]{5,4,3,2,1,0:T(8,128)(2,1)S(1)}, f32[256,256]{1,0:T(8,128)S(1)}, f32[3,32,256]{2,1,0:T(8,128)S(1)}) custom-call(s32[18]{0:T(128)S(1)} %copy-done.3, s32[12]{0:T(128)S(1)} %copy-done.4, bf16[4,2,3,32,256]{4,3,2,1,0:T(8,128)(2,1)S(1)} %pad_maximum_fusion.3.low, bf16[4,2,3,32,256]{4,3,2,1,0:T(8,128)(2,1)S(1)} %pad_maximum_fusion.4.high, ...), custom_call_target="tpu_custom_call" | custom-call | flops 1006632960 | bytes 524288 | tf_op jit(solution)/shard_map/prepare/pallas_call | solution.py:242
  41.3 5.9 %collective-permute-done.7 = bf16[4,2,3,32,256]{4,3,2,1,0:T(8,128)(2,1)S(1)} collective-permute-done((bf16[4,2,3,32,256]{4,3,2,1,0:T(8,128)(2,1)S(1)}, bf16[4,2,3,32,256]{4,3,2,1,0:T(8,128)(2,1)S(1)}, u32[]{:S(2)}, u32[]{:S(2)}) %collective-permute-start.7) | collective-permute-done | bytes 393248 | tf_op jit(solution)/shard_map/ppermute | solution.py:165
  47.2 0.1 convert_add_fusion.1.total_low
  47.3 0.3 collective-permute-start.8
  47.7 0.5 collective-permute-done.10
  48.2 0.1 convert_add_fusion.total_high
  48.3 1.2 %sums.1 = f32[3,8,32,256]{3,2,1,0:T(8,128)S(1)} custom-call(bf16[2,2,4,3,32,256]{5,4,3,2,1,0:T(8,128)(2,1)S(1)} %get-tuple-element.54.rows, f32[4,2,3,32,256]{4,3,2,1,0:T(8,128)S(1)} %convert_add_fusion.1.total_low, f32[4,2,3,32,256]{4,3,2,1,0:T(8,128)S(1)} %convert_add_fusion.total_high, f32[256,256]{1,0:T(8,128)S(1)} %get-tuple-element.50.linked, ...), custom_call_target="tpu_custom_call" | custom-call | tf_op jit(solution)/shard_map/sums/pallas_call | solution.py:271
  49.5 0.8 %collective-permute-start.13 = (bf16[3,4,32,256]{3,2,1,0:T(8,128)(2,1)S(1)}, bf16[3,4,32,256]{3,2,1,0:T(8,128)(2,1)S(1)}, u32[]{:S(2)}, u32[]{:S(2)}) collective-permute-start(bf16[3,4,32,256]{3,2,1,0:T(8,128)(2,1)S(1)} %fusion), channel_id=1, source_target_pairs={{0,1},{1,0},{2,3},{3,2},{4,5},{5,4},{6,7},{7,6},{8,9},{9,8},{10,11... | collective-permute-start | bytes 589832 | tf_op jit(solution)/shard_map/ppermute | solution.py:165
  50.4 1.3 %collective-permute-start.11 = (bf16[2,2,3,32,256]{4,3,2,1,0:T(8,128)(2,1)S(1)}, bf16[2,2,3,32,256]{4,3,2,1,0:T(8,128)(2,1)S(1)}, u32[]{:S(2)}, u32[]{:S(2)}) collective-permute-start(bf16[2,2,3,32,256]{4,3,2,1,0:T(8,128)(2,1)S(1)} %fusion.2), channel_id=1, source_target_pairs={{0,1},{1,0},{2,3},{3,2},{4,5},{5,4},{6,7},{7,6},{8,9},{9,8},{10,11... | collective-permute-start | bytes 589832 | tf_op jit(solution)/shard_map/ppermute | solution.py:165
  51.7 1.8 %collective-permute-done.8 = bf16[2,2,3,32,256]{4,3,2,1,0:T(8,128)(2,1)S(1)} collective-permute-done((bf16[2,2,3,32,256]{4,3,2,1,0:T(8,128)(2,1)S(1)}, bf16[2,2,3,32,256]{4,3,2,1,0:T(8,128)(2,1)S(1)}, u32[]{:S(2)}, u32[]{:S(2)}) %collective-permute-start.8) | collective-permute-done | bytes 196640 | tf_op jit(solution)/shard_map/ppermute | solution.py:165
  53.6 1.9 %collective-permute-start.9 = (bf16[1,2,3,32,256]{4,3,2,1,0:T(8,128)(2,1)S(1)}, bf16[1,2,3,32,256]{4,3,2,1,0:T(8,128)(2,1)S(1)}, u32[]{:S(2)}, u32[]{:S(2)}) collective-permute-start(bf16[1,2,3,32,256]{4,3,2,1,0:T(8,128)(2,1)S(1)} %dynamic-slice_convert_fusion.1), channel_id=1, source_target_pairs={{0,4},{1,5},{2,6},{3,7},{4,0},{5,1},{6,2},{7,3},{8,12},{9,13},{10,... | collective-permute-start | bytes 294920 | tf_op jit(solution)/shard_map/ppermute | solution.py:165
  55.5 1.9 %collective-permute-done.13 = bf16[3,4,32,256]{3,2,1,0:T(8,128)(2,1)S(1)} collective-permute-done((bf16[3,4,32,256]{3,2,1,0:T(8,128)(2,1)S(1)}, bf16[3,4,32,256]{3,2,1,0:T(8,128)(2,1)S(1)}, u32[]{:S(2)}, u32[]{:S(2)}) %collective-permute-start.13) | collective-permute-done | bytes 196640 | tf_op jit(solution)/shard_map/ppermute | solution.py:165
  57.5 1.3 %collective-permute-start.14 = (bf16[3,2,32,256]{3,2,0,1:T(8,128)(2,1)S(1)}, bf16[3,2,32,256]{3,2,0,1:T(8,128)(2,1)S(1)}, u32[]{:S(2)}, u32[]{:S(2)}) collective-permute-start(bf16[3,2,32,256]{3,2,0,1:T(8,128)(2,1)S(1)} %fusion.3), channel_id=1, source_target_pairs={{0,2},{1,3},{2,0},{3,1},{4,6},{5,7},{6,4},{7,5},{8,10},{9,11},{10,... | collective-permute-start | bytes 294920 | tf_op jit(solution)/shard_map/ppermute | solution.py:165
  58.8 0.8 %collective-permute-done.11 = bf16[2,2,3,32,256]{4,3,2,1,0:T(8,128)(2,1)S(1)} collective-permute-done((bf16[2,2,3,32,256]{4,3,2,1,0:T(8,128)(2,1)S(1)}, bf16[2,2,3,32,256]{4,3,2,1,0:T(8,128)(2,1)S(1)}, u32[]{:S(2)}, u32[]{:S(2)}) %collective-permute-start.11) | collective-permute-done | bytes 196640 | tf_op jit(solution)/shard_map/ppermute | solution.py:165
  59.7 3.1 %collective-permute-done.14 = bf16[3,2,32,256]{3,2,0,1:T(8,128)(2,1)S(1)} collective-permute-done((bf16[3,2,32,256]{3,2,0,1:T(8,128)(2,1)S(1)}, bf16[3,2,32,256]{3,2,0,1:T(8,128)(2,1)S(1)}, u32[]{:S(2)}, u32[]{:S(2)}) %collective-permute-start.14) | collective-permute-done | bytes 98336 | tf_op jit(solution)/shard_map/ppermute | solution.py:165
  62.8 2.4 %collective-permute-start.15 = (bf16[3,1,32,256]{3,2,0,1:T(8,128)(2,1)S(1)}, bf16[3,1,32,256]{3,2,0,1:T(8,128)(2,1)S(1)}, u32[]{:S(2)}, u32[]{:S(2)}) collective-permute-start(bf16[3,1,32,256]{3,2,0,1:T(8,128)(2,1)S(1)} %dynamic-slice_convert_fusion.2), channel_id=1, source_target_pairs={{0,4},{1,5},{2,6},{3,7},{4,0},{5,1},{6,2},{7,3},{8,12},{9,13},{10,... | collective-permute-start | bytes 147464 | tf_op jit(solution)/shard_map/ppermute | solution.py:165
  65.1 0.7 collective-permute-start.12
  65.8 2.5 %collective-permute-done.15 = bf16[3,1,32,256]{3,2,0,1:T(8,128)(2,1)S(1)} collective-permute-done((bf16[3,1,32,256]{3,2,0,1:T(8,128)(2,1)S(1)}, bf16[3,1,32,256]{3,2,0,1:T(8,128)(2,1)S(1)}, u32[]{:S(2)}, u32[]{:S(2)}) %collective-permute-start.15) | collective-permute-done | bytes 49184 | tf_op jit(solution)/shard_map/ppermute | solution.py:165
  68.4 0.1 collective-permute-start.16
  68.5 1.3 %collective-permute-done.16 = f32[3,32,256]{2,1,0:T(8,128)S(1)} collective-permute-done((f32[3,32,256]{2,1,0:T(8,128)S(1)}, f32[3,32,256]{2,1,0:T(8,128)S(1)}, u32[]{:S(2)}, u32[]{:S(2)}) %collective-permute-start.16) | collective-permute-done | bytes 98336 | tf_op jit(solution)/shard_map/ppermute | solution.py:165
  69.8 0.6 collective-permute-start.17
  70.4 1.4 %collective-permute-done.12 = bf16[1,2,3,32,256]{4,3,2,1,0:T(8,128)(2,1)S(1)} collective-permute-done((bf16[1,2,3,32,256]{4,3,2,1,0:T(8,128)(2,1)S(1)}, bf16[1,2,3,32,256]{4,3,2,1,0:T(8,128)(2,1)S(1)}, u32[]{:S(2)}, u32[]{:S(2)}) %collective-permute-start.12) | collective-permute-done | bytes 98336 | tf_op jit(solution)/shard_map/ppermute | solution.py:165
  71.8 1.8 %columns.1 = (f32[6,32,256]{2,1,0:T(8,128)}, f32[6,32,256]{2,1,0:T(8,128)}) custom-call(s32[18]{0:T(128)S(1)} %copy-done.3, s32[12]{0:T(128)S(1)} %copy-done.4, f32[2,3,32,256]{3,2,1,0:T(8,128)S(1)} %dynamic-slice_bitcast_fusion.1.kept_low, bf16[2,3,32,256]{3,2,1,0:T(8,128)(2,1)S(1)} %bitcast.76, f32[2,3,32,256]{3,2,1,0:T(8,128)S(1)} %dynamic-slice_bitcast_fusion.kept_high, ...), custom_call_target="tpu_custom_call" | custom-call | tf_op jit(solution)/shard_map/columns/pallas_call | solution.py:283
  73.5 1.1 %collective-permute-done.17 = f32[3,32,256]{2,1,0:T(8,128)S(1)} collective-permute-done((f32[3,32,256]{2,1,0:T(8,128)S(1)}, f32[3,32,256]{2,1,0:T(8,128)S(1)}, u32[]{:S(2)}, u32[]{:S(2)}) %collective-permute-start.17) | collective-permute-done | bytes 98336 | tf_op jit(solution)/shard_map/ppermute | solution.py:165
  74.7 0.6 slice_bitcast_fusion
  (34 shorter events, 0.7 us)
Async XLA Ops:
  1.6 16.2 %collective-permute-start.2 = (bf16[1,2,6,32,256]{4,3,2,1,0:T(8,128)(2,1)S(1)}, bf16[1,2,6,32,256]{4,3,2,1,0:T(8,128)(2,1)S(1)}, u32[]{:S(2)}, u32[]{:S(2)}) collective-permute-start(bf16[1,2,6,32,256]{4,3,2,1,0:T(8,128)(2,1)S(1)} %maximum_bitcast_fusion), channel_id=1, source_target_pairs={{0,4},{1,5},{2,6},{3,7},{4,0},{5,1},{6,2},{7,3},{8,12},{9,13},{10,... | collective-permute-start | bytes 589832 | tf_op jit(solution)/shard_map/ppermute | solution.py:165
  6.6 12.5 %collective-permute-start.1 = (bf16[2,3,32,256]{3,2,1,0:T(8,128)(2,1)S(1)}, bf16[2,3,32,256]{3,2,1,0:T(8,128)(2,1)S(1)}, u32[]{:S(2)}, u32[]{:S(2)}) collective-permute-start(bf16[2,3,32,256]{3,2,1,0:T(8,128)(2,1)S(1)} %get-tuple-element.71), channel_id=1, source_target_pairs={{0,4},{1,12},{2,20},{3,28},{4,0},{5,8},{6,16},{7,24},{8,5},{9,13},... | collective-permute-start | bytes 294920 | tf_op jit(solution)/shard_map/ppermute | solution.py:203
  6.7 12.4 %collective-permute-start = (bf16[2,3,32,256]{3,2,1,0:T(8,128)(2,1)S(1)}, bf16[2,3,32,256]{3,2,1,0:T(8,128)(2,1)S(1)}, u32[]{:S(2)}, u32[]{:S(2)}) collective-permute-start(bf16[2,3,32,256]{3,2,1,0:T(8,128)(2,1)S(1)} %get-tuple-element.72), channel_id=1, source_target_pairs={{0,0},{1,8},{2,16},{3,24},{4,4},{5,12},{6,20},{7,28},{8,1},{9,9},{... | collective-permute-start | bytes 294920 | tf_op jit(solution)/shard_map/ppermute | solution.py:203
  19.2 9.2 %collective-permute-start.3 = (bf16[1,2,2,3,32,256]{5,4,3,2,1,0:T(8,128)(2,1)S(1)}, bf16[1,2,2,3,32,256]{5,4,3,2,1,0:T(8,128)(2,1)S(1)}, u32[]{:S(2)}, u32[]{:S(2)}) collective-permute-start(bf16[1,2,2,3,32,256]{5,4,3,2,1,0:T(8,128)(2,1)S(1)} %maximum_bitcast_fusion.1), channel_id=1, source_target_pairs={{0,16},{8,24},{16,0},{24,8},{1,17},{9,25},{17,1},{25,9},{2,18},{10... | collective-permute-start | bytes 589832 | tf_op jit(solution)/shard_map/ppermute | solution.py:165
  22.8 7.4 %collective-permute-start.5 = (bf16[2,2,3,32,256]{4,3,2,1,0:T(8,128)(2,1)S(1)}, bf16[2,2,3,32,256]{4,3,2,1,0:T(8,128)(2,1)S(1)}, u32[]{:S(2)}, u32[]{:S(2)}) collective-permute-start(bf16[2,2,3,32,256]{4,3,2,1,0:T(8,128)(2,1)S(1)} %get-tuple-element.69), channel_id=1, source_target_pairs={{0,1},{1,0},{2,3},{3,2},{4,5},{5,4},{6,7},{7,6},{8,9},{9,8},{10,11... | collective-permute-start | bytes 589832 | tf_op jit(solution)/shard_map/ppermute | solution.py:165
  24.2 6.4 %collective-permute-start.4 = (bf16[2,2,3,32,256]{4,3,2,1,0:T(8,128)(2,1)S(1)}, bf16[2,2,3,32,256]{4,3,2,1,0:T(8,128)(2,1)S(1)}, u32[]{:S(2)}, u32[]{:S(2)}) collective-permute-start(bf16[2,2,3,32,256]{4,3,2,1,0:T(8,128)(2,1)S(1)} %get-tuple-element.70), channel_id=1, source_target_pairs={{0,2},{1,3},{2,0},{3,1},{4,6},{5,7},{6,4},{7,5},{8,10},{9,11},{10,... | collective-permute-start | bytes 589832 | tf_op jit(solution)/shard_map/ppermute | solution.py:165
  28.5 4.1 %copy-start = (bf16[6,1,3,1,256,256]{5,4,3,2,1,0:T(8,128)(2,1)S(1)}, bf16[6,1,3,1,256,256]{5,4,3,2,1,0:T(8,128)(2,1)}, u32[]{:S(2)}) copy-start(bf16[6,1,3,1,256,256]{5,4,3,2,1,0:T(8,128)(2,1)} %param.8) | copy-start | bytes 7077892
  28.5 4.1 %copy-start.1 = (f32[256,256]{1,0:T(8,128)S(1)}, f32[256,256]{1,0:T(8,128)}, u32[]{:S(2)}) copy-start(f32[256,256]{1,0:T(8,128)} %inv1.3) | copy-start | bytes 786436
  28.5 4.1 %copy-start.2 = (f32[256,256]{1,0:T(8,128)S(1)}, f32[256,256]{1,0:T(8,128)}, u32[]{:S(2)}) copy-start(f32[256,256]{1,0:T(8,128)} %inv2.3) | copy-start | bytes 786436
  28.5 4.1 %copy-start.3 = (s32[18]{0:T(128)S(1)}, s32[18]{0:T(128)}, u32[]{:S(2)}) copy-start(s32[18]{0:T(128)} %struct1.5) | copy-start | bytes 220
  28.5 4.1 %copy-start.4 = (s32[12]{0:T(128)S(1)}, s32[12]{0:T(128)}, u32[]{:S(2)}) copy-start(s32[12]{0:T(128)} %struct2.5) | copy-start | bytes 148
  30.6 1.8 %collective-permute-start.6 = (bf16[2,2,2,3,32,256]{5,4,3,2,1,0:T(8,128)(2,1)S(1)}, bf16[2,2,2,3,32,256]{5,4,3,2,1,0:T(8,128)(2,1)S(1)}, u32[]{:S(2)}, u32[]{:S(2)}) collective-permute-start(bf16[2,2,2,3,32,256]{5,4,3,2,1,0:T(8,128)(2,1)S(1)} %pad_maximum_fusion.2), channel_id=1, source_target_pairs={{0,8},{8,0},{16,24},{24,16},{1,9},{9,1},{17,25},{25,17},{2,10},{10... | collective-permute-start | bytes 1179656 | tf_op jit(solution)/shard_map/ppermute | solution.py:165
  32.5 5.1 %copy-start.5 = (bf16[256,256]{1,0:T(8,128)(2,1)S(1)}, bf16[256,256]{1,0:T(8,128)(2,1)}, u32[]{:S(2)}) copy-start(bf16[256,256]{1,0:T(8,128)(2,1)} %link.1) | copy-start | bytes 393220
  35.9 11.2 %collective-permute-start.7 = (bf16[4,2,3,32,256]{4,3,2,1,0:T(8,128)(2,1)S(1)}, bf16[4,2,3,32,256]{4,3,2,1,0:T(8,128)(2,1)S(1)}, u32[]{:S(2)}, u32[]{:S(2)}) collective-permute-start(bf16[4,2,3,32,256]{4,3,2,1,0:T(8,128)(2,1)S(1)} %get-tuple-element.39), channel_id=1, source_target_pairs={{0,1},{1,0},{2,3},{3,2},{4,5},{5,4},{6,7},{7,6},{8,9},{9,8},{10,11... | collective-permute-start | bytes 1179656 | tf_op jit(solution)/shard_map/ppermute | solution.py:165
  37.3 10.9 %collective-permute-start.10 = (bf16[4,2,3,32,256]{4,3,2,1,0:T(8,128)(2,1)S(1)}, bf16[4,2,3,32,256]{4,3,2,1,0:T(8,128)(2,1)S(1)}, u32[]{:S(2)}, u32[]{:S(2)}) collective-permute-start(bf16[4,2,3,32,256]{4,3,2,1,0:T(8,128)(2,1)S(1)} %get-tuple-element.45), channel_id=1, source_target_pairs={{0,2},{1,3},{2,0},{3,1},{4,6},{5,7},{6,4},{7,5},{8,10},{9,11},{10,... | collective-permute-start | bytes 1179656 | tf_op jit(solution)/shard_map/ppermute | solution.py:165
  47.3 6.2 %collective-permute-start.8 = (bf16[2,2,3,32,256]{4,3,2,1,0:T(8,128)(2,1)S(1)}, bf16[2,2,3,32,256]{4,3,2,1,0:T(8,128)(2,1)S(1)}, u32[]{:S(2)}, u32[]{:S(2)}) collective-permute-start(bf16[2,2,3,32,256]{4,3,2,1,0:T(8,128)(2,1)S(1)} %fusion.1), channel_id=1, source_target_pairs={{0,2},{1,3},{2,0},{3,1},{4,6},{5,7},{6,4},{7,5},{8,10},{9,11},{10,... | collective-permute-start | bytes 589832 | tf_op jit(solution)/shard_map/ppermute | solution.py:165
  49.5 7.9 %collective-permute-start.13 = (bf16[3,4,32,256]{3,2,1,0:T(8,128)(2,1)S(1)}, bf16[3,4,32,256]{3,2,1,0:T(8,128)(2,1)S(1)}, u32[]{:S(2)}, u32[]{:S(2)}) collective-permute-start(bf16[3,4,32,256]{3,2,1,0:T(8,128)(2,1)S(1)} %fusion), channel_id=1, source_target_pairs={{0,1},{1,0},{2,3},{3,2},{4,5},{5,4},{6,7},{7,6},{8,9},{9,8},{10,11... | collective-permute-start | bytes 589832 | tf_op jit(solution)/shard_map/ppermute | solution.py:165
  50.4 9.2 %collective-permute-start.11 = (bf16[2,2,3,32,256]{4,3,2,1,0:T(8,128)(2,1)S(1)}, bf16[2,2,3,32,256]{4,3,2,1,0:T(8,128)(2,1)S(1)}, u32[]{:S(2)}, u32[]{:S(2)}) collective-permute-start(bf16[2,2,3,32,256]{4,3,2,1,0:T(8,128)(2,1)S(1)} %fusion.2), channel_id=1, source_target_pairs={{0,1},{1,0},{2,3},{3,2},{4,5},{5,4},{6,7},{7,6},{8,9},{9,8},{10,11... | collective-permute-start | bytes 589832 | tf_op jit(solution)/shard_map/ppermute | solution.py:165
  53.6 16.8 %collective-permute-start.9 = (bf16[1,2,3,32,256]{4,3,2,1,0:T(8,128)(2,1)S(1)}, bf16[1,2,3,32,256]{4,3,2,1,0:T(8,128)(2,1)S(1)}, u32[]{:S(2)}, u32[]{:S(2)}) collective-permute-start(bf16[1,2,3,32,256]{4,3,2,1,0:T(8,128)(2,1)S(1)} %dynamic-slice_convert_fusion.1), channel_id=1, source_target_pairs={{0,4},{1,5},{2,6},{3,7},{4,0},{5,1},{6,2},{7,3},{8,12},{9,13},{10,... | collective-permute-start | bytes 294920 | tf_op jit(solution)/shard_map/ppermute | solution.py:165
  57.5 5.2 %collective-permute-start.14 = (bf16[3,2,32,256]{3,2,0,1:T(8,128)(2,1)S(1)}, bf16[3,2,32,256]{3,2,0,1:T(8,128)(2,1)S(1)}, u32[]{:S(2)}, u32[]{:S(2)}) collective-permute-start(bf16[3,2,32,256]{3,2,0,1:T(8,128)(2,1)S(1)} %fusion.3), channel_id=1, source_target_pairs={{0,2},{1,3},{2,0},{3,1},{4,6},{5,7},{6,4},{7,5},{8,10},{9,11},{10,... | collective-permute-start | bytes 294920 | tf_op jit(solution)/shard_map/ppermute | solution.py:165
  62.8 5.6 %collective-permute-start.15 = (bf16[3,1,32,256]{3,2,0,1:T(8,128)(2,1)S(1)}, bf16[3,1,32,256]{3,2,0,1:T(8,128)(2,1)S(1)}, u32[]{:S(2)}, u32[]{:S(2)}) collective-permute-start(bf16[3,1,32,256]{3,2,0,1:T(8,128)(2,1)S(1)} %dynamic-slice_convert_fusion.2), channel_id=1, source_target_pairs={{0,4},{1,5},{2,6},{3,7},{4,0},{5,1},{6,2},{7,3},{8,12},{9,13},{10,... | collective-permute-start | bytes 147464 | tf_op jit(solution)/shard_map/ppermute | solution.py:165
  65.1 6.6 %collective-permute-start.12 = (bf16[1,2,3,32,256]{4,3,2,1,0:T(8,128)(2,1)S(1)}, bf16[1,2,3,32,256]{4,3,2,1,0:T(8,128)(2,1)S(1)}, u32[]{:S(2)}, u32[]{:S(2)}) collective-permute-start(bf16[1,2,3,32,256]{4,3,2,1,0:T(8,128)(2,1)S(1)} %dynamic-slice_convert_fusion), channel_id=1, source_target_pairs={{0,4},{1,5},{2,6},{3,7},{4,0},{5,1},{6,2},{7,3},{8,12},{9,13},{10,... | collective-permute-start | bytes 294920 | tf_op jit(solution)/shard_map/ppermute | solution.py:165
  68.4 1.4 %collective-permute-start.16 = (f32[3,32,256]{2,1,0:T(8,128)S(1)}, f32[3,32,256]{2,1,0:T(8,128)S(1)}, u32[]{:S(2)}, u32[]{:S(2)}) collective-permute-start(f32[3,32,256]{2,1,0:T(8,128)S(1)} %add_bitcast_fusion), channel_id=1, source_target_pairs={{0,8},{8,0},{16,24},{24,16},{1,9},{9,1},{17,25},{25,17},{2,10},{10... | collective-permute-start | bytes 294920 | tf_op jit(solution)/shard_map/ppermute | solution.py:165
  69.8 4.9 %collective-permute-start.17 = (f32[3,32,256]{2,1,0:T(8,128)S(1)}, f32[3,32,256]{2,1,0:T(8,128)S(1)}, u32[]{:S(2)}, u32[]{:S(2)}) collective-permute-start(f32[3,32,256]{2,1,0:T(8,128)S(1)} %add.57), channel_id=1, source_target_pairs={{0,16},{8,24},{16,0},{24,8},{1,17},{9,25},{17,1},{25,9},{2,18},{10... | collective-permute-start | bytes 294920 | tf_op jit(solution)/shard_map/ppermute | solution.py:165
